TPU v7x, 512 devices: a whole 4x4x16 slice. The times are simulated.
512 devices in a mesh: gx: 16 (over y, x), gy: 32 (over z, core).
Axes of the slice: x: 4, y: 4, z: 16, core: 2. Of those that a mesh axis runs over, the one named last changes fastest.
Arguments:
- probes: bfloat16 [32, 256, 32, 128], P('gx', 'gy'), may hold values from -6 to 6
- leaf_basis: bfloat16 [128, 64], replicated, may hold values from -0.5 to 0.5
- up_transfer: bfloat16 [7, 4, 64, 64], replicated, may hold values from -0.375 to 0.375
- down_transfer: bfloat16 [7, 4, 64, 64], replicated, may hold values from -0.75 to 0.75
- coupling: bfloat16 [8, 40, 64, 64], replicated, may hold values from -0.15625 to 0.15625
- far_ids: int32 [8, 4, 27], replicated, may hold values from 0 to 39
Outputs:
- product: bfloat16 [32, 256, 32, 128], P('gx', 'gy')
Inputs may be any that keep to these rules, and one draw needn't show every extreme that they name: `far_ids`: each entry picks one of the 40 coupling matrices of its level.
All inputs are finite; a program needn't handle non-finite values.
Results may differ from a plain program's by a relative error of at most 0.012.
Values may be sent and summed in bfloat16 or wider, within the bound.
No kernel may reach another device: no remote copies, remote signals or barrier semaphores. Data moves between devices by JAX's collectives and lax.ppermute only.
A program may use at most 128 MiB of HBM per device.

v0:
```python
import jax
import jax.numpy as jnp
from jax import lax
from jax.sharding import PartitionSpec as P

LEAF_ROWS = 8
LEAF_COLS = 16


length_scale = 1.5


def shifted(block, axis, distance):
    devices = range(lax.axis_size(axis))
    route = [(i - distance, i) for i in devices if i - distance in devices]
    return lax.ppermute(block, axis, route)


def with_halo(value, sides, width):
    for axis, dim in sides:
        count, length = (lax.axis_size(axis), value.shape[dim])
        up = [(i, (i + 1) % count) for i in range(count - 1)]
        down = [(j, i) for i, j in up]
        last = lax.slice_in_dim(value, length - width, length, axis=dim)
        leading = lax.slice_in_dim(value, 0, width, axis=dim)
        before = lax.ppermute(last, axis, up)
        after = lax.ppermute(leading, axis, down)
        value = jnp.concatenate([before, value, after], axis=dim)
    return value


def slot_offsets(type_row, type_col):
    offsets = []
    for off_row in range(-2 - type_row, 4 - type_row):
        for off_col in range(-2 - type_col, 4 - type_col):
            if max(abs(off_row), abs(off_col)) > 1:
                offsets.append((off_row, off_col))
    return offsets


def kernel_tables(rows_leaf, cols_leaf):
    points = jnp.arange(rows_leaf * cols_leaf, dtype=jnp.int32)
    point_row = (points // cols_leaf).astype(jnp.float32)
    point_col = (points % cols_leaf).astype(jnp.float32)
    tables = []
    for off_row in (-1, 0, 1):
        for off_col in (-1, 0, 1):
            apart_row = point_row[:, None] + off_row * rows_leaf - point_row[None, :]
            apart_col = point_col[:, None] + off_col * cols_leaf - point_col[None, :]
            scaled = jnp.sqrt(3.0 * (apart_row * apart_row + apart_col * apart_col)) / length_scale
            tables.append(((1.0 + scaled) * jnp.exp(-scaled)).astype(jnp.bfloat16))
    return jnp.stack(tables)


def along_rows(values, offset):
    return shifted(values, "gx", offset)


def along_cols(values, offset):
    return shifted(values, "gy", offset)


def tile_level(tile_size, height):
    nodes_dev = max(1, tile_size >> height)
    ascent = max(0, height - (tile_size.bit_length() - 1))
    return (nodes_dev, ascent)


def widen_dim(values, axis_dim, count_dev, nodes_dev, ascent, shifter):
    stride_dev = 1 << ascent
    reach_dev = 3 if nodes_dev == 1 else (nodes_dev + 2) // nodes_dev
    pieces = []
    for distance in range(reach_dev, 0, -1):
        moved = distance * stride_dev
        pieces.append(shifter(values, moved) if moved < count_dev else jnp.zeros_like(values))
    pieces.append(values)
    for distance in range(1, reach_dev + 1):
        moved = distance * stride_dev
        pieces.append(shifter(values, -moved) if moved < count_dev else jnp.zeros_like(values))
    joined = jnp.concatenate(pieces, axis=axis_dim)
    return lax.slice_in_dim(
        joined, reach_dev * nodes_dev - 3, reach_dev * nodes_dev + nodes_dev + 3, axis=axis_dim
    )


def join_types(first_part, second_part, axis_dim, nodes_dev, bit_value):
    if nodes_dev > 1:
        stacked = jnp.stack([first_part, second_part], axis=axis_dim + 1)
        target_shape = list(first_part.shape)
        target_shape[axis_dim] = 2 * target_shape[axis_dim]
        return stacked.reshape(target_shape)
    return jnp.where(bit_value == 0, first_part, second_part)


def far_terms(widened, coupling_level, ids_level, nodes_row, nodes_col, bit_row, bit_col):
    count_p, rank_size = (widened.shape[2], widened.shape[3])
    count_row = max(1, nodes_row // 2)
    count_col = max(1, nodes_col // 2)
    results = []
    for type_row in (0, 1):
        row_parts = []
        for type_col in (0, 1):
            first_row = type_row if nodes_row > 1 else 0
            first_col = type_col if nodes_col > 1 else 0
            offsets = slot_offsets(type_row, type_col)
            chosen = jnp.take(coupling_level, ids_level[2 * type_row + type_col], axis=0)
            chosen = chosen.reshape(len(offsets) * rank_size, rank_size)
            pieces = []
            for off_row, off_col in offsets:
                start_row = first_row + 3 + off_row
                start_col = first_col + 3 + off_col
                pieces.append(
                    lax.slice(
                        widened,
                        (start_row, start_col, 0, 0),
                        (
                            start_row + 2 * count_row - 1,
                            start_col + 2 * count_col - 1,
                            count_p,
                            rank_size,
                        ),
                        (2, 2, 1, 1),
                    )
                )
            stacked = jnp.concatenate(pieces, axis=3)
            summed = jnp.einsum(
                "ijpk,kq->ijpq", stacked, chosen, preferred_element_type=jnp.float32
            )
            row_parts.append(summed)
        results.append(join_types(row_parts[0], row_parts[1], 1, nodes_col, bit_col))
    return join_types(results[0], results[1], 0, nodes_row, bit_row)


def gather_children(values, axis_dim, nodes_dev, ascent, count_dev, shifter):
    if nodes_dev > 1:
        target_shape = list(values.shape)
        target_shape[axis_dim : axis_dim + 1] = [nodes_dev // 2, 2]
        return values.reshape(target_shape)
    if 1 << ascent >= count_dev:
        return jnp.stack([values, jnp.zeros_like(values)], axis=axis_dim + 1)
    partner = shifter(values, -(1 << ascent))
    return jnp.stack([values, partner], axis=axis_dim + 1)


def spread_parent(values, nodes_dev, ascent, count_dev, device_index, shifter):
    if nodes_dev > 1 or 1 << ascent >= count_dev:
        return values
    own_bit = device_index // (1 << ascent) % 2
    return jnp.where(own_bit == 1, shifter(values, 1 << ascent), values)


def pick_child(spread, axis_dim, nodes_dev, bit_value):
    if nodes_dev > 1:
        return spread
    return jnp.where(
        bit_value == 0,
        lax.slice_in_dim(spread, 0, 1, axis=axis_dim + 1),
        lax.slice_in_dim(spread, 1, 2, axis=axis_dim + 1),
    )


def shards(probes, leaf_basis, up_transfer, down_transfer, coupling, far_ids):
    tile_x, tile_y, count_p, leaf_size = probes.shape
    rank_size = leaf_basis.shape[1]
    levels = coupling.shape[0]
    rows_count = lax.axis_size("gx")
    cols_count = lax.axis_size("gy")
    row_index = lax.axis_index("gx")
    col_index = lax.axis_index("gy")
    padded = with_halo(probes, (("gx", 0), ("gy", 1)), 1)
    tables = kernel_tables(LEAF_ROWS, LEAF_COLS).reshape(9 * leaf_size, leaf_size)
    near_pieces = []
    for off_row in (-1, 0, 1):
        for off_col in (-1, 0, 1):
            near_pieces.append(
                padded[1 + off_row : 1 + off_row + tile_x, 1 + off_col : 1 + off_col + tile_y]
            )
    near_stack = jnp.concatenate(near_pieces, axis=3).reshape(-1, 9 * leaf_size)
    near_sum = jnp.dot(near_stack, tables, preferred_element_type=jnp.float32)
    first = jnp.dot(probes.reshape(-1, leaf_size), leaf_basis, preferred_element_type=jnp.float32)
    ladder = [first.reshape(tile_x, tile_y, count_p, rank_size).astype(jnp.bfloat16)]
    for height in range(levels - 1):
        nodes_row, ascent_row = tile_level(tile_x, height)
        nodes_col, ascent_col = tile_level(tile_y, height)
        grouped = gather_children(ladder[-1], 0, nodes_row, ascent_row, rows_count, along_rows)
        grouped = gather_children(grouped, 2, nodes_col, ascent_col, cols_count, along_cols)
        parent_coef = jnp.einsum(
            "iajbpr,abrq->ijpq",
            grouped,
            up_transfer[height].reshape(2, 2, rank_size, rank_size),
            preferred_element_type=jnp.float32,
        )
        ladder.append(parent_coef.astype(jnp.bfloat16))
    carried = None
    for height in reversed(range(levels)):
        nodes_row, ascent_row = tile_level(tile_x, height)
        nodes_col, ascent_col = tile_level(tile_y, height)
        bit_row = row_index // (1 << ascent_row) % 2
        bit_col = col_index // (1 << ascent_col) % 2
        widened = widen_dim(ladder[height], 0, rows_count, nodes_row, ascent_row, along_rows)
        widened = widen_dim(widened, 1, cols_count, nodes_col, ascent_col, along_cols)
        summed = far_terms(
            widened, coupling[height], far_ids[height], nodes_row, nodes_col, bit_row, bit_col
        )
        if carried is not None:
            parent = carried
            parent = spread_parent(parent, nodes_row, ascent_row, rows_count, row_index, along_rows)
            parent = spread_parent(parent, nodes_col, ascent_col, cols_count, col_index, along_cols)
            spread = jnp.einsum(
                "ijpr,abrq->iajbpq",
                parent,
                down_transfer[height].reshape(2, 2, rank_size, rank_size),
                preferred_element_type=jnp.float32,
            )
            spread = pick_child(spread, 0, nodes_row, bit_row)
            spread = pick_child(spread, 2, nodes_col, bit_col)
            summed = summed + spread.reshape(summed.shape)
        carried = summed.astype(jnp.bfloat16)
    far_sum = jnp.einsum(
        "nr,qr->nq", carried.reshape(-1, rank_size), leaf_basis, preferred_element_type=jnp.float32
    )
    return (near_sum + far_sum).reshape(tile_x, tile_y, count_p, leaf_size).astype(jnp.bfloat16)


def solution(mesh):
    in_specs = (P("gx", "gy", None, None), P(), P(), P(), P(), P())
    out_specs = P("gx", "gy", None, None)
    return jax.shard_map(shards, mesh=mesh, in_specs=in_specs, out_specs=out_specs, check_vma=False)
```

profile of v0, /device:TPU:1, one launch (start us, length us, event | category | flops | bytes accessed | tf_op | source)
XLA Modules:
  0.0 677.7 jit_solution(12341392390233094556)
XLA Ops:
  5.0 7.0 %collective-permute-start.10 = (bf16[1,4,32,64]{3,2,1,0:T(8,128)(2,1)}, bf16[1,4,32,64]{3,2,1,0:T(8,128)(2,1)}, u32[]{:S(2)}, u32[]{:S(2)}) collective-permute-start(bf16[1,4,32,64]{3,2,1,0:T(8,128)(2,1)} %bitcast.34), channel_id=1, source_target_pairs={{0,96},{32,128},{64,160},{96,192},{128,224},{160,256},{192,288},{2... | collective-permute-start | bytes 49160 | tf_op jit(solution)/shard_map/ppermute | solution.py:16
  12.0 3.8 collective-permute-start.11
  26.7 5.1 slice_bitcast_fusion.7
  133.3 6.6 collective-permute-start.4
  150.8 9.9 %collective-permute-start.18 = (bf16[1,2,32,64]{3,2,1,0:T(8,128)(2,1)S(1)}, bf16[1,2,32,64]{3,2,1,0:T(8,128)(2,1)S(1)}, u32[]{:S(2)}, u32[]{:S(2)}) collective-permute-start(bf16[1,2,32,64]{3,2,1,0:T(8,128)(2,1)S(1)} %bitcast.680), channel_id=1, source_target_pairs={{0,192},{32,224},{64,256},{96,288},{128,320},{160,352},{192,384},{... | collective-permute-start | bytes 24584 | tf_op jit(solution)/shard_map/ppermute | solution.py:16
  165.6 5.4 collective-permute-start.20
  174.3 3.8 collective-permute-done.21
  181.4 3.9 collective-permute-done.22
  187.8 4.4 collective-permute-done.23
  200.5 3.7 collective-permute-start.28
  211.6 4.0 collective-permute-done.30
  215.6 16.2 %collective-permute-start.38 = (bf16[1,2,1,32,64]{4,3,2,1,0:T(8,128)(2,1)S(1)}, bf16[1,2,1,32,64]{4,3,2,1,0:T(8,128)(2,1)S(1)}, u32[]{:S(2)}, u32[]{:S(2)}) collective-permute-start(bf16[1,2,1,32,64]{4,3,2,1,0:T(8,128)(2,1)S(1)} %get-tuple-element.415), channel_id=1, source_target_pairs={{1,0},{2,1},{3,2},{4,3},{5,4},{6,5},{7,6},{8,7},{9,8},{10,9},{11,1... | collective-permute-start | bytes 24584 | tf_op jit(solution)/shard_map/ppermute | solution.py:16
  236.2 4.1 collective-permute-done.31
  256.2 5.3 collective-permute-done.54
  261.6 8.0 %collective-permute-start.37 = (bf16[7,1,32,64]{3,2,1,0:T(8,128)(2,1)}, bf16[7,1,32,64]{3,2,1,0:T(8,128)(2,1)S(1)}, u32[]{:S(2)}, u32[]{:S(2)}) collective-permute-start(bf16[7,1,32,64]{3,2,1,0:T(8,128)(2,1)} %constant_dynamic-update-slice_fusion.40), channel_id=1, source_target_pairs={{0,3},{1,4},{2,5},{3,6},{4,7},{5,8},{6,9},{7,10},{8,11},{9,12},{10... | collective-permute-start | bytes 86024 | tf_op jit(solution)/shard_map/ppermute | solution.py:16
  272.2 4.4 collective-permute-start.32
  285.0 3.7 collective-permute-done.34
  290.5 4.2 collective-permute-done.35
  298.7 3.8 collective-permute-done.36
  310.3 3.6 collective-permute-done.61
  319.5 3.9 collective-permute-done.1
  323.4 21.3 %collective-permute-start.17 = (bf16[7,4,32,64]{3,2,1,0:T(8,128)(2,1)}, bf16[7,4,32,64]{3,2,1,0:T(8,128)(2,1)}, u32[]{:S(2)}, u32[]{:S(2)}) collective-permute-start(bf16[7,4,32,64]{3,2,1,0:T(8,128)(2,1)} %copy-done.63), channel_id=1, source_target_pairs={{1,0},{2,1},{3,2},{4,3},{5,4},{6,5},{7,6},{8,7},{9,8},{10,9},{11,1... | collective-permute-start | bytes 344072 | tf_op jit(solution)/shard_map/ppermute | solution.py:16
  345.3 19.0 %collective-permute-start.16 = (bf16[7,4,32,64]{3,2,1,0:T(8,128)(2,1)}, bf16[7,4,32,64]{3,2,1,0:T(8,128)(2,1)}, u32[]{:S(2)}, u32[]{:S(2)}) collective-permute-start(bf16[7,4,32,64]{3,2,1,0:T(8,128)(2,1)} %copy-done.63), channel_id=1, source_target_pairs={{0,1},{1,2},{2,3},{3,4},{4,5},{5,6},{6,7},{7,8},{8,9},{9,10},{10,1... | collective-permute-start | bytes 344072 | tf_op jit(solution)/shard_map/ppermute | solution.py:16
  365.2 3.7 collective-permute-start.24
  369.9 5.0 collective-permute-start.25
  375.8 3.8 collective-permute-start.46
  381.3 5.6 collective-permute-start.41
  388.5 5.1 collective-permute-start.42
  402.4 5.6 collective-permute-done.44
  412.6 6.5 collective-permute-done.45
  419.2 10.5 %collective-permute-start.53 = (bf16[7,1,32,64]{3,2,1,0:T(8,128)(2,1)}, bf16[7,1,32,64]{3,2,1,0:T(8,128)(2,1)}, u32[]{:S(2)}, u32[]{:S(2)}) collective-permute-start(bf16[7,1,32,64]{3,2,1,0:T(8,128)(2,1)} %constant_dynamic-update-slice_fusion.52), channel_id=1, source_target_pairs={{0,12},{1,13},{2,14},{3,15},{4,16},{5,17},{6,18},{7,19},{8,20},{9,... | collective-permute-start | bytes 86024 | tf_op jit(solution)/shard_map/ppermute | solution.py:16
  437.7 3.9 collective-permute-start.48
  447.8 8.4 %collective-permute-done.50 = bf16[7,1,32,64]{3,2,1,0:T(8,128)(2,1)S(1)} collective-permute-done((bf16[7,1,32,64]{3,2,1,0:T(8,128)(2,1)}, bf16[7,1,32,64]{3,2,1,0:T(8,128)(2,1)S(1)}, u32[]{:S(2)}, u32[]{:S(2)}) %collective-permute-start.50) | collective-permute-done | bytes 28704 | tf_op jit(solution)/shard_map/ppermute | solution.py:16
  458.1 8.6 %collective-permute-done.51 = bf16[7,1,32,64]{3,2,1,0:T(8,128)(2,1)S(1)} collective-permute-done((bf16[7,1,32,64]{3,2,1,0:T(8,128)(2,1)}, bf16[7,1,32,64]{3,2,1,0:T(8,128)(2,1)S(1)}, u32[]{:S(2)}, u32[]{:S(2)}) %collective-permute-start.51) | collective-permute-done | bytes 28704 | tf_op jit(solution)/shard_map/ppermute | solution.py:16
  471.5 6.2 collective-permute-done.52
  477.6 7.6 %collective-permute-start.60 = (bf16[7,1,32,64]{3,2,1,0:T(8,128)(2,1)}, bf16[7,1,32,64]{3,2,1,0:T(8,128)(2,1)}, u32[]{:S(2)}, u32[]{:S(2)}) collective-permute-start(bf16[7,1,32,64]{3,2,1,0:T(8,128)(2,1)} %constant_dynamic-update-slice_fusion.57), channel_id=1, source_target_pairs={{0,24},{1,25},{2,26},{3,27},{4,28},{5,29},{6,30},{7,31},{32,56},{3... | collective-permute-start | bytes 86024 | tf_op jit(solution)/shard_map/ppermute | solution.py:16
  493.9 5.7 collective-permute-start.55
  526.4 12.4 %collective-permute-start.62 = (bf16[7,1,32,64]{3,2,1,0:T(8,128)(2,1)}, bf16[7,1,32,64]{3,2,1,0:T(8,128)(2,1)}, u32[]{:S(2)}, u32[]{:S(2)}) collective-permute-start(bf16[7,1,32,64]{3,2,1,0:T(8,128)(2,1)} %constant_dynamic-update-slice_fusion.62), channel_id=1, source_target_pairs={{0,16},{1,17},{2,18},{3,19},{4,20},{5,21},{6,22},{7,23},{8,24},{9,... | collective-permute-start | bytes 86024 | tf_op jit(solution)/shard_map/ppermute | solution.py:16
  543.1 36.2 %collective-permute-start.9 = (bf16[8,8,32,64]{3,2,1,0:T(8,128)(2,1)S(1)}, bf16[8,8,32,64]{3,2,1,0:T(8,128)(2,1)}, u32[]{:S(2)}, u32[]{:S(2)}) collective-permute-start(bf16[8,8,32,64]{3,2,1,0:T(8,128)(2,1)S(1)} %slice.2347), channel_id=1, source_target_pairs={{1,0},{2,1},{3,2},{4,3},{5,4},{6,5},{7,6},{8,7},{9,8},{10,9},{11,1... | collective-permute-start | bytes 786440 | tf_op jit(solution)/shard_map/ppermute | solution.py:16
  585.2 19.0 %collective-permute-start.8 = (bf16[8,8,32,64]{3,2,1,0:T(8,128)(2,1)S(1)}, bf16[8,8,32,64]{3,2,1,0:T(8,128)(2,1)}, u32[]{:S(2)}, u32[]{:S(2)}) collective-permute-start(bf16[8,8,32,64]{3,2,1,0:T(8,128)(2,1)S(1)} %slice.2347), channel_id=1, source_target_pairs={{0,1},{1,2},{2,3},{3,4},{4,5},{5,6},{6,7},{7,8},{8,9},{9,10},{10,1... | collective-permute-start | bytes 786440 | tf_op jit(solution)/shard_map/ppermute | solution.py:16
  608.4 8.3 %collective-permute-start.64 = (bf16[1,1,32,64]{3,2,1,0:T(8,128)(2,1)S(1)}, bf16[1,1,32,64]{3,2,1,0:T(8,128)(2,1)S(1)}, u32[]{:S(2)}, u32[]{:S(2)}) collective-permute-start(bf16[1,1,32,64]{3,2,1,0:T(8,128)(2,1)S(1)} %fusion.24), channel_id=1, source_target_pairs={{0,8},{1,9},{2,10},{3,11},{4,12},{5,13},{6,14},{7,15},{8,16},{9,17... | collective-permute-start | bytes 12296 | tf_op jit(solution)/shard_map/ppermute | solution.py:16
  617.5 4.4 collective-permute-start.2
  624.9 3.8 collective-permute-done.3
  628.7 4.5 collective-permute-start.65
  634.4 4.9 collective-permute-start.66
  640.1 5.8 collective-permute-start.67
  650.3 5.3 collective-permute-start.69
  656.7 4.6 collective-permute-start.70
  (832 shorter events, 324.1 us)
Async XLA Ops:
  3.8 141.8 %collective-permute-start.13 = (bf16[1,4,32,64]{3,2,1,0:T(8,128)(2,1)}, bf16[1,4,32,64]{3,2,1,0:T(8,128)(2,1)}, u32[]{:S(2)}, u32[]{:S(2)}) collective-permute-start(bf16[1,4,32,64]{3,2,1,0:T(8,128)(2,1)} %bitcast.34), channel_id=1, source_target_pairs={{32,0},{64,32},{96,64},{128,96},{160,128},{192,160},{224,192},{256... | collective-permute-start | bytes 49160 | tf_op jit(solution)/shard_map/ppermute | solution.py:16
  5.0 126.1 %collective-permute-start.10 = (bf16[1,4,32,64]{3,2,1,0:T(8,128)(2,1)}, bf16[1,4,32,64]{3,2,1,0:T(8,128)(2,1)}, u32[]{:S(2)}, u32[]{:S(2)}) collective-permute-start(bf16[1,4,32,64]{3,2,1,0:T(8,128)(2,1)} %bitcast.34), channel_id=1, source_target_pairs={{0,96},{32,128},{64,160},{96,192},{128,224},{160,256},{192,288},{2... | collective-permute-start | bytes 49160 | tf_op jit(solution)/shard_map/ppermute | solution.py:16
  12.0 121.3 %collective-permute-start.11 = (bf16[1,4,32,64]{3,2,1,0:T(8,128)(2,1)}, bf16[1,4,32,64]{3,2,1,0:T(8,128)(2,1)}, u32[]{:S(2)}, u32[]{:S(2)}) collective-permute-start(bf16[1,4,32,64]{3,2,1,0:T(8,128)(2,1)} %bitcast.34), channel_id=1, source_target_pairs={{0,64},{32,96},{64,128},{96,160},{128,192},{160,224},{192,256},{22... | collective-permute-start | bytes 49160 | tf_op jit(solution)/shard_map/ppermute | solution.py:16
  15.8 124.8 %collective-permute-start.12 = (bf16[1,4,32,64]{3,2,1,0:T(8,128)(2,1)}, bf16[1,4,32,64]{3,2,1,0:T(8,128)(2,1)}, u32[]{:S(2)}, u32[]{:S(2)}) collective-permute-start(bf16[1,4,32,64]{3,2,1,0:T(8,128)(2,1)} %bitcast.34), channel_id=1, source_target_pairs={{0,32},{32,64},{64,96},{96,128},{128,160},{160,192},{192,224},{224... | collective-permute-start | bytes 49160 | tf_op jit(solution)/shard_map/ppermute | solution.py:16
  18.3 130.4 %collective-permute-start.14 = (bf16[1,4,32,64]{3,2,1,0:T(8,128)(2,1)}, bf16[1,4,32,64]{3,2,1,0:T(8,128)(2,1)}, u32[]{:S(2)}, u32[]{:S(2)}) collective-permute-start(bf16[1,4,32,64]{3,2,1,0:T(8,128)(2,1)} %bitcast.34), channel_id=1, source_target_pairs={{64,0},{96,32},{128,64},{160,96},{192,128},{224,160},{256,192},{28... | collective-permute-start | bytes 49160 | tf_op jit(solution)/shard_map/ppermute | solution.py:16
  131.1 19.7 %collective-permute-start.15 = (bf16[1,4,32,64]{3,2,1,0:T(8,128)(2,1)}, bf16[1,4,32,64]{3,2,1,0:T(8,128)(2,1)S(1)}, u32[]{:S(2)}, u32[]{:S(2)}) collective-permute-start(bf16[1,4,32,64]{3,2,1,0:T(8,128)(2,1)} %bitcast.34), channel_id=1, source_target_pairs={{96,0},{128,32},{160,64},{192,96},{224,128},{256,160},{288,192},{3... | collective-permute-start | bytes 49160 | tf_op jit(solution)/shard_map/ppermute | solution.py:16
  133.3 212.0 %collective-permute-start.4 = (bf16[2,8,32,64]{3,2,1,0:T(8,128)(2,1)S(1)}, bf16[2,8,32,64]{3,2,1,0:T(8,128)(2,1)}, u32[]{:S(2)}, u32[]{:S(2)}) collective-permute-start(bf16[2,8,32,64]{3,2,1,0:T(8,128)(2,1)S(1)} %convolution_convert_fusion), channel_id=1, source_target_pairs={{0,64},{32,96},{64,128},{96,160},{128,192},{160,224},{192,256},{22... | collective-permute-start | bytes 196616 | tf_op jit(solution)/shard_map/ppermute | solution.py:16
  140.6 224.6 %collective-permute-start.5 = (bf16[2,8,32,64]{3,2,1,0:T(8,128)(2,1)S(1)}, bf16[2,8,32,64]{3,2,1,0:T(8,128)(2,1)}, u32[]{:S(2)}, u32[]{:S(2)}) collective-permute-start(bf16[2,8,32,64]{3,2,1,0:T(8,128)(2,1)S(1)} %convolution_convert_fusion), channel_id=1, source_target_pairs={{0,32},{32,64},{64,96},{96,128},{128,160},{160,192},{192,224},{224... | collective-permute-start | bytes 196616 | tf_op jit(solution)/shard_map/ppermute | solution.py:16
  145.6 224.3 %collective-permute-start.6 = (bf16[2,8,32,64]{3,2,1,0:T(8,128)(2,1)S(1)}, bf16[2,8,32,64]{3,2,1,0:T(8,128)(2,1)}, u32[]{:S(2)}, u32[]{:S(2)}) collective-permute-start(bf16[2,8,32,64]{3,2,1,0:T(8,128)(2,1)S(1)} %convolution_convert_fusion), channel_id=1, source_target_pairs={{32,0},{64,32},{96,64},{128,96},{160,128},{192,160},{224,192},{256... | collective-permute-start | bytes 196616 | tf_op jit(solution)/shard_map/ppermute | solution.py:16
  148.7 227.1 %collective-permute-start.7 = (bf16[2,8,32,64]{3,2,1,0:T(8,128)(2,1)S(1)}, bf16[2,8,32,64]{3,2,1,0:T(8,128)(2,1)}, u32[]{:S(2)}, u32[]{:S(2)}) collective-permute-start(bf16[2,8,32,64]{3,2,1,0:T(8,128)(2,1)S(1)} %convolution_convert_fusion), channel_id=1, source_target_pairs={{64,0},{96,32},{128,64},{160,96},{192,128},{224,160},{256,192},{28... | collective-permute-start | bytes 196616 | tf_op jit(solution)/shard_map/ppermute | solution.py:16
  150.8 10.7 %collective-permute-start.18 = (bf16[1,2,32,64]{3,2,1,0:T(8,128)(2,1)S(1)}, bf16[1,2,32,64]{3,2,1,0:T(8,128)(2,1)S(1)}, u32[]{:S(2)}, u32[]{:S(2)}) collective-permute-start(bf16[1,2,32,64]{3,2,1,0:T(8,128)(2,1)S(1)} %bitcast.680), channel_id=1, source_target_pairs={{0,192},{32,224},{64,256},{96,288},{128,320},{160,352},{192,384},{... | collective-permute-start | bytes 24584 | tf_op jit(solution)/shard_map/ppermute | solution.py:16
  165.6 6.3 collective-permute-start.20
  171.8 6.2 collective-permute-start.21
  178.1 7.2 %collective-permute-start.22 = (bf16[1,2,32,64]{3,2,1,0:T(8,128)(2,1)S(1)}, bf16[1,2,32,64]{3,2,1,0:T(8,128)(2,1)S(1)}, u32[]{:S(2)}, u32[]{:S(2)}) collective-permute-start(bf16[1,2,32,64]{3,2,1,0:T(8,128)(2,1)S(1)} %bitcast.684), channel_id=1, source_target_pairs={{128,0},{160,32},{192,64},{224,96},{256,128},{288,160},{320,192},{... | collective-permute-start | bytes 24584 | tf_op jit(solution)/shard_map/ppermute | solution.py:16
  185.3 6.9 %collective-permute-start.23 = (bf16[1,2,32,64]{3,2,1,0:T(8,128)(2,1)S(1)}, bf16[1,2,32,64]{3,2,1,0:T(8,128)(2,1)S(1)}, u32[]{:S(2)}, u32[]{:S(2)}) collective-permute-start(bf16[1,2,32,64]{3,2,1,0:T(8,128)(2,1)S(1)} %bitcast.686), channel_id=1, source_target_pairs={{192,0},{224,32},{256,64},{288,96},{320,128},{352,160},{384,192},{... | collective-permute-start | bytes 24584 | tf_op jit(solution)/shard_map/ppermute | solution.py:16
  215.6 19.2 %collective-permute-start.38 = (bf16[1,2,1,32,64]{4,3,2,1,0:T(8,128)(2,1)S(1)}, bf16[1,2,1,32,64]{4,3,2,1,0:T(8,128)(2,1)S(1)}, u32[]{:S(2)}, u32[]{:S(2)}) collective-permute-start(bf16[1,2,1,32,64]{4,3,2,1,0:T(8,128)(2,1)S(1)} %get-tuple-element.415), channel_id=1, source_target_pairs={{1,0},{2,1},{3,2},{4,3},{5,4},{6,5},{7,6},{8,7},{9,8},{10,9},{11,1... | collective-permute-start | bytes 24584 | tf_op jit(solution)/shard_map/ppermute | solution.py:16
  254.3 7.2 %collective-permute-start.54 = (bf16[1,2,1,32,64]{4,3,2,1,0:T(8,128)(2,1)S(1)}, bf16[1,2,1,32,64]{4,3,2,1,0:T(8,128)(2,1)S(1)}, u32[]{:S(2)}, u32[]{:S(2)}) collective-permute-start(bf16[1,2,1,32,64]{4,3,2,1,0:T(8,128)(2,1)S(1)} %get-tuple-element.419), channel_id=1, source_target_pairs={{4,0},{5,1},{6,2},{7,3},{8,4},{9,5},{10,6},{11,7},{12,8},{13,9},{1... | collective-permute-start | bytes 24584 | tf_op jit(solution)/shard_map/ppermute | solution.py:16
  261.6 10.6 %collective-permute-start.37 = (bf16[7,1,32,64]{3,2,1,0:T(8,128)(2,1)}, bf16[7,1,32,64]{3,2,1,0:T(8,128)(2,1)S(1)}, u32[]{:S(2)}, u32[]{:S(2)}) collective-permute-start(bf16[7,1,32,64]{3,2,1,0:T(8,128)(2,1)} %constant_dynamic-update-slice_fusion.40), channel_id=1, source_target_pairs={{0,3},{1,4},{2,5},{3,6},{4,7},{5,8},{6,9},{7,10},{8,11},{9,12},{10... | collective-permute-start | bytes 86024 | tf_op jit(solution)/shard_map/ppermute | solution.py:16
  282.4 6.2 collective-permute-start.34
  288.6 6.1 collective-permute-start.35
  294.7 7.7 %collective-permute-start.36 = (bf16[7,1,32,64]{3,2,1,0:T(8,128)(2,1)}, bf16[7,1,32,64]{3,2,1,0:T(8,128)(2,1)}, u32[]{:S(2)}, u32[]{:S(2)}) collective-permute-start(bf16[7,1,32,64]{3,2,1,0:T(8,128)(2,1)} %constant_dynamic-update-slice_fusion.40), channel_id=1, source_target_pairs={{3,0},{4,1},{5,2},{6,3},{7,4},{8,5},{9,6},{10,7},{11,8},{12,9},{13... | collective-permute-start | bytes 86024 | tf_op jit(solution)/shard_map/ppermute | solution.py:16
  302.5 11.5 %collective-permute-start.61 = (bf16[1,2,1,32,64]{4,3,2,1,0:T(8,128)(2,1)}, bf16[1,2,1,32,64]{4,3,2,1,0:T(8,128)(2,1)S(1)}, u32[]{:S(2)}, u32[]{:S(2)}) collective-permute-start(bf16[1,2,1,32,64]{4,3,2,1,0:T(8,128)(2,1)} %get-tuple-element.417), channel_id=1, source_target_pairs={{8,0},{9,1},{10,2},{11,3},{12,4},{13,5},{14,6},{15,7},{16,8},{17,9... | collective-permute-start | bytes 24584 | tf_op jit(solution)/shard_map/ppermute | solution.py:16
  323.4 341.4 %collective-permute-start.17 = (bf16[7,4,32,64]{3,2,1,0:T(8,128)(2,1)}, bf16[7,4,32,64]{3,2,1,0:T(8,128)(2,1)}, u32[]{:S(2)}, u32[]{:S(2)}) collective-permute-start(bf16[7,4,32,64]{3,2,1,0:T(8,128)(2,1)} %copy-done.63), channel_id=1, source_target_pairs={{1,0},{2,1},{3,2},{4,3},{5,4},{6,5},{7,6},{8,7},{9,8},{10,9},{11,1... | collective-permute-start | bytes 344072 | tf_op jit(solution)/shard_map/ppermute | solution.py:16
  345.3 319.5 %collective-permute-start.16 = (bf16[7,4,32,64]{3,2,1,0:T(8,128)(2,1)}, bf16[7,4,32,64]{3,2,1,0:T(8,128)(2,1)}, u32[]{:S(2)}, u32[]{:S(2)}) collective-permute-start(bf16[7,4,32,64]{3,2,1,0:T(8,128)(2,1)} %copy-done.63), channel_id=1, source_target_pairs={{0,1},{1,2},{2,3},{3,4},{4,5},{5,6},{6,7},{7,8},{8,9},{9,10},{10,1... | collective-permute-start | bytes 344072 | tf_op jit(solution)/shard_map/ppermute | solution.py:16
  365.2 128.7 %collective-permute-start.24 = (bf16[7,2,32,64]{3,2,1,0:T(8,128)(2,1)}, bf16[7,2,32,64]{3,2,1,0:T(8,128)(2,1)}, u32[]{:S(2)}, u32[]{:S(2)}) collective-permute-start(bf16[7,2,32,64]{3,2,1,0:T(8,128)(2,1)} %constant_dynamic-update-slice_fusion.33), channel_id=1, source_target_pairs={{0,1},{1,2},{2,3},{3,4},{4,5},{5,6},{6,7},{7,8},{8,9},{9,10},{10,1... | collective-permute-start | bytes 172040 | tf_op jit(solution)/shard_map/ppermute | solution.py:16
  369.9 131.3 %collective-permute-start.25 = (bf16[7,2,32,64]{3,2,1,0:T(8,128)(2,1)}, bf16[7,2,32,64]{3,2,1,0:T(8,128)(2,1)}, u32[]{:S(2)}, u32[]{:S(2)}) collective-permute-start(bf16[7,2,32,64]{3,2,1,0:T(8,128)(2,1)} %constant_dynamic-update-slice_fusion.33), channel_id=1, source_target_pairs={{1,0},{2,1},{3,2},{4,3},{5,4},{6,5},{7,6},{8,7},{9,8},{10,9},{11,1... | collective-permute-start | bytes 172040 | tf_op jit(solution)/shard_map/ppermute | solution.py:16
  381.3 7.2 %collective-permute-start.41 = (bf16[7,1,32,64]{3,2,1,0:T(8,128)(2,1)}, bf16[7,1,32,64]{3,2,1,0:T(8,128)(2,1)S(1)}, u32[]{:S(2)}, u32[]{:S(2)}) collective-permute-start(bf16[7,1,32,64]{3,2,1,0:T(8,128)(2,1)} %constant_dynamic-update-slice_fusion.47), channel_id=1, source_target_pairs={{0,4},{1,5},{2,6},{3,7},{4,8},{5,9},{6,10},{7,11},{8,12},{9,13},{1... | collective-permute-start | bytes 86024 | tf_op jit(solution)/shard_map/ppermute | solution.py:16
  388.5 6.6 collective-permute-start.42
  400.5 7.5 %collective-permute-start.44 = (bf16[7,1,32,64]{3,2,1,0:T(8,128)(2,1)}, bf16[7,1,32,64]{3,2,1,0:T(8,128)(2,1)S(1)}, u32[]{:S(2)}, u32[]{:S(2)}) collective-permute-start(bf16[7,1,32,64]{3,2,1,0:T(8,128)(2,1)} %constant_dynamic-update-slice_fusion.47), channel_id=1, source_target_pairs={{4,0},{5,1},{6,2},{7,3},{8,4},{9,5},{10,6},{11,7},{12,8},{13,9},{1... | collective-permute-start | bytes 86024 | tf_op jit(solution)/shard_map/ppermute | solution.py:16
  408.0 11.1 %collective-permute-start.45 = (bf16[7,1,32,64]{3,2,1,0:T(8,128)(2,1)}, bf16[7,1,32,64]{3,2,1,0:T(8,128)(2,1)}, u32[]{:S(2)}, u32[]{:S(2)}) collective-permute-start(bf16[7,1,32,64]{3,2,1,0:T(8,128)(2,1)} %constant_dynamic-update-slice_fusion.47), channel_id=1, source_target_pairs={{6,0},{7,1},{8,2},{9,3},{10,4},{11,5},{12,6},{13,7},{14,8},{15,9},... | collective-permute-start | bytes 86024 | tf_op jit(solution)/shard_map/ppermute | solution.py:16
  419.2 18.5 %collective-permute-start.53 = (bf16[7,1,32,64]{3,2,1,0:T(8,128)(2,1)}, bf16[7,1,32,64]{3,2,1,0:T(8,128)(2,1)}, u32[]{:S(2)}, u32[]{:S(2)}) collective-permute-start(bf16[7,1,32,64]{3,2,1,0:T(8,128)(2,1)} %constant_dynamic-update-slice_fusion.52), channel_id=1, source_target_pairs={{0,12},{1,13},{2,14},{3,15},{4,16},{5,17},{6,18},{7,19},{8,20},{9,... | collective-permute-start | bytes 86024 | tf_op jit(solution)/shard_map/ppermute | solution.py:16
  445.9 10.3 %collective-permute-start.50 = (bf16[7,1,32,64]{3,2,1,0:T(8,128)(2,1)}, bf16[7,1,32,64]{3,2,1,0:T(8,128)(2,1)S(1)}, u32[]{:S(2)}, u32[]{:S(2)}) collective-permute-start(bf16[7,1,32,64]{3,2,1,0:T(8,128)(2,1)} %constant_dynamic-update-slice_fusion.52), channel_id=1, source_target_pairs={{4,0},{5,1},{6,2},{7,3},{8,4},{9,5},{10,6},{11,7},{12,8},{13,9},{1... | collective-permute-start | bytes 86024 | tf_op jit(solution)/shard_map/ppermute | solution.py:16
  456.2 10.5 %collective-permute-start.51 = (bf16[7,1,32,64]{3,2,1,0:T(8,128)(2,1)}, bf16[7,1,32,64]{3,2,1,0:T(8,128)(2,1)S(1)}, u32[]{:S(2)}, u32[]{:S(2)}) collective-permute-start(bf16[7,1,32,64]{3,2,1,0:T(8,128)(2,1)} %constant_dynamic-update-slice_fusion.52), channel_id=1, source_target_pairs={{8,0},{9,1},{10,2},{11,3},{12,4},{13,5},{14,6},{15,7},{16,8},{17,9... | collective-permute-start | bytes 86024 | tf_op jit(solution)/shard_map/ppermute | solution.py:16
  466.7 10.9 %collective-permute-start.52 = (bf16[7,1,32,64]{3,2,1,0:T(8,128)(2,1)}, bf16[7,1,32,64]{3,2,1,0:T(8,128)(2,1)}, u32[]{:S(2)}, u32[]{:S(2)}) collective-permute-start(bf16[7,1,32,64]{3,2,1,0:T(8,128)(2,1)} %constant_dynamic-update-slice_fusion.52), channel_id=1, source_target_pairs={{12,0},{13,1},{14,2},{15,3},{16,4},{17,5},{18,6},{19,7},{20,8},{21... | collective-permute-start | bytes 86024 | tf_op jit(solution)/shard_map/ppermute | solution.py:16
  477.6 39.7 %collective-permute-start.60 = (bf16[7,1,32,64]{3,2,1,0:T(8,128)(2,1)}, bf16[7,1,32,64]{3,2,1,0:T(8,128)(2,1)}, u32[]{:S(2)}, u32[]{:S(2)}) collective-permute-start(bf16[7,1,32,64]{3,2,1,0:T(8,128)(2,1)} %constant_dynamic-update-slice_fusion.57), channel_id=1, source_target_pairs={{0,24},{1,25},{2,26},{3,27},{4,28},{5,29},{6,30},{7,31},{32,56},{3... | collective-permute-start | bytes 86024 | tf_op jit(solution)/shard_map/ppermute | solution.py:16
  493.9 26.1 %collective-permute-start.55 = (bf16[7,1,32,64]{3,2,1,0:T(8,128)(2,1)}, bf16[7,1,32,64]{3,2,1,0:T(8,128)(2,1)}, u32[]{:S(2)}, u32[]{:S(2)}) collective-permute-start(bf16[7,1,32,64]{3,2,1,0:T(8,128)(2,1)} %constant_dynamic-update-slice_fusion.57), channel_id=1, source_target_pairs={{0,16},{1,17},{2,18},{3,19},{4,20},{5,21},{6,22},{7,23},{8,24},{9,... | collective-permute-start | bytes 86024 | tf_op jit(solution)/shard_map/ppermute | solution.py:16
  501.1 21.6 %collective-permute-start.56 = (bf16[7,1,32,64]{3,2,1,0:T(8,128)(2,1)}, bf16[7,1,32,64]{3,2,1,0:T(8,128)(2,1)}, u32[]{:S(2)}, u32[]{:S(2)}) collective-permute-start(bf16[7,1,32,64]{3,2,1,0:T(8,128)(2,1)} %constant_dynamic-update-slice_fusion.57), channel_id=1, source_target_pairs={{0,8},{1,9},{2,10},{3,11},{4,12},{5,13},{6,14},{7,15},{8,16},{9,17... | collective-permute-start | bytes 86024 | tf_op jit(solution)/shard_map/ppermute | solution.py:16
  517.3 9.0 %collective-permute-start.57 = (bf16[7,1,32,64]{3,2,1,0:T(8,128)(2,1)}, bf16[7,1,32,64]{3,2,1,0:T(8,128)(2,1)S(1)}, u32[]{:S(2)}, u32[]{:S(2)}) collective-permute-start(bf16[7,1,32,64]{3,2,1,0:T(8,128)(2,1)} %constant_dynamic-update-slice_fusion.57), channel_id=1, source_target_pairs={{8,0},{9,1},{10,2},{11,3},{12,4},{13,5},{14,6},{15,7},{16,8},{17,9... | collective-permute-start | bytes 86024 | tf_op jit(solution)/shard_map/ppermute | solution.py:16
  520.1 19.3 %collective-permute-start.58 = (bf16[7,1,32,64]{3,2,1,0:T(8,128)(2,1)}, bf16[7,1,32,64]{3,2,1,0:T(8,128)(2,1)S(1)}, u32[]{:S(2)}, u32[]{:S(2)}) collective-permute-start(bf16[7,1,32,64]{3,2,1,0:T(8,128)(2,1)} %constant_dynamic-update-slice_fusion.57), channel_id=1, source_target_pairs={{16,0},{17,1},{18,2},{19,3},{20,4},{21,5},{22,6},{23,7},{24,8},{25... | collective-permute-start | bytes 86024 | tf_op jit(solution)/shard_map/ppermute | solution.py:16
  522.8 20.3 %collective-permute-start.59 = (bf16[7,1,32,64]{3,2,1,0:T(8,128)(2,1)}, bf16[7,1,32,64]{3,2,1,0:T(8,128)(2,1)}, u32[]{:S(2)}, u32[]{:S(2)}) collective-permute-start(bf16[7,1,32,64]{3,2,1,0:T(8,128)(2,1)} %constant_dynamic-update-slice_fusion.57), channel_id=1, source_target_pairs={{24,0},{25,1},{26,2},{27,3},{28,4},{29,5},{30,6},{31,7},{56,32},{5... | collective-permute-start | bytes 86024 | tf_op jit(solution)/shard_map/ppermute | solution.py:16
  526.4 58.8 %collective-permute-start.62 = (bf16[7,1,32,64]{3,2,1,0:T(8,128)(2,1)}, bf16[7,1,32,64]{3,2,1,0:T(8,128)(2,1)}, u32[]{:S(2)}, u32[]{:S(2)}) collective-permute-start(bf16[7,1,32,64]{3,2,1,0:T(8,128)(2,1)} %constant_dynamic-update-slice_fusion.62), channel_id=1, source_target_pairs={{0,16},{1,17},{2,18},{3,19},{4,20},{5,21},{6,22},{7,23},{8,24},{9,... | collective-permute-start | bytes 86024 | tf_op jit(solution)/shard_map/ppermute | solution.py:16
  539.4 65.5 %collective-permute-start.63 = (bf16[7,1,32,64]{3,2,1,0:T(8,128)(2,1)}, bf16[7,1,32,64]{3,2,1,0:T(8,128)(2,1)}, u32[]{:S(2)}, u32[]{:S(2)}) collective-permute-start(bf16[7,1,32,64]{3,2,1,0:T(8,128)(2,1)} %constant_dynamic-update-slice_fusion.62), channel_id=1, source_target_pairs={{16,0},{17,1},{18,2},{19,3},{20,4},{21,5},{22,6},{23,7},{24,8},{25... | collective-permute-start | bytes 86024 | tf_op jit(solution)/shard_map/ppermute | solution.py:16
  543.1 126.1 %collective-permute-start.9 = (bf16[8,8,32,64]{3,2,1,0:T(8,128)(2,1)S(1)}, bf16[8,8,32,64]{3,2,1,0:T(8,128)(2,1)}, u32[]{:S(2)}, u32[]{:S(2)}) collective-permute-start(bf16[8,8,32,64]{3,2,1,0:T(8,128)(2,1)S(1)} %slice.2347), channel_id=1, source_target_pairs={{1,0},{2,1},{3,2},{4,3},{5,4},{6,5},{7,6},{8,7},{9,8},{10,9},{11,1... | collective-permute-start | bytes 786440 | tf_op jit(solution)/shard_map/ppermute | solution.py:16
  585.2 84.1 %collective-permute-start.8 = (bf16[8,8,32,64]{3,2,1,0:T(8,128)(2,1)S(1)}, bf16[8,8,32,64]{3,2,1,0:T(8,128)(2,1)}, u32[]{:S(2)}, u32[]{:S(2)}) collective-permute-start(bf16[8,8,32,64]{3,2,1,0:T(8,128)(2,1)S(1)} %slice.2347), channel_id=1, source_target_pairs={{0,1},{1,2},{2,3},{3,4},{4,5},{5,6},{6,7},{7,8},{8,9},{9,10},{10,1... | collective-permute-start | bytes 786440 | tf_op jit(solution)/shard_map/ppermute | solution.py:16
  608.4 9.0 %collective-permute-start.64 = (bf16[1,1,32,64]{3,2,1,0:T(8,128)(2,1)S(1)}, bf16[1,1,32,64]{3,2,1,0:T(8,128)(2,1)S(1)}, u32[]{:S(2)}, u32[]{:S(2)}) collective-permute-start(bf16[1,1,32,64]{3,2,1,0:T(8,128)(2,1)S(1)} %fusion.24), channel_id=1, source_target_pairs={{0,8},{1,9},{2,10},{3,11},{4,12},{5,13},{6,14},{7,15},{8,16},{9,17... | collective-permute-start | bytes 12296 | tf_op jit(solution)/shard_map/ppermute | solution.py:16
  640.1 6.5 collective-permute-start.67
  650.3 6.1 collective-permute-start.69
  662.3 6.5 collective-permute-start.71
  (243 other events, 2623.7 us)
where the time goes:
time: 691 us; the launch traced here: 678 us
  starting transfers between devices  332 us (48%)
  local copies, waits for them, and re-layouts  153 us (22%)
  waiting for transfers between devices  111 us (16%)
  other arithmetic  42.4 us (6%)
  matrix products  35.2 us (5%)
    ppermute x68, starting transfers between devices, shifted(): return lax.ppermute(block, axis, route)  323 us
    ppermute x68, waiting for transfers between devices, shifted(): return lax.ppermute(block, axis, route)  103 us
    gather x32, local copies, waits for them, and re-layouts, far_terms(): jnp.take(coupling_level, ids_level[2 * type_row + type_col], axis=0)  59.3 us
    dot_general x32, matrix products, far_terms(): jnp.einsum('ijpk,kq->ijpq', stacked, chosen, preferred_element_type=jnp.f...  27.2 us
    slice x36, local copies, waits for them, and re-layouts, far_terms(): lax.slice(widened, (start_row, start_col, 0, 0), (start_row + 2 * count_r...  27.1 us
    concatenate x32, local copies, waits for them, and re-layouts, far_terms(): stacked = jnp.concatenate(pieces, axis=3)  26.2 us
    unnamed x476, local copies, waits for them, and re-layouts  26.1 us
    select_n x28, other arithmetic, far_terms(): jnp.take(coupling_level, ids_level[2 * type_row + type_col], axis=0)  21.4 us
  transfers between devices with their start and end apart: 72, of which 44 were waited for; matrix products, arithmetic and copies ran while one was open for 32% of the time, Pallas kernels for 0%

commit v1 on v0

v1 whole, which is shorter than its diff:
```python
import jax
import jax.numpy as jnp
from jax import lax
from jax.experimental import pallas as pl
from jax.experimental.pallas import tpu as pltpu
from jax.sharding import PartitionSpec as P

LEAF_ROWS = 8
LEAF_COLS = 16
RANK = 64
PROBES = 32
BF = jnp.bfloat16
F32 = jnp.float32

length_scale = 1.5


def dot(left, right):
    return jnp.dot(left, right, preferred_element_type=F32)


def lanes(parts):
    return jnp.concatenate(parts, axis=-1)


def block_slot(e, f, wr, wc):
    return 6 * wr + wc - 3 * min(max(wr - 1 - e, 0), 3) - (
        min(max(wc - 1 - f, 0), 3) if e + 1 <= wr <= e + 3 else 0
    )


def is_near(e, f, wr, wc):
    return e + 1 <= wr <= e + 3 and f + 1 <= wc <= f + 3


def places():
    row = lax.axis_index("gx")
    col = lax.axis_index("gy")
    return row, col, col // 2, col % 2


def prepare_kernel(ids, coupling, w0, w1, w2, w3, w4, w5, table):
    row, col, _, _ = places()

    def pair(level, e, wr, wc):
        halves = []
        for f in (0, 1):
            if is_near(e, f, wr, wc):
                halves.append(jnp.zeros((RANK, RANK), BF))
            else:
                halves.append(coupling[level, ids[level, 2 * e + f, block_slot(e, f, wr, wc)]])
        return lanes(halves)

    for wr in range(6):
        for wc in range(6):
            at = pl.ds((6 * wr + wc) * RANK, RANK)
            for e in (0, 1):
                w0[at, pl.ds(128 * e, 128)] = pair(0, e, wr, wc)

    for level, out, bit in ((1, w1, row % 2), (2, w2, (row // 2) % 2)):
        for e in (0, 1):

            @pl.when(bit == e)
            def _(level=level, out=out, e=e):
                for wr in range(6):
                    for wc in range(6):
                        out[pl.ds((6 * wr + wc) * RANK, RANK), :] = pair(level, e, wr, wc)

    def single(level, e, f, wr, wc):
        row_in = jnp.logical_and(wr >= e + 1, wr <= e + 3)
        col_in = jnp.logical_and(wc >= f + 1, wc <= f + 3)
        skipped = 3 * jnp.clip(wr - 1 - e, 0, 3) + jnp.where(row_in, jnp.clip(wc - 1 - f, 0, 3), 0)
        slot = jnp.clip(6 * wr + wc - skipped, 0, 26)
        keep = jnp.where(jnp.logical_and(row_in, col_in), 0.0, 1.0)
        block = coupling[level, ids[level, 2 * e + f, slot]]
        return block * jnp.full((RANK, RANK), keep, F32).astype(BF)

    e3, f3 = (row // 4) % 2, col % 2
    first3 = 2 - 2 * (row // 8)
    for r in range(4):
        for wc in range(6):
            w3[pl.ds((6 * r + wc) * RANK, RANK), :] = single(3, e3, f3, r + first3, wc)
    e4, f4 = row // 8, (col // 2) % 2
    for wc in range(6):
        for r in range(2):
            w4[pl.ds((2 * wc + r) * RANK, RANK), :] = single(4, e4, f4, jnp.int32(2 + r), wc)
    for level in (5, 6, 7):
        f = (col // (1 << (level - 3))) % 2
        for wc in range(6):
            w5[level - 5, pl.ds(wc * RANK, RANK), :] = single(
                level, jnp.int32(0), f, jnp.int32(2), wc
            )

    size = LEAF_ROWS * LEAF_COLS
    theirs = lax.broadcasted_iota(jnp.int32, (size, size), 0)
    ours = lax.broadcasted_iota(jnp.int32, (size, size), 1)
    rows_apart = (theirs // LEAF_COLS - ours // LEAF_COLS).astype(F32)
    cols_apart = (theirs % LEAF_COLS - ours % LEAF_COLS).astype(F32)
    for u in (-1, 0, 1):
        for v in (-1, 0, 1):
            apart_row = rows_apart + float(u * LEAF_ROWS)
            apart_col = cols_apart + float(v * LEAF_COLS)
            scaled = jnp.sqrt(3.0 * (apart_row * apart_row + apart_col * apart_col)) / length_scale
            value = (1.0 + scaled) * jnp.exp(-scaled)
            table[pl.ds((3 * (u + 1) + v + 1) * size, size), :] = value.astype(BF)


def vmem(shape, kind=BF):
    return jax.ShapeDtypeStruct(shape, kind)


def call(kernel, out_shape, scratch=(), flops=1 << 24, read=1 << 21, **specs):
    return pl.pallas_call(
        kernel,
        out_shape=out_shape,
        **specs,
        scratch_shapes=list(scratch),
        compiler_params=pltpu.CompilerParams(vmem_limit_bytes=48 << 20),
        cost_estimate=pl.CostEstimate(flops=flops, bytes_accessed=read, transcendentals=0),
    )


def pair_basis(basis):
    zero = jnp.zeros_like(basis)
    return jnp.concatenate([lanes([basis, zero]), lanes([zero, basis])], axis=0)


def leaf_coeffs(tile, wide_basis):
    rows = tile.shape[0]
    split = tile.reshape(rows, 4, 2, PROBES, 128)
    joined = lanes([split[:, :, 0], split[:, :, 1]]).reshape(-1, 256)
    return dot(joined, wide_basis).astype(BF).reshape(rows, 4, PROBES, 128)


def to_pairs(nodes):
    lead = nodes.shape[:-3]
    split = nodes.reshape(lead + (nodes.shape[-3] // 2, 2, PROBES, RANK))
    return lanes([split[..., 0, :, :], split[..., 1, :, :]])


def raise_pairs(pairs, transfer):
    rows, count = pairs.shape[:2]
    split = pairs.reshape(rows // 2, 2, count, PROBES, 128)
    joined = lanes([split[:, 0], split[:, 1]]).reshape(-1, 256)
    return dot(joined, transfer).astype(BF).reshape(rows // 2, count, PROBES, RANK)


def first_kernel(own, other, basis, up, sent, mine, others):
    _, _, _, core = places()
    wide = pair_basis(basis[...])
    transfer = up[0].reshape(4 * RANK, RANK)
    for which, tile, kept in ((core, own, mine), (1 - core, other, others)):
        coeffs = leaf_coeffs(tile[...], wide)
        kept[...] = coeffs
        pairs = to_pairs(raise_pairs(coeffs, transfer)[0])
        for peer in range(16):
            sent[peer, pl.ds(2 * which, 2)] = pairs


def second_kernel(
    gathered, own, mine, above, below, basis, up,
    far_out, side_out, third_out, mate_out, rim, level2, level3,
    padded1, padded2,
):
    row, _, _, core = places()
    wide = pair_basis(basis[...])
    pairs2 = to_pairs(raise_pairs(gathered[...], up[1].reshape(4 * RANK, RANK)))
    pairs3 = to_pairs(raise_pairs(pairs2, up[2].reshape(4 * RANK, RANK)))[:, 0]
    nodes4 = raise_pairs(pairs3[:, None], up[3].reshape(4 * RANK, RANK))
    far_out[...] = lanes([nodes4[0, 0], nodes4[1, 0]])
    level2[...] = pairs2
    level3[...] = pairs3
    third_out[...] = pairs3
    rim[pl.ds(0, 2)] = leaf_coeffs(above[...], wide)
    rim[pl.ds(2, 2)] = leaf_coeffs(below[...], wide)

    edge_pair = 3 * core
    edge_col = 7 * core
    nothing = jnp.zeros((2, PROBES, 128), BF)
    padded1[pl.ds(0, 2)] = nothing
    padded1[pl.ds(18, 2)] = nothing
    padded2[pl.ds(0, 2)] = nothing
    padded2[pl.ds(10, 2)] = nothing
    for r in range(16):
        padded1[r + 2] = gathered[r, edge_pair]
    for r in range(8):
        padded2[r + 2] = level2[r, core]
    side_out[0] = above[1, edge_col]
    side_out[1] = own[0, edge_col]
    side_out[2] = own[1, edge_col]
    side_out[3] = below[0, edge_col]
    side_out[4] = rim[0, edge_pair]
    side_out[5] = rim[1, edge_pair]
    side_out[6] = mine[0, edge_pair]
    side_out[7] = mine[1, edge_pair]
    side_out[8] = rim[2, edge_pair]
    side_out[9] = rim[3, edge_pair]
    side_out[pl.ds(10, 6)] = padded1[pl.ds(2 * (row // 2), 6)]
    side_out[pl.ds(16, 6)] = padded2[pl.ds(2 * (row // 4), 6)]
    side_out[pl.ds(22, 4)] = pairs3
    mate_out[0] = above[1, 7 - edge_col]
    mate_out[1] = below[0, 7 - edge_col]
    for r in range(4):
        mate_out[2 + r] = rim[r, 3 - edge_pair]


def third_kernel(
    own, other, above, below, mine, others, rim, gathered, level2, level3,
    side, third, mate, top, w0, w1, w2, w3, w4, w5, table, basis, up, down,
    out,
    near, window0, padded1, window1, padded2, window2, window3, padded4, padded5, padded6, padded7,
):
    row, col, chip, core = places()
    wide = pair_basis(basis[...])

    blank = jnp.zeros((2, PROBES, 128), BF)
    padded4[pl.ds(0, 2)] = blank
    padded4[pl.ds(18, 2)] = blank
    for c in range(16):
        padded4[c + 2] = top[(chip - c + 16) % 16]
    by_col = jnp.concatenate([up[4, 0], up[4, 2], up[4, 1], up[4, 3]], axis=0)
    all4 = padded4[pl.ds(2, 16)].reshape(8, 2, PROBES, 128)
    nodes5 = dot(lanes([all4[:, 0], all4[:, 1]]).reshape(-1, 256), by_col)
    nodes5 = nodes5.astype(BF).reshape(8, PROBES, RANK)

    def raise_row(nodes, level):
        pairs = to_pairs(nodes).reshape(-1, 128)
        both = jnp.concatenate([up[level, 0], up[level, 1]], axis=0)
        return dot(pairs, both).astype(BF).reshape(-1, PROBES, RANK)

    nodes6 = raise_row(nodes5, 5)
    nodes7 = raise_row(nodes6, 6)
    gap = jnp.zeros((2, PROBES, RANK), BF)
    for padded, nodes in ((padded5, nodes5), (padded6, nodes6), (padded7, nodes7)):
        count = nodes.shape[0]
        padded[pl.ds(0, 2)] = gap
        padded[pl.ds(2, count)] = nodes
        padded[pl.ds(2 + count, 2)] = gap

    def far_row(padded, level):
        start = 2 * (col // (1 << (level - 2)))
        return dot(lanes([padded[start + k] for k in range(6)]), w5[level - 5])

    def lowered(local, level):
        e = (row // (1 << (level - 1))) % 2
        f = (col // (1 << (level - 3))) % 2
        return dot(local, down[level, 2 * e + f])

    local = far_row(padded7, 7).astype(BF)
    local = (far_row(padded6, 6) + lowered(local, 6)).astype(BF)
    local = (far_row(padded5, 5) + lowered(local, 5)).astype(BF)
    start4 = 2 * (chip // 2)
    far4 = dot(lanes([padded4[start4 + k] for k in range(6)]), w4[...])
    local = (far4 + lowered(local, 4)).astype(BF)

    for r in range(4):
        window3[r, 2 * core] = side[22 + r]
        window3[r, 1] = level3[r]
        window3[r, 2 - 2 * core] = third[r]
    far3 = dot(lanes([window3[r, k] for r in range(4) for k in range(3)]), w3[...])
    local3 = (far3 + lowered(local, 3)).astype(BF)

    empty2 = jnp.zeros((2, 2, PROBES, 128), BF)
    padded2[pl.ds(0, 2)] = empty2
    padded2[pl.ds(2, 8)] = level2[...]
    padded2[pl.ds(10, 2)] = empty2
    for w in range(6):
        for k in range(2):
            window2[w, k + 1 - core] = padded2[2 * (row // 4) + w, k]
        window2[w, 2 * core] = side[16 + w]
    far2 = dot(lanes([window2[w, k] for w in range(6) for k in range(3)]), w2[...])
    e2 = (row // 2) % 2
    local2 = (far2 + dot(local3, lanes([down[2, 2 * e2], down[2, 2 * e2 + 1]]))).astype(BF)

    empty1 = jnp.zeros((2, 4, PROBES, 128), BF)
    padded1[pl.ds(0, 2)] = empty1
    padded1[pl.ds(2, 16)] = gathered[...]
    padded1[pl.ds(18, 2)] = empty1
    for w in range(6):
        for k in range(3):
            window1[w, k + 1 - core] = padded1[2 * (row // 2) + w, k + core]
        window1[w, 3 * core] = side[10 + w]
    far1 = dot(
        lanes([window1[w, pl.ds(k, 2)].reshape(-1, 128) for w in range(6) for k in range(3)]),
        w1[...],
    )
    e1 = row % 2
    down1 = lanes([down[1, 2 * e1], down[1, 2 * e1 + 1]])
    none1 = jnp.zeros_like(down1)
    down1 = jnp.concatenate([lanes([down1, none1]), lanes([none1, down1])], axis=0)
    spread1 = dot(local2, down1)
    spread1 = jnp.concatenate([spread1[:, :128], spread1[:, 128:]], axis=0)
    local1 = (far1 + spread1).astype(BF)

    window0[pl.ds(0, 2), pl.ds(1, 4)] = rim[pl.ds(0, 2)]
    window0[pl.ds(2, 2), pl.ds(1, 4)] = mine[...]
    window0[pl.ds(4, 2), pl.ds(1, 4)] = rim[pl.ds(2, 2)]
    for w in range(6):
        window0[w, 5 * core] = side[4 + w]
    for r in range(2):
        window0[r, 5 - 5 * core] = mate[2 + r]
        window0[2 + r, 5 - 5 * core] = others[r, 3 * core]
        window0[4 + r, 5 - 5 * core] = mate[4 + r]
    far0 = dot(
        lanes([window0[w, pl.ds(k, 4)].reshape(-1, 128) for w in range(6) for k in range(3)]),
        w0[...],
    )
    down0 = lanes([down[0, k] for k in range(4)])
    none0 = jnp.zeros_like(down0)
    down0 = jnp.concatenate([lanes([down0, none0]), lanes([none0, down0])], axis=0)
    spread0 = dot(local1, down0).reshape(2, PROBES, 512)
    spread0 = jnp.stack([spread0[:, :, :256], spread0[:, :, 256:]], axis=1).reshape(-1, 256)
    local0 = (far0 + spread0).astype(BF)

    near[0, pl.ds(1, 8)] = above[1]
    near[1, pl.ds(1, 8)] = own[0]
    near[2, pl.ds(1, 8)] = own[1]
    near[3, pl.ds(1, 8)] = below[0]
    for r in range(4):
        near[r, 9 * core] = side[r]
    near[0, 9 - 9 * core] = mate[0]
    near[1, 9 - 9 * core] = other[0, 7 * core]
    near[2, 9 - 9 * core] = other[1, 7 * core]
    near[3, 9 - 9 * core] = mate[1]
    for e in (0, 1):
        joined = lanes([near[e + u, pl.ds(v, 8)].reshape(-1, 128) for u in range(3) for v in range(3)])
        near_sum = dot(joined, table[...]).reshape(8, PROBES, 128)
        far_sum = lax.dot_general(
            local0[:, 128 * e : 128 * e + 128], wide, (((1,), (1,)), ((), ())),
            preferred_element_type=F32,
        ).reshape(4, PROBES, 256)
        for q in range(4):
            for f in (0, 1):
                part = far_sum[q, :, 128 * f : 128 * f + 128]
                out[e, 2 * q + f] = (near_sum[2 * q + f] + part).astype(BF)


def route(rule, size_x, size_y):
    pairs = []
    for a in range(size_x):
        for b in range(size_y):
            x, y = rule(a, b)
            if 0 <= x < size_x and 0 <= y < size_y:
                pairs.append((a * size_y + b, x * size_y + y))
    return pairs


def across(core):
    return 1 if core else -1


def shards(probes, leaf_basis, up_transfer, down_transfer, coupling, far_ids):
    size_x, size_y = lax.axis_size("gx"), lax.axis_size("gy")
    both = ("gx", "gy")

    def move(value, rule):
        return lax.ppermute(value, both, route(rule, size_x, size_y))

    other = move(probes, lambda a, b: (a, b ^ 1))
    above = move(probes, lambda a, b: (a + 1, b))
    below = move(probes, lambda a, b: (a - 1, b))

    smem = pl.BlockSpec(memory_space=pltpu.SMEM)
    whole = pl.BlockSpec(memory_space=pltpu.VMEM)
    w0, w1, w2, w3, w4, w5, table = call(
        prepare_kernel,
        [
            vmem((36 * RANK, 256)), vmem((36 * RANK, 128)), vmem((36 * RANK, 128)),
            vmem((24 * RANK, RANK)), vmem((12 * RANK, RANK)), vmem((3, 6 * RANK, RANK)),
            vmem((9 * 128, 128)),
        ],
        in_specs=[smem, whole],
    )(far_ids, coupling)

    sent, mine, others = call(
        first_kernel,
        [vmem((16, 4, PROBES, 128)), vmem((2, 4, PROBES, 128)), vmem((2, 4, PROBES, 128))],
    )(probes, other, leaf_basis, up_transfer)
    gathered = lax.all_to_all(sent, "gx", 0, 0)

    far_out, side_out, third_out, mate_out, rim, level2, level3 = call(
        second_kernel,
        [
            vmem((PROBES, 128)), vmem((26, PROBES, 128)), vmem((4, PROBES, 128)),
            vmem((6, PROBES, 128)), vmem((4, 4, PROBES, 128)), vmem((8, 2, PROBES, 128)),
            vmem((4, PROBES, 128)),
        ],
        scratch=[pltpu.VMEM((20, PROBES, 128), BF), pltpu.VMEM((12, PROBES, 128), BF)],
    )(gathered, probes, mine, above, below, leaf_basis, up_transfer)

    chips = size_y // 2
    top = move(far_out, lambda a, b: (a, 2 * ((b // 2 + a) % chips) + b % 2))
    side = move(side_out, lambda a, b: (a, b + across(b % 2)))
    third = move(third_out, lambda a, b: (a, b + 3 - 6 * (b % 2)))
    mate = move(mate_out, lambda a, b: (a, b ^ 1))
    top = lax.all_to_all(jnp.broadcast_to(top, (size_x,) + top.shape), "gx", 0, 0)

    block = (PROBES, 128)
    scratch = [
        pltpu.VMEM(lead + block, BF)
        for lead in ((4, 10), (6, 6), (20, 4), (6, 4), (12, 2), (6, 3), (4, 3), (20,))
    ] + [pltpu.VMEM((count + 4, PROBES, RANK), BF) for count in (8, 4, 2)]
    return call(third_kernel, vmem(probes.shape), scratch=scratch)(
        probes, other, above, below, mine, others, rim, gathered, level2, level3,
        side, third, mate, top, w0, w1, w2, w3, w4, w5, table,
        leaf_basis, up_transfer, down_transfer,
    )


def solution(mesh):
    in_specs = (P("gx", "gy", None, None), P(), P(), P(), P(), P())
    out_specs = P("gx", "gy", None, None)
    return jax.shard_map(shards, mesh=mesh, in_specs=in_specs, out_specs=out_specs, check_vma=False)
```

time: 691 us -> 85.2 us (0.12)
  the two profiles are of different devices: /device:TPU:1 before, /device:TPU:2 now
where the time goes in v1:
time: 85.2 us; the launch traced here: 84.1 us
  starting transfers between devices  38 us (45%)
  local copies, waits for them, and re-layouts  18.9 us (22%)
  waiting for transfers between devices  15.5 us (18%)
  Pallas kernels  11.6 us (14%)
    unnamed x51, local copies, waits for them, and re-layouts  18.2 us
    ppermute x7, starting transfers between devices, move(): return lax.ppermute(value, both, route(rule, size_x, size_y))  17.3 us
    ppermute x7, waiting for transfers between devices, move(): return lax.ppermute(value, both, route(rule, size_x, size_y))  14.7 us
    all_to_all x1, starting transfers between devices, shards(): lax.all_to_all(jnp.broadcast_to(top, (size_x,) + top.shape), 'gx', 0, 0)  11.5 us
    all_to_all x1, starting transfers between devices, shards(): gathered = lax.all_to_all(sent, 'gx', 0, 0)  9.27 us
    pallas_call x1, Pallas kernels, shards(): call(third_kernel, vmem(probes.shape), scratch=scratch)  4.6 us
    pallas_call x1, Pallas kernels, shards(): call(prepare_kernel, [vmem((36 * RANK, 256)), vmem((36 * RANK, 128)), vme...  3.89 us
  transfers between devices with their start and end apart: 9, of which 4 were waited for; matrix products, arithmetic and copies ran while one was open for 2% of the time, Pallas kernels for 5%

profile of v1, /device:TPU:2, one launch (start us, length us, event | category | flops | bytes accessed | tf_op | source)
XLA Modules:
  0.0 84.1 jit_solution(7747007332720492469)
XLA Ops:
  0.0 1.9 %collective-permute-start = (bf16[2,8,32,128]{3,2,1,0:T(8,128)(2,1)}, bf16[2,8,32,128]{3,2,1,0:T(8,128)(2,1)S(1)}, u32[]{:S(2)}, u32[]{:S(2)}) collective-permute-start(bf16[2,8,32,128]{3,2,1,0:T(8,128)(2,1)} %own.5), channel_id=1, source_target_pairs={{0,1},{1,0},{2,3},{3,2},{4,5},{5,4},{6,7},{7,6},{8,9},{9,8},{10,11... | collective-permute-start | bytes 393224 | tf_op jit(solution)/shard_map/ppermute | solution.py:357
  1.9 0.8 copy.7.basis
  2.7 0.7 collective-permute-done.other
  3.4 1.0 %copy-done = bf16[7,4,64,64]{3,2,1,0:T(8,128)(2,1)S(1)} copy-done((bf16[7,4,64,64]{3,2,1,0:T(8,128)(2,1)S(1)}, bf16[7,4,64,64]{3,2,1,0:T(8,128)(2,1)}, u32[]{:S(2)}) %copy-start) | copy-done | bytes 229400
  4.5 0.9 %copy-done.4 = bf16[2,8,32,128]{3,2,1,0:T(8,128)(2,1)S(1)} copy-done((bf16[2,8,32,128]{3,2,1,0:T(8,128)(2,1)S(1)}, bf16[2,8,32,128]{3,2,1,0:T(8,128)(2,1)}, u32[]{:S(2)}) %copy-start.4) | copy-done | bytes 131096
  5.4 1.5 %shard_map.64 = (bf16[16,4,32,128]{3,2,1,0:T(8,128)(2,1)}, bf16[2,4,32,128]{3,2,1,0:T(8,128)(2,1)S(1)}, bf16[2,4,32,128]{3,2,1,0:T(8,128)(2,1)S(1)}) custom-call(bf16[2,8,32,128]{3,2,1,0:T(8,128)(2,1)S(1)} %copy-done.4, bf16[2,8,32,128]{3,2,1,0:T(8,128)(2,1)S(1)} %collective-permute-done.other, bf16[128,64]{1,0:T(8,128)(2,1)S(1)} %copy.7.basis, ...), custom_call_target="tpu_custom_call" | custom-call | flops 16777216 | bytes 2097152 | tf_op jit(solution)/shard_map/pallas_call | solution.py:375
  6.8 0.6 copy-done.18
  7.5 9.3 %all-to-all-start = ((bf16[16,4,32,128]{3,2,1,0:T(8,128)(2,1)}), bf16[16,4,32,128]{3,2,1,0:T(8,128)(2,1)S(1)}, u32[]{:S(2)}, u32[]{:S(2)}) async-start(bf16[16,4,32,128]{3,2,1,0:T(8,128)(2,1)} %get-tuple-element.24), calls=%async_computation | async-start | bytes 1048576 | tf_op jit(solution)/shard_map/all_to_all | solution.py:379
  16.7 2.1 %collective-permute-start.2 = (bf16[2,8,32,128]{3,2,1,0:T(8,128)(2,1)}, bf16[2,8,32,128]{3,2,1,0:T(8,128)(2,1)S(1)}, u32[]{:S(2)}, u32[]{:S(2)}) collective-permute-start(bf16[2,8,32,128]{3,2,1,0:T(8,128)(2,1)} %own.5), channel_id=1, source_target_pairs={{32,0},{33,1},{34,2},{35,3},{36,4},{37,5},{38,6},{39,7},{40,8},{41... | collective-permute-start | bytes 393224 | tf_op jit(solution)/shard_map/ppermute | solution.py:357
  18.9 3.7 %collective-permute-start.1 = (bf16[2,8,32,128]{3,2,1,0:T(8,128)(2,1)}, bf16[2,8,32,128]{3,2,1,0:T(8,128)(2,1)S(1)}, u32[]{:S(2)}, u32[]{:S(2)}) collective-permute-start(bf16[2,8,32,128]{3,2,1,0:T(8,128)(2,1)} %own.5), channel_id=1, source_target_pairs={{0,32},{1,33},{2,34},{3,35},{4,36},{5,37},{6,38},{7,39},{8,40},{9,... | collective-permute-start | bytes 393224 | tf_op jit(solution)/shard_map/ppermute | solution.py:357
  22.6 5.0 %collective-permute-done.2.below = bf16[2,8,32,128]{3,2,1,0:T(8,128)(2,1)S(1)} collective-permute-done((bf16[2,8,32,128]{3,2,1,0:T(8,128)(2,1)}, bf16[2,8,32,128]{3,2,1,0:T(8,128)(2,1)S(1)}, u32[]{:S(2)}, u32[]{:S(2)}) %collective-permute-start.2) | collective-permute-done | bytes 131104 | tf_op jit(solution)/shard_map/ppermute | solution.py:357
  27.6 0.0 collective-permute-done.1.above
  27.6 0.8 all-to-all-done.gathered
  28.4 1.0 %copy-done.1 = bf16[7,4,64,64]{3,2,1,0:T(8,128)(2,1)S(1)} copy-done((bf16[7,4,64,64]{3,2,1,0:T(8,128)(2,1)S(1)}, bf16[7,4,64,64]{3,2,1,0:T(8,128)(2,1)}, u32[]{:S(2)}) %copy-start.1) | copy-done | bytes 229400
  29.4 0.9 %copy-done.5 = bf16[2,8,32,128]{3,2,1,0:T(8,128)(2,1)S(1)} copy-done((bf16[2,8,32,128]{3,2,1,0:T(8,128)(2,1)S(1)}, bf16[2,8,32,128]{3,2,1,0:T(8,128)(2,1)}, u32[]{:S(2)}) %copy-start.5) | copy-done | bytes 131096
  30.3 1.6 %shard_map.65 = (bf16[32,128]{1,0:T(8,128)(2,1)S(1)}, bf16[26,32,128]{2,1,0:T(8,128)(2,1)}, bf16[4,32,128]{2,1,0:T(8,128)(2,1)}, bf16[6,32,128]{2,1,0:T(8,128)(2...) custom-call(bf16[16,4,32,128]{3,2,1,0:T(8,128)(2,1)S(1)} %all-to-all-, ...), custom_call_target="tpu_custom_call" | custom-call | flops 16777216 | bytes 2097152 | tf_op jit(solution)/shard_map/pallas_call | solution.py:381
  31.9 0.6 copy-done.20
  32.5 1.3 %collective-permute-start.3 = (bf16[26,32,128]{2,1,0:T(8,128)(2,1)}, bf16[26,32,128]{2,1,0:T(8,128)(2,1)}, u32[]{:S(2)}, u32[]{:S(2)}) collective-permute-start(bf16[26,32,128]{2,1,0:T(8,128)(2,1)} %get-tuple-element.28), channel_id=1, source_target_pairs={{1,2},{2,1},{3,4},{4,3},{5,6},{6,5},{7,8},{8,7},{9,10},{10,9},{11,... | collective-permute-start | bytes 638984 | tf_op jit(solution)/shard_map/ppermute | solution.py:357
  33.9 2.7 %collective-permute-start.6 = (bf16[32,128]{1,0:T(8,128)(2,1)S(1)}, bf16[32,128]{1,0:T(8,128)(2,1)S(1)}, u32[]{:S(2)}, u32[]{:S(2)}) collective-permute-start(bf16[32,128]{1,0:T(8,128)(2,1)S(1)} %get-tuple-element.31), channel_id=1, source_target_pairs={{0,0},{1,1},{2,2},{3,3},{4,4},{5,5},{6,6},{7,7},{8,8},{9,9},{10,10... | collective-permute-start | bytes 24584 | tf_op jit(solution)/shard_map/ppermute | solution.py:357
  36.6 9.0 %collective-permute-done.6 = bf16[32,128]{1,0:T(8,128)(2,1)S(1)} collective-permute-done((bf16[32,128]{1,0:T(8,128)(2,1)S(1)}, bf16[32,128]{1,0:T(8,128)(2,1)S(1)}, u32[]{:S(2)}, u32[]{:S(2)}) %collective-permute-start.6) | collective-permute-done | bytes 8224 | tf_op jit(solution)/shard_map/ppermute | solution.py:357
  45.6 0.7 broadcast_in_dim.3
  46.3 11.5 %all-to-all-start.1 = ((bf16[16,32,128]{2,1,0:T(8,128)(2,1)}), bf16[16,32,128]{2,1,0:T(8,128)(2,1)S(1)}, u32[]{:S(2)}, u32[]{:S(2)}) async-start(bf16[16,32,128]{2,1,0:T(8,128)(2,1)} %broadcast_in_dim.3), calls=%async_computation.1 | async-start | bytes 262144 | tf_op jit(solution)/shard_map/all_to_all | solution.py:396
  57.8 2.1 %collective-permute-start.5 = (bf16[6,32,128]{2,1,0:T(8,128)(2,1)}, bf16[6,32,128]{2,1,0:T(8,128)(2,1)S(1)}, u32[]{:S(2)}, u32[]{:S(2)}) collective-permute-start(bf16[6,32,128]{2,1,0:T(8,128)(2,1)} %get-tuple-element.30), channel_id=1, source_target_pairs={{0,1},{1,0},{2,3},{3,2},{4,5},{5,4},{6,7},{7,6},{8,9},{9,8},{10,11... | collective-permute-start | bytes 147464 | tf_op jit(solution)/shard_map/ppermute | solution.py:357
  59.9 3.3 %collective-permute-start.4 = (bf16[4,32,128]{2,1,0:T(8,128)(2,1)}, bf16[4,32,128]{2,1,0:T(8,128)(2,1)S(1)}, u32[]{:S(2)}, u32[]{:S(2)}) collective-permute-start(bf16[4,32,128]{2,1,0:T(8,128)(2,1)} %get-tuple-element.29), channel_id=1, source_target_pairs={{0,3},{2,5},{3,0},{4,7},{5,2},{6,9},{7,4},{8,11},{9,6},{10,13},{11... | collective-permute-start | bytes 98312 | tf_op jit(solution)/shard_map/ppermute | solution.py:357
  63.2 0.0 copy-start.24
  63.2 0.7 copy-done.24
  64.0 3.9 %shard_map.66 = (bf16[2304,256]{1,0:T(8,128)(2,1)S(1)}, bf16[2304,128]{1,0:T(8,128)(2,1)S(1)}, bf16[2304,128]{1,0:T(8,128)(2,1)S(1)}, bf16[1536,64]{1,0:T(8,128)...) custom-call(s32[8,4,27]{2,1,0:T(4,128)S(1)} %copy-done.24, ...), custom_call_target="tpu_custom_call" | custom-call | flops 16777216 | bytes 2097152 | tf_op jit(solution)/shard_map/pallas_call | solution.py:365
  67.9 1.0 %copy-done.3 = bf16[2304,256]{1,0:T(8,128)(2,1)} copy-done((bf16[2304,256]{1,0:T(8,128)(2,1)}, bf16[2304,256]{1,0:T(8,128)(2,1)S(1)}, u32[]{:S(2)}) %copy-start.3) | copy-done | bytes 1179672
  68.9 0.7 copy-done.8
  69.7 0.7 copy-done.10
  70.4 0.7 copy-done.12
  71.1 0.7 copy-done.14
  71.8 0.0 collective-permute-done.4.third
  71.8 0.6 copy-done.22
  72.4 0.0 collective-permute-done.5.mate
  72.4 0.0 all-to-all-done.1.top
  72.4 0.0 collective-permute-done.3.side
  72.4 0.0 copy-done.2
  72.4 0.0 copy-done.6
  72.4 1.0 %copy-done.9 = bf16[1536,64]{1,0:T(8,128)(2,1)S(1)} copy-done((bf16[1536,64]{1,0:T(8,128)(2,1)S(1)}, bf16[1536,64]{1,0:T(8,128)(2,1)}, u32[]{:S(2)}) %copy-start.9) | copy-done | bytes 196632
  73.4 1.0 %copy-done.11 = bf16[3,384,64]{2,1,0:T(8,128)(2,1)S(1)} copy-done((bf16[3,384,64]{2,1,0:T(8,128)(2,1)S(1)}, bf16[3,384,64]{2,1,0:T(8,128)(2,1)}, u32[]{:S(2)}) %copy-start.11) | copy-done | bytes 147480
  74.4 1.0 %copy-done.13 = bf16[1152,128]{1,0:T(8,128)(2,1)S(1)} copy-done((bf16[1152,128]{1,0:T(8,128)(2,1)S(1)}, bf16[1152,128]{1,0:T(8,128)(2,1)}, u32[]{:S(2)}) %copy-start.13) | copy-done | bytes 294936
  75.3 0.9 %copy-done.15 = bf16[768,64]{1,0:T(8,128)(2,1)S(1)} copy-done((bf16[768,64]{1,0:T(8,128)(2,1)S(1)}, bf16[768,64]{1,0:T(8,128)(2,1)}, u32[]{:S(2)}) %copy-start.15) | copy-done | bytes 98328
  76.3 0.9 %copy-done.17 = bf16[8,2,32,128]{3,2,1,0:T(8,128)(2,1)S(1)} copy-done((bf16[8,2,32,128]{3,2,1,0:T(8,128)(2,1)S(1)}, bf16[8,2,32,128]{3,2,1,0:T(8,128)(2,1)}, u32[]{:S(2)}) %copy-start.17) | copy-done | bytes 131096
  77.2 0.8 copy-done.19
  78.0 0.8 copy-done.21
  78.8 0.8 copy-done.23
  79.5 4.6 %shard_map.67 = bf16[2,8,32,128]{3,2,1,0:T(8,128)(2,1)} custom-call(bf16[2,8,32,128]{3,2,1,0:T(8,128)(2,1)S(1)} %copy-done.6, bf16[2,8,32,128]{3,2,1,0:T(8,128)(2,1)S(1)} %collective-permute-done.other, bf16[2,8,32,128]{3,2,1,0:T(8,128)(2,1)S(1)} %collective-permute-done.1.above, bf16[2,8,32,128]{3,2,1,0:T(8,128)(2,1)S(1)} %collective-permute-done.2.below, ...), custom_call_target="tpu_custom_call" | custom-call | flops 16777216 | bytes 2097152 | tf_op jit(solution)/shard_map/pallas_call | solution.py:403
  (26 shorter events, 0.0 us)
Async XLA Ops:
  0.0 3.4 %collective-permute-start = (bf16[2,8,32,128]{3,2,1,0:T(8,128)(2,1)}, bf16[2,8,32,128]{3,2,1,0:T(8,128)(2,1)S(1)}, u32[]{:S(2)}, u32[]{:S(2)}) collective-permute-start(bf16[2,8,32,128]{3,2,1,0:T(8,128)(2,1)} %own.5), channel_id=1, source_target_pairs={{0,1},{1,0},{2,3},{3,2},{4,5},{5,4},{6,7},{7,6},{8,9},{9,8},{10,11... | collective-permute-start | bytes 393224 | tf_op jit(solution)/shard_map/ppermute | solution.py:357
  3.4 1.0 %copy-start = (bf16[7,4,64,64]{3,2,1,0:T(8,128)(2,1)S(1)}, bf16[7,4,64,64]{3,2,1,0:T(8,128)(2,1)}, u32[]{:S(2)}) copy-start(bf16[7,4,64,64]{3,2,1,0:T(8,128)(2,1)} %up.5) | copy-start | bytes 688132
  4.5 0.9 %copy-start.4 = (bf16[2,8,32,128]{3,2,1,0:T(8,128)(2,1)S(1)}, bf16[2,8,32,128]{3,2,1,0:T(8,128)(2,1)}, u32[]{:S(2)}) copy-start(bf16[2,8,32,128]{3,2,1,0:T(8,128)(2,1)} %own.5) | copy-start | bytes 393220
  5.4 67.0 %copy-start.2 = (bf16[7,4,64,64]{3,2,1,0:T(8,128)(2,1)S(1)}, bf16[7,4,64,64]{3,2,1,0:T(8,128)(2,1)}, u32[]{:S(2)}) copy-start(bf16[7,4,64,64]{3,2,1,0:T(8,128)(2,1)} %up.5) | copy-start | bytes 688132
  5.4 67.0 %copy-start.6 = (bf16[2,8,32,128]{3,2,1,0:T(8,128)(2,1)S(1)}, bf16[2,8,32,128]{3,2,1,0:T(8,128)(2,1)}, u32[]{:S(2)}) copy-start(bf16[2,8,32,128]{3,2,1,0:T(8,128)(2,1)} %own.5) | copy-start | bytes 393220
  5.4 67.0 %copy-start.7 = (bf16[7,4,64,64]{3,2,1,0:T(8,128)(2,1)S(1)}, bf16[7,4,64,64]{3,2,1,0:T(8,128)(2,1)}, u32[]{:S(2)}) copy-start(bf16[7,4,64,64]{3,2,1,0:T(8,128)(2,1)} %down.1) | copy-start | bytes 688132
  6.8 0.6 copy-start.18
  7.5 20.9 %all-to-all-start = ((bf16[16,4,32,128]{3,2,1,0:T(8,128)(2,1)}), bf16[16,4,32,128]{3,2,1,0:T(8,128)(2,1)S(1)}, u32[]{:S(2)}, u32[]{:S(2)}) async-start(bf16[16,4,32,128]{3,2,1,0:T(8,128)(2,1)} %get-tuple-element.24), calls=%async_computation | async-start | bytes 1048576 | tf_op jit(solution)/shard_map/all_to_all | solution.py:379
  16.7 10.8 %collective-permute-start.2 = (bf16[2,8,32,128]{3,2,1,0:T(8,128)(2,1)}, bf16[2,8,32,128]{3,2,1,0:T(8,128)(2,1)S(1)}, u32[]{:S(2)}, u32[]{:S(2)}) collective-permute-start(bf16[2,8,32,128]{3,2,1,0:T(8,128)(2,1)} %own.5), channel_id=1, source_target_pairs={{32,0},{33,1},{34,2},{35,3},{36,4},{37,5},{38,6},{39,7},{40,8},{41... | collective-permute-start | bytes 393224 | tf_op jit(solution)/shard_map/ppermute | solution.py:357
  18.9 8.7 %collective-permute-start.1 = (bf16[2,8,32,128]{3,2,1,0:T(8,128)(2,1)}, bf16[2,8,32,128]{3,2,1,0:T(8,128)(2,1)S(1)}, u32[]{:S(2)}, u32[]{:S(2)}) collective-permute-start(bf16[2,8,32,128]{3,2,1,0:T(8,128)(2,1)} %own.5), channel_id=1, source_target_pairs={{0,32},{1,33},{2,34},{3,35},{4,36},{5,37},{6,38},{7,39},{8,40},{9,... | collective-permute-start | bytes 393224 | tf_op jit(solution)/shard_map/ppermute | solution.py:357
  28.4 1.0 %copy-start.1 = (bf16[7,4,64,64]{3,2,1,0:T(8,128)(2,1)S(1)}, bf16[7,4,64,64]{3,2,1,0:T(8,128)(2,1)}, u32[]{:S(2)}) copy-start(bf16[7,4,64,64]{3,2,1,0:T(8,128)(2,1)} %up.5) | copy-start | bytes 688132
  29.4 0.9 %copy-start.5 = (bf16[2,8,32,128]{3,2,1,0:T(8,128)(2,1)S(1)}, bf16[2,8,32,128]{3,2,1,0:T(8,128)(2,1)}, u32[]{:S(2)}) copy-start(bf16[2,8,32,128]{3,2,1,0:T(8,128)(2,1)} %own.5) | copy-start | bytes 393220
  31.9 0.6 copy-start.20
  32.5 13.7 %copy-start.16 = (bf16[8,2,32,128]{3,2,1,0:T(8,128)(2,1)}, bf16[8,2,32,128]{3,2,1,0:T(8,128)(2,1)S(1)}, u32[]{:S(2)}) copy-start(bf16[8,2,32,128]{3,2,1,0:T(8,128)(2,1)S(1)} %get-tuple-element.26.level2) | copy-start | bytes 393220
  32.5 39.8 %collective-permute-start.3 = (bf16[26,32,128]{2,1,0:T(8,128)(2,1)}, bf16[26,32,128]{2,1,0:T(8,128)(2,1)}, u32[]{:S(2)}, u32[]{:S(2)}) collective-permute-start(bf16[26,32,128]{2,1,0:T(8,128)(2,1)} %get-tuple-element.28), channel_id=1, source_target_pairs={{1,2},{2,1},{3,4},{4,3},{5,6},{6,5},{7,8},{8,7},{9,10},{10,9},{11,... | collective-permute-start | bytes 638984 | tf_op jit(solution)/shard_map/ppermute | solution.py:357
  33.9 11.7 %collective-permute-start.6 = (bf16[32,128]{1,0:T(8,128)(2,1)S(1)}, bf16[32,128]{1,0:T(8,128)(2,1)S(1)}, u32[]{:S(2)}, u32[]{:S(2)}) collective-permute-start(bf16[32,128]{1,0:T(8,128)(2,1)S(1)} %get-tuple-element.31), channel_id=1, source_target_pairs={{0,0},{1,1},{2,2},{3,3},{4,4},{5,5},{6,6},{7,7},{8,8},{9,9},{10,10... | collective-permute-start | bytes 24584 | tf_op jit(solution)/shard_map/ppermute | solution.py:357
  46.3 26.1 %all-to-all-start.1 = ((bf16[16,32,128]{2,1,0:T(8,128)(2,1)}), bf16[16,32,128]{2,1,0:T(8,128)(2,1)S(1)}, u32[]{:S(2)}, u32[]{:S(2)}) async-start(bf16[16,32,128]{2,1,0:T(8,128)(2,1)} %broadcast_in_dim.3), calls=%async_computation.1 | async-start | bytes 262144 | tf_op jit(solution)/shard_map/all_to_all | solution.py:396
  57.8 14.6 %collective-permute-start.5 = (bf16[6,32,128]{2,1,0:T(8,128)(2,1)}, bf16[6,32,128]{2,1,0:T(8,128)(2,1)S(1)}, u32[]{:S(2)}, u32[]{:S(2)}) collective-permute-start(bf16[6,32,128]{2,1,0:T(8,128)(2,1)} %get-tuple-element.30), channel_id=1, source_target_pairs={{0,1},{1,0},{2,3},{3,2},{4,5},{5,4},{6,7},{7,6},{8,9},{9,8},{10,11... | collective-permute-start | bytes 147464 | tf_op jit(solution)/shard_map/ppermute | solution.py:357
  59.9 11.9 %collective-permute-start.4 = (bf16[4,32,128]{2,1,0:T(8,128)(2,1)}, bf16[4,32,128]{2,1,0:T(8,128)(2,1)S(1)}, u32[]{:S(2)}, u32[]{:S(2)}) collective-permute-start(bf16[4,32,128]{2,1,0:T(8,128)(2,1)} %get-tuple-element.29), channel_id=1, source_target_pairs={{0,3},{2,5},{3,0},{4,7},{5,2},{6,9},{7,4},{8,11},{9,6},{10,13},{11... | collective-permute-start | bytes 98312 | tf_op jit(solution)/shard_map/ppermute | solution.py:357
  63.2 0.7 copy-start.24
  67.8 1.1 %copy-start.3 = (bf16[2304,256]{1,0:T(8,128)(2,1)}, bf16[2304,256]{1,0:T(8,128)(2,1)S(1)}, u32[]{:S(2)}) copy-start(bf16[2304,256]{1,0:T(8,128)(2,1)S(1)} %get-tuple-element.32.w0) | copy-start | bytes 3538948
  68.9 0.7 copy-start.8
  69.6 0.7 copy-start.10
  70.4 0.7 copy-start.12
  71.1 0.7 copy-start.14
  71.8 0.6 copy-start.22
  72.4 1.0 %copy-start.9 = (bf16[1536,64]{1,0:T(8,128)(2,1)S(1)}, bf16[1536,64]{1,0:T(8,128)(2,1)}, u32[]{:S(2)}) copy-start(bf16[1536,64]{1,0:T(8,128)(2,1)} %copy-done.8) | copy-start | bytes 589828
  73.4 1.0 %copy-start.11 = (bf16[3,384,64]{2,1,0:T(8,128)(2,1)S(1)}, bf16[3,384,64]{2,1,0:T(8,128)(2,1)}, u32[]{:S(2)}) copy-start(bf16[3,384,64]{2,1,0:T(8,128)(2,1)} %copy-done.10) | copy-start | bytes 442372
  74.4 1.0 %copy-start.13 = (bf16[1152,128]{1,0:T(8,128)(2,1)S(1)}, bf16[1152,128]{1,0:T(8,128)(2,1)}, u32[]{:S(2)}) copy-start(bf16[1152,128]{1,0:T(8,128)(2,1)} %copy-done.12) | copy-start | bytes 884740
  75.3 0.9 %copy-start.15 = (bf16[768,64]{1,0:T(8,128)(2,1)S(1)}, bf16[768,64]{1,0:T(8,128)(2,1)}, u32[]{:S(2)}) copy-start(bf16[768,64]{1,0:T(8,128)(2,1)} %copy-done.14) | copy-start | bytes 294916
  76.3 0.9 %copy-start.17 = (bf16[8,2,32,128]{3,2,1,0:T(8,128)(2,1)S(1)}, bf16[8,2,32,128]{3,2,1,0:T(8,128)(2,1)}, u32[]{:S(2)}) copy-start(bf16[8,2,32,128]{3,2,1,0:T(8,128)(2,1)} %copy-done.16) | copy-start | bytes 393220
  77.2 0.8 copy-start.19
  78.0 0.8 copy-start.21
  78.8 0.8 copy-start.23

commit v2 on v1

v2 whole, which is shorter than its diff:
```python
import jax
import jax.numpy as jnp
from jax import lax
from jax.experimental import pallas as pl
from jax.experimental.pallas import tpu as pltpu
from jax.sharding import PartitionSpec as P

LEAF_ROWS = 8
LEAF_COLS = 16
RANK = 64
PROBES = 32
BF = jnp.bfloat16
F32 = jnp.float32

length_scale = 1.5


def dot(left, right):
    return jnp.dot(left, right, preferred_element_type=F32)


def lanes(parts):
    return jnp.concatenate(parts, axis=-1)


def block_slot(e, f, wr, wc):
    return 6 * wr + wc - 3 * min(max(wr - 1 - e, 0), 3) - (
        min(max(wc - 1 - f, 0), 3) if e + 1 <= wr <= e + 3 else 0
    )


def is_near(e, f, wr, wc):
    return e + 1 <= wr <= e + 3 and f + 1 <= wc <= f + 3


def places():
    row = lax.axis_index("gx")
    col = lax.axis_index("gy")
    return row, col, col // 2, col % 2


def prepare_kernel(
    ids_far, coupling_far, up_far, down_far, basis_far, own_far,
    w0, w1, w2, w3, w4, w5, table, wide, up, down0, down1, down2, down3, own,
    ids, coupling, down, basis, ids_sem, level_sems, sems,
):
    row, col, _, _ = places()
    first = pltpu.make_async_copy(ids_far, ids, ids_sem)
    first.start()
    levels = []
    for level in range(8):
        levels.append(
            pltpu.make_async_copy(coupling_far.at[level], coupling.at[level], level_sems.at[level])
        )
    levels[0].start()
    small = [
        pltpu.make_async_copy(source, target, sems.at[at])
        for at, (source, target) in enumerate(
            ((basis_far, basis), (own_far, own), (up_far, up), (down_far, down))
        )
    ]
    for copy in small:
        copy.start()
    for copy in levels[1:]:
        copy.start()

    size = LEAF_ROWS * LEAF_COLS
    theirs = lax.broadcasted_iota(jnp.int32, (size, size), 0)
    ours = lax.broadcasted_iota(jnp.int32, (size, size), 1)
    rows_apart = (theirs // LEAF_COLS - ours // LEAF_COLS).astype(F32)
    cols_apart = (theirs % LEAF_COLS - ours % LEAF_COLS).astype(F32)
    for u in (-1, 0, 1):
        for v in (-1, 0, 1):
            apart_row = rows_apart + float(u * LEAF_ROWS)
            apart_col = cols_apart + float(v * LEAF_COLS)
            scaled = jnp.sqrt(3.0 * (apart_row * apart_row + apart_col * apart_col)) / length_scale
            value = (1.0 + scaled) * jnp.exp(-scaled)
            table[pl.ds((3 * (u + 1) + v + 1) * size, size), :] = value.astype(BF)

    def pair(level, e, wr, wc):
        halves = []
        for f in (0, 1):
            if is_near(e, f, wr, wc):
                halves.append(jnp.zeros((RANK, RANK), BF))
            else:
                halves.append(coupling[level, ids[level, 2 * e + f, block_slot(e, f, wr, wc)]])
        return lanes(halves)

    first.wait()
    levels[0].wait()
    for wr in range(6):
        for wc in range(6):
            at = pl.ds((6 * wr + wc) * RANK, RANK)
            for e in (0, 1):
                w0[at, pl.ds(128 * e, 128)] = pair(0, e, wr, wc)

    for level, out, bit in ((1, w1, row % 2), (2, w2, (row // 2) % 2)):
        levels[level].wait()
        for e in (0, 1):

            @pl.when(bit == e)
            def _(level=level, out=out, e=e):
                for wr in range(6):
                    for wc in range(6):
                        out[pl.ds((6 * wr + wc) * RANK, RANK), :] = pair(level, e, wr, wc)

    def single(level, e, f, wr, wc):
        row_in = jnp.logical_and(wr >= e + 1, wr <= e + 3)
        col_in = jnp.logical_and(wc >= f + 1, wc <= f + 3)
        skipped = 3 * jnp.clip(wr - 1 - e, 0, 3) + jnp.where(row_in, jnp.clip(wc - 1 - f, 0, 3), 0)
        slot = jnp.clip(6 * wr + wc - skipped, 0, 26)
        keep = jnp.where(jnp.logical_and(row_in, col_in), 0.0, 1.0)
        block = coupling[level, ids[level, 2 * e + f, slot]]
        return block * jnp.full((RANK, RANK), keep, F32).astype(BF)

    levels[3].wait()
    e3, f3 = (row // 4) % 2, col % 2
    first3 = 2 - 2 * (row // 8)
    for r in range(4):
        for wc in range(6):
            w3[pl.ds((6 * r + wc) * RANK, RANK), :] = single(3, e3, f3, r + first3, wc)
    levels[4].wait()
    e4, f4 = row // 8, (col // 2) % 2
    for wc in range(6):
        for r in range(2):
            w4[pl.ds((2 * wc + r) * RANK, RANK), :] = single(4, e4, f4, jnp.int32(2 + r), wc)
    for level in (5, 6, 7):
        levels[level].wait()
        f = (col // (1 << (level - 3))) % 2
        for wc in range(6):
            w5[level - 5, pl.ds(wc * RANK, RANK), :] = single(
                level, jnp.int32(0), f, jnp.int32(2), wc
            )

    for copy in small:
        copy.wait()
    blank = jnp.zeros_like(basis)
    wide[...] = jnp.concatenate([lanes([basis[...], blank]), lanes([blank, basis[...]])], axis=0)
    all0 = lanes([down[0, k] for k in range(4)])
    none0 = jnp.zeros_like(all0)
    down0[...] = jnp.concatenate([lanes([all0, none0]), lanes([none0, all0])], axis=0)
    e1, e2 = row % 2, (row // 2) % 2
    both1 = lanes([down[1, 2 * e1], down[1, 2 * e1 + 1]])
    none1 = jnp.zeros_like(both1)
    down1[...] = jnp.concatenate([lanes([both1, none1]), lanes([none1, both1])], axis=0)
    down2[...] = lanes([down[2, 2 * e2], down[2, 2 * e2 + 1]])
    for level in (3, 4, 5, 6):
        e = (row // (1 << (level - 1))) % 2
        f = (col // (1 << (level - 3))) % 2
        down3[level - 3] = down[level, 2 * e + f]


def array(shape, kind=BF):
    return jax.ShapeDtypeStruct(shape, kind)


def call(kernel, out_shape, scratch=(), flops=1 << 24, read=1 << 21, **specs):
    return pl.pallas_call(
        kernel,
        out_shape=out_shape,
        **specs,
        scratch_shapes=list(scratch),
        compiler_params=pltpu.CompilerParams(vmem_limit_bytes=16 << 20),
        cost_estimate=pl.CostEstimate(flops=flops, bytes_accessed=read, transcendentals=0),
    )


def leaf_coeffs(tile, wide_basis):
    rows = tile.shape[0]
    split = tile.reshape(rows, 4, 2, PROBES, 128)
    joined = lanes([split[:, :, 0], split[:, :, 1]]).reshape(-1, 256)
    coeffs = lax.dot_general(
        joined, wide_basis, (((1,), (1,)), ((), ())), preferred_element_type=F32
    )
    return coeffs.astype(BF).reshape(rows, 4, PROBES, 128)


def to_pairs(nodes):
    lead = nodes.shape[:-3]
    split = nodes.reshape(lead + (nodes.shape[-3] // 2, 2, PROBES, RANK))
    return lanes([split[..., 0, :, :], split[..., 1, :, :]])


def raise_pairs(pairs, transfer):
    rows, count = pairs.shape[:2]
    split = pairs.reshape(rows // 2, 2, count, PROBES, 128)
    joined = lanes([split[:, 0], split[:, 1]]).reshape(-1, 256)
    return dot(joined, transfer).astype(BF).reshape(rows // 2, count, PROBES, RANK)


def first_kernel(own, other, above, below, wide, up, sent, mine, beside, rim):
    _, _, _, core = places()
    transfer = up[0].reshape(4 * RANK, RANK)
    kept = {}
    for which, tile in ((core, own), (1 - core, other)):
        coeffs = leaf_coeffs(tile[...], wide[...])
        kept[tile is own] = coeffs
        pairs = to_pairs(raise_pairs(coeffs, transfer)[0])
        for peer in range(16):
            sent[peer, pl.ds(2 * which, 2)] = pairs
    mine[...] = kept[True]
    rim[pl.ds(0, 2)] = leaf_coeffs(above[...], wide[...])
    rim[pl.ds(2, 2)] = leaf_coeffs(below[...], wide[...])

    for r in (0, 1):
        beside[r] = other[r, 7 * core]

        @pl.when(core == 0)
        def _(r=r):
            beside[2 + r] = kept[False][r, 0]

        @pl.when(core == 1)
        def _(r=r):
            beside[2 + r] = kept[False][r, 3]


def second_kernel(
    gathered, own, mine, above, below, rim, up,
    far_out, side_out, third_out, mate_out, level2, level3,
    padded1, padded2,
):
    row, _, _, core = places()
    pairs2 = to_pairs(raise_pairs(gathered[...], up[1].reshape(4 * RANK, RANK)))
    pairs3 = to_pairs(raise_pairs(pairs2, up[2].reshape(4 * RANK, RANK)))[:, 0]
    nodes4 = raise_pairs(pairs3[:, None], up[3].reshape(4 * RANK, RANK))
    far_out[...] = lanes([nodes4[0, 0], nodes4[1, 0]])
    level2[...] = pairs2
    level3[...] = pairs3
    third_out[...] = pairs3

    edge_pair = 3 * core
    edge_col = 7 * core
    nothing = jnp.zeros((2, PROBES, 128), BF)
    padded1[pl.ds(0, 2)] = nothing
    padded1[pl.ds(18, 2)] = nothing
    padded2[pl.ds(0, 2)] = nothing
    padded2[pl.ds(10, 2)] = nothing
    for r in range(16):
        padded1[r + 2] = gathered[r, edge_pair]
    for r in range(8):
        padded2[r + 2] = level2[r, core]
    side_out[0] = above[1, edge_col]
    side_out[1] = own[0, edge_col]
    side_out[2] = own[1, edge_col]
    side_out[3] = below[0, edge_col]
    side_out[4] = rim[0, edge_pair]
    side_out[5] = rim[1, edge_pair]
    side_out[6] = mine[0, edge_pair]
    side_out[7] = mine[1, edge_pair]
    side_out[8] = rim[2, edge_pair]
    side_out[9] = rim[3, edge_pair]
    side_out[pl.ds(10, 6)] = padded1[pl.ds(2 * (row // 2), 6)]
    side_out[pl.ds(16, 6)] = padded2[pl.ds(2 * (row // 4), 6)]
    side_out[pl.ds(22, 4)] = pairs3
    mate_out[0] = above[1, 7 - edge_col]
    mate_out[1] = below[0, 7 - edge_col]
    for r in range(4):
        mate_out[2 + r] = rim[r, 3 - edge_pair]


def third_kernel(
    own, above, below, mine, beside, rim, gathered, level2, level3,
    side, third, mate, w0, w1, w2, w3, table,
    near_sum, far0, far1, far2, far3, tag,
    near, window0, padded1, window1, padded2, window2, window3,
):
    row, _, _, core = places()

    window0[pl.ds(0, 2), pl.ds(1, 4)] = rim[pl.ds(0, 2)]
    window0[pl.ds(2, 2), pl.ds(1, 4)] = mine[...]
    window0[pl.ds(4, 2), pl.ds(1, 4)] = rim[pl.ds(2, 2)]
    for w in range(6):
        window0[w, 5 * core] = side[4 + w]
    for r in range(2):
        window0[r, 5 - 5 * core] = mate[2 + r]
        window0[2 + r, 5 - 5 * core] = beside[2 + r]
        window0[4 + r, 5 - 5 * core] = mate[4 + r]
    far0[...] = dot(
        lanes([window0[w, pl.ds(k, 4)].reshape(-1, 128) for w in range(6) for k in range(3)]),
        w0[...],
    )

    near[0, pl.ds(1, 8)] = above[1]
    near[1, pl.ds(1, 8)] = own[0]
    near[2, pl.ds(1, 8)] = own[1]
    near[3, pl.ds(1, 8)] = below[0]
    for r in range(4):
        near[r, 9 * core] = side[r]
    near[0, 9 - 9 * core] = mate[0]
    near[1, 9 - 9 * core] = beside[0]
    near[2, 9 - 9 * core] = beside[1]
    near[3, 9 - 9 * core] = mate[1]
    for e in (0, 1):
        joined = lanes([near[e + u, pl.ds(v, 8)].reshape(-1, 128) for u in range(3) for v in range(3)])
        near_sum[e] = dot(joined, table[...]).reshape(8, PROBES, 128)

    empty1 = jnp.zeros((2, 4, PROBES, 128), BF)
    padded1[pl.ds(0, 2)] = empty1
    padded1[pl.ds(2, 16)] = gathered[...]
    padded1[pl.ds(18, 2)] = empty1
    for w in range(6):
        for k in range(3):
            window1[w, k + 1 - core] = padded1[2 * (row // 2) + w, k + core]
        window1[w, 3 * core] = side[10 + w]
    far1[...] = dot(
        lanes([window1[w, pl.ds(k, 2)].reshape(-1, 128) for w in range(6) for k in range(3)]),
        w1[...],
    )

    empty2 = jnp.zeros((2, 2, PROBES, 128), BF)
    padded2[pl.ds(0, 2)] = empty2
    padded2[pl.ds(2, 8)] = level2[...]
    padded2[pl.ds(10, 2)] = empty2
    for w in range(6):
        for k in range(2):
            window2[w, k + 1 - core] = padded2[2 * (row // 4) + w, k]
        window2[w, 2 * core] = side[16 + w]
    far2[...] = dot(lanes([window2[w, k] for w in range(6) for k in range(3)]), w2[...])

    for r in range(4):
        window3[r, 2 * core] = side[22 + r]
        window3[r, 1] = level3[r]
        window3[r, 2 - 2 * core] = third[r]
    far3[...] = dot(lanes([window3[r, k] for r in range(4) for k in range(3)]), w3[...])
    tag[...] = jnp.zeros_like(tag)


def copies_kernel(block, tag, out):
    for peer in range(16):
        out[peer] = block[...]


def fourth_kernel(
    top, near_sum, far0, far1, far2, far3, w4, w5, wide, up, down0, down1, down2, down3,
    out,
    padded4, padded5, padded6, padded7,
):
    _, col, chip, _ = places()

    blank = jnp.zeros((2, PROBES, 128), BF)
    padded4[pl.ds(0, 2)] = blank
    padded4[pl.ds(18, 2)] = blank
    for c in range(16):
        padded4[c + 2] = top[(chip - c + 16) % 16]
    by_col = jnp.concatenate([up[4, 0], up[4, 2], up[4, 1], up[4, 3]], axis=0)
    all4 = padded4[pl.ds(2, 16)].reshape(8, 2, PROBES, 128)
    nodes5 = dot(lanes([all4[:, 0], all4[:, 1]]).reshape(-1, 256), by_col)
    nodes5 = nodes5.astype(BF).reshape(8, PROBES, RANK)

    def raise_row(nodes, level):
        pairs = to_pairs(nodes).reshape(-1, 128)
        both = jnp.concatenate([up[level, 0], up[level, 1]], axis=0)
        return dot(pairs, both).astype(BF).reshape(-1, PROBES, RANK)

    nodes6 = raise_row(nodes5, 5)
    nodes7 = raise_row(nodes6, 6)
    gap = jnp.zeros((2, PROBES, RANK), BF)
    for padded, nodes in ((padded5, nodes5), (padded6, nodes6), (padded7, nodes7)):
        count = nodes.shape[0]
        padded[pl.ds(0, 2)] = gap
        padded[pl.ds(2, count)] = nodes
        padded[pl.ds(2 + count, 2)] = gap

    def far_row(padded, level):
        start = 2 * (col // (1 << (level - 2)))
        return dot(lanes([padded[start + k] for k in range(6)]), w5[level - 5])

    start4 = 2 * (chip // 2)
    far4 = dot(lanes([padded4[start4 + k] for k in range(6)]), w4[...])
    local = far_row(padded7, 7).astype(BF)
    local = (far_row(padded6, 6) + dot(local, down3[3])).astype(BF)
    local = (far_row(padded5, 5) + dot(local, down3[2])).astype(BF)
    local = (far4 + dot(local, down3[1])).astype(BF)
    local = (far3[...] + dot(local, down3[0])).astype(BF)
    local2 = (far2[...] + dot(local, down2[...])).astype(BF)
    spread1 = dot(local2, down1[...])
    spread1 = jnp.concatenate([spread1[:, :128], spread1[:, 128:]], axis=0)
    local1 = (far1[...] + spread1).astype(BF)
    spread0 = dot(local1, down0[...]).reshape(2, PROBES, 512)
    spread0 = jnp.stack([spread0[:, :, :256], spread0[:, :, 256:]], axis=1).reshape(-1, 256)
    local0 = (far0[...] + spread0).astype(BF)
    for e in (0, 1):
        far_sum = dot(local0[:, 128 * e : 128 * e + 128], wide[...]).reshape(4, PROBES, 256)
        for q in range(4):
            for f in (0, 1):
                part = far_sum[q, :, 128 * f : 128 * f + 128]
                out[e, 2 * q + f] = (near_sum[e, 2 * q + f] + part).astype(BF)


def route(rule, size_x, size_y):
    pairs = []
    for a in range(size_x):
        for b in range(size_y):
            x, y = rule(a, b)
            if 0 <= x < size_x and 0 <= y < size_y:
                pairs.append((a * size_y + b, x * size_y + y))
    return pairs


def across(core):
    return 1 if core else -1


def shards(probes, leaf_basis, up_transfer, down_transfer, coupling, far_ids):
    size_x, size_y = lax.axis_size("gx"), lax.axis_size("gy")
    both = ("gx", "gy")

    def move(value, rule):
        return lax.ppermute(value, both, route(rule, size_x, size_y))

    other = move(probes, lambda a, b: (a, b ^ 1))
    above = move(probes, lambda a, b: (a + 1, b))
    below = move(probes, lambda a, b: (a - 1, b))

    hbm = pl.BlockSpec(memory_space=pltpu.MemorySpace.HBM)
    block = (PROBES, 128)
    w0, w1, w2, w3, w4, w5, table, wide, up, down0, down1, down2, down3, own = call(
        prepare_kernel,
        [
            array((36 * RANK, 256)), array((36 * RANK, 128)), array((36 * RANK, 128)),
            array((24 * RANK, RANK)), array((12 * RANK, RANK)), array((3, 6 * RANK, RANK)),
            array((9 * 128, 128)), array((128, 256)), array(up_transfer.shape),
            array((128, 512)), array((128, 256)), array((RANK, 128)), array((4, RANK, RANK)),
            array(probes.shape),
        ],
        in_specs=[hbm] * 6,
        scratch=[
            pltpu.SMEM(far_ids.shape, jnp.int32), pltpu.VMEM(coupling.shape, BF),
            pltpu.VMEM(down_transfer.shape, BF), pltpu.VMEM(leaf_basis.shape[::-1], BF),
            pltpu.SemaphoreType.DMA, pltpu.SemaphoreType.DMA((8,)), pltpu.SemaphoreType.DMA((4,)),
        ],
    )(
        *[
            pltpu.with_memory_space_constraint(value, pltpu.MemorySpace.HBM)
            for value in (far_ids, coupling, up_transfer, down_transfer, leaf_basis.T, probes)
        ]
    )

    sent, mine, beside, rim = call(
        first_kernel,
        [array((16, 4) + block), array((2, 4) + block), array((4,) + block), array((4, 4) + block)],
    )(own, other, above, below, wide, up)
    gathered = lax.all_to_all(sent, "gx", 0, 0)

    far_out, side_out, third_out, mate_out, level2, level3 = call(
        second_kernel,
        [
            array(block), array((26,) + block), array((4,) + block), array((6,) + block),
            array((8, 2) + block), array((4,) + block),
        ],
        scratch=[pltpu.VMEM((20,) + block, BF), pltpu.VMEM((12,) + block, BF)],
    )(gathered, own, mine, above, below, rim, up)

    chips = size_y // 2
    side = move(side_out, lambda a, b: (a, b + across(b % 2)))
    third = move(third_out, lambda a, b: (a, b + 3 - 6 * (b % 2)))
    mate = move(mate_out, lambda a, b: (a, b ^ 1))
    top = move(far_out, lambda a, b: (a, 2 * ((b // 2 + a) % chips) + b % 2))

    near_sum, far0, far1, far2, far3, tag = call(
        third_kernel,
        [
            array((2, 8) + block, F32), array((4 * PROBES, 256), F32),
            array((2 * PROBES, 128), F32), array((PROBES, 128), F32), array((PROBES, RANK), F32),
            array((8, 128), F32),
        ],
        scratch=[
            pltpu.VMEM(lead + block, BF)
            for lead in ((4, 10), (6, 6), (20, 4), (6, 4), (12, 2), (6, 3), (4, 3))
        ],
    )(
        own, above, below, mine, beside, rim, gathered, level2, level3, side, third, mate,
        w0, w1, w2, w3, table,
    )
    copies = call(copies_kernel, array((16,) + block))(top, tag)
    top = lax.all_to_all(copies, "gx", 0, 0)

    return call(
        fourth_kernel,
        array(probes.shape),
        scratch=[pltpu.VMEM((20,) + block, BF)]
        + [pltpu.VMEM((count + 4, PROBES, RANK), BF) for count in (8, 4, 2)],
    )(top, near_sum, far0, far1, far2, far3, w4, w5, wide, up, down0, down1, down2, down3)


def solution(mesh):
    in_specs = (P("gx", "gy", None, None), P(), P(), P(), P(), P())
    out_specs = P("gx", "gy", None, None)
    return jax.shard_map(shards, mesh=mesh, in_specs=in_specs, out_specs=out_specs, check_vma=False)
```

time: 85.2 us -> 72 us (0.85)
  the two profiles are of different devices: /device:TPU:2 before, /device:TPU:1 now
where the time goes in v2:
time: 72 us; the launch traced here: 71.7 us
  blocking collectives  40.4 us (56%)
  starting transfers between devices  23 us (32%)
  Pallas kernels  7.88 us (11%)
    all_to_all x1, blocking collectives, shards(): top = lax.all_to_all(copies, 'gx', 0, 0)  26.4 us
    ppermute x7, starting transfers between devices, move(): return lax.ppermute(value, both, route(rule, size_x, size_y))  23 us
    all_to_all x1, blocking collectives, shards(): gathered = lax.all_to_all(sent, 'gx', 0, 0)  14 us
    pallas_call x1, Pallas kernels, shards(): call(prepare_kernel, [array((36 * RANK, 256)), array((36 * RANK, 128)), a...  3.05 us
    pallas_call x1, Pallas kernels, shards(): call(fourth_kernel, array(probes.shape), scratch=[pltpu.VMEM((20,) + bloc...  2.53 us
  transfers between devices with their start and end apart: 7, of which 1 were waited for; matrix products, arithmetic and copies ran while one was open for 0% of the time, Pallas kernels for 5%

profile of v2, /device:TPU:1, one launch (start us, length us, event | category | flops | bytes accessed | tf_op | source)
XLA Modules:
  0.0 71.7 jit_solution(16726278660941411686)
XLA Ops:
  0.0 8.8 %collective-permute-start = (bf16[2,8,32,128]{3,2,1,0:T(8,128)(2,1)}, bf16[2,8,32,128]{3,2,1,0:T(8,128)(2,1)S(1)}, u32[]{:S(2)}, u32[]{:S(2)}) collective-permute-start(bf16[2,8,32,128]{3,2,1,0:T(8,128)(2,1)} %own_far.1), channel_id=1, source_target_pairs={{0,1},{1,0},{2,3},{3,2},{4,5},{5,4},{6,7},{7,6},{8,9},{9,8},{10,11... | collective-permute-start | bytes 393224 | tf_op jit(solution)/shard_map/ppermute | solution.py:409
  8.8 1.3 %collective-permute-start.2 = (bf16[2,8,32,128]{3,2,1,0:T(8,128)(2,1)}, bf16[2,8,32,128]{3,2,1,0:T(8,128)(2,1)S(1)}, u32[]{:S(2)}, u32[]{:S(2)}) collective-permute-start(bf16[2,8,32,128]{3,2,1,0:T(8,128)(2,1)} %own_far.1), channel_id=1, source_target_pairs={{32,0},{33,1},{34,2},{35,3},{36,4},{37,5},{38,6},{39,7},{40,8},{41... | collective-permute-start | bytes 393224 | tf_op jit(solution)/shard_map/ppermute | solution.py:409
  10.1 4.0 %collective-permute-start.1 = (bf16[2,8,32,128]{3,2,1,0:T(8,128)(2,1)}, bf16[2,8,32,128]{3,2,1,0:T(8,128)(2,1)S(1)}, u32[]{:S(2)}, u32[]{:S(2)}) collective-permute-start(bf16[2,8,32,128]{3,2,1,0:T(8,128)(2,1)} %own_far.1), channel_id=1, source_target_pairs={{0,32},{1,33},{2,34},{3,35},{4,36},{5,37},{6,38},{7,39},{8,40},{9,... | collective-permute-start | bytes 393224 | tf_op jit(solution)/shard_map/ppermute | solution.py:409
  14.1 3.1 %shard_map.64 = (bf16[2304,256]{1,0:T(8,128)(2,1)S(1)}, bf16[2304,128]{1,0:T(8,128)(2,1)S(1)}, bf16[2304,128]{1,0:T(8,128)(2,1)S(1)}, bf16[1536,64]{1,0:T(8,128)...) custom-call(s32[8,4,27]{2,1,0:T(4,128)} %ids_far.1, ...), custom_call_target="tpu_custom_call" | custom-call | flops 16777216 | bytes 2097152 | tf_op jit(solution)/shard_map/pallas_call | solution.py:417
  17.1 0.0 collective-permute-done.other
  17.2 0.0 collective-permute-done.2.below
  17.2 0.0 collective-permute-done.1.above
  17.2 0.6 shard_map.65
  17.8 14.0 %all_to_all.10.gathered = bf16[16,4,32,128]{3,2,1,0:T(8,128)(2,1)S(1)} all-to-all(bf16[16,4,32,128]{3,2,1,0:T(8,128)(2,1)S(1)} %get-tuple-element.38), channel_id=1, replica_groups=mesh['gx'=16,'gy'=32] {'gx'}, dimensions={0} | all-to-all | bytes 1048576 | tf_op jit(solution)/shard_map/all_to_all | solution.py:443
  31.8 0.8 %shard_map.66 = (bf16[32,128]{1,0:T(8,128)(2,1)S(1)}, bf16[26,32,128]{2,1,0:T(8,128)(2,1)S(1)}, bf16[4,32,128]{2,1,0:T(8,128)(2,1)S(1)}, bf16[6,32,128]{2,1,0:T(...) custom-call(bf16[16,4,32,128]{3,2,1,0:T(8,128)(2,1)S(1)} %all_to_all.10.gathered, ...), custom_call_target="tpu_custom_call" | custom-call | flops 16777216 | bytes 2097152 | tf_op jit(solution)/shard_map/pallas_call | solution.py:445
  32.5 5.7 %collective-permute-start.4 = (bf16[26,32,128]{2,1,0:T(8,128)(2,1)S(1)}, bf16[26,32,128]{2,1,0:T(8,128)(2,1)S(1)}, u32[]{:S(2)}, u32[]{:S(2)}) collective-permute-start(bf16[26,32,128]{2,1,0:T(8,128)(2,1)S(1)} %get-tuple-element.45), channel_id=1, source_target_pairs={{1,2},{2,1},{3,4},{4,3},{5,6},{6,5},{7,8},{8,7},{9,10},{10,9},{11,... | collective-permute-start | bytes 638984 | tf_op jit(solution)/shard_map/ppermute | solution.py:409
  38.2 1.9 %collective-permute-start.6 = (bf16[6,32,128]{2,1,0:T(8,128)(2,1)S(1)}, bf16[6,32,128]{2,1,0:T(8,128)(2,1)S(1)}, u32[]{:S(2)}, u32[]{:S(2)}) collective-permute-start(bf16[6,32,128]{2,1,0:T(8,128)(2,1)S(1)} %get-tuple-element.47), channel_id=1, source_target_pairs={{0,1},{1,0},{2,3},{3,2},{4,5},{5,4},{6,7},{7,6},{8,9},{9,8},{10,11... | collective-permute-start | bytes 147464 | tf_op jit(solution)/shard_map/ppermute | solution.py:409
  40.2 0.7 collective-permute-start.5
  40.8 0.7 collective-permute-start.3
  41.5 0.0 collective-permute-done.5.third
  41.5 0.0 collective-permute-done.6.mate
  41.5 0.2 collective-permute-done.4.side
  41.7 0.9 %shard_map.67 = (f32[2,8,32,128]{3,2,1,0:T(8,128)S(1)}, f32[128,256]{1,0:T(8,128)S(1)}, f32[64,128]{1,0:T(8,128)S(1)}, f32[32,128]{1,0:T(8,128)S(1)}, f32[32,64]{1,0:T(8,128)S(1)}, /*index=5*/f32[8,128]{1,0:T(8,128)S(1)}) custom-call(bf16[2,8,32,128]{3,2,1,0:T(8,128)(2,1)S(1)} %get-tuple-element.35.own, ...), custom_call_target="tpu_custom_call" | custom-call | flops 16777216 | bytes 2097152 | tf_op jit(solution)/shard_map/pallas_call | solution.py:460
  42.6 0.0 collective-permute-done.3.block
  42.7 26.4 %all_to_all.11.top = bf16[16,32,128]{2,1,0:T(8,128)(2,1)S(1)} all-to-all(bf16[16,32,128]{2,1,0:T(8,128)(2,1)S(1)} %shard_map.68), channel_id=1, replica_groups=mesh['gx'=16,'gy'=32] {'gx'}, dimensions={0} | all-to-all | bytes 262144 | tf_op jit(solution)/shard_map/all_to_all | solution.py:476
  69.1 2.5 %shard_map.69 = bf16[2,8,32,128]{3,2,1,0:T(8,128)(2,1)} custom-call(bf16[16,32,128]{2,1,0:T(8,128)(2,1)S(1)} %all_to_all.11.top, f32[2,8,32,128]{3,2,1,0:T(8,128)S(1)} %get-tuple-element.54.near_sum, f32[128,256]{1,0:T(8,128)S(1)} %get-tuple-element.55.far0, f32[64,128]{1,0:T(8,128)S(1)} %get-tuple-element.56.far1, f32[32,128]{1,0:T(8,128)S(1)} %get-tuple-element.57.far2, ...), custom_call_target="tpu_custom_call" | custom-call | flops 16777216 | bytes 2097152 | tf_op jit(solution)/shard_map/pallas_call | solution.py:478
  (1 shorter events, 0.0 us)
Async XLA Ops:
  0.0 17.1 %collective-permute-start = (bf16[2,8,32,128]{3,2,1,0:T(8,128)(2,1)}, bf16[2,8,32,128]{3,2,1,0:T(8,128)(2,1)S(1)}, u32[]{:S(2)}, u32[]{:S(2)}) collective-permute-start(bf16[2,8,32,128]{3,2,1,0:T(8,128)(2,1)} %own_far.1), channel_id=1, source_target_pairs={{0,1},{1,0},{2,3},{3,2},{4,5},{5,4},{6,7},{7,6},{8,9},{9,8},{10,11... | collective-permute-start | bytes 393224 | tf_op jit(solution)/shard_map/ppermute | solution.py:409
  8.8 8.4 %collective-permute-start.2 = (bf16[2,8,32,128]{3,2,1,0:T(8,128)(2,1)}, bf16[2,8,32,128]{3,2,1,0:T(8,128)(2,1)S(1)}, u32[]{:S(2)}, u32[]{:S(2)}) collective-permute-start(bf16[2,8,32,128]{3,2,1,0:T(8,128)(2,1)} %own_far.1), channel_id=1, source_target_pairs={{32,0},{33,1},{34,2},{35,3},{36,4},{37,5},{38,6},{39,7},{40,8},{41... | collective-permute-start | bytes 393224 | tf_op jit(solution)/shard_map/ppermute | solution.py:409
  10.1 7.1 %collective-permute-start.1 = (bf16[2,8,32,128]{3,2,1,0:T(8,128)(2,1)}, bf16[2,8,32,128]{3,2,1,0:T(8,128)(2,1)S(1)}, u32[]{:S(2)}, u32[]{:S(2)}) collective-permute-start(bf16[2,8,32,128]{3,2,1,0:T(8,128)(2,1)} %own_far.1), channel_id=1, source_target_pairs={{0,32},{1,33},{2,34},{3,35},{4,36},{5,37},{6,38},{7,39},{8,40},{9,... | collective-permute-start | bytes 393224 | tf_op jit(solution)/shard_map/ppermute | solution.py:409
  32.5 9.2 %collective-permute-start.4 = (bf16[26,32,128]{2,1,0:T(8,128)(2,1)S(1)}, bf16[26,32,128]{2,1,0:T(8,128)(2,1)S(1)}, u32[]{:S(2)}, u32[]{:S(2)}) collective-permute-start(bf16[26,32,128]{2,1,0:T(8,128)(2,1)S(1)} %get-tuple-element.45), channel_id=1, source_target_pairs={{1,2},{2,1},{3,4},{4,3},{5,6},{6,5},{7,8},{8,7},{9,10},{10,9},{11,... | collective-permute-start | bytes 638984 | tf_op jit(solution)/shard_map/ppermute | solution.py:409
  38.2 3.3 %collective-permute-start.6 = (bf16[6,32,128]{2,1,0:T(8,128)(2,1)S(1)}, bf16[6,32,128]{2,1,0:T(8,128)(2,1)S(1)}, u32[]{:S(2)}, u32[]{:S(2)}) collective-permute-start(bf16[6,32,128]{2,1,0:T(8,128)(2,1)S(1)} %get-tuple-element.47), channel_id=1, source_target_pairs={{0,1},{1,0},{2,3},{3,2},{4,5},{5,4},{6,7},{7,6},{8,9},{9,8},{10,11... | collective-permute-start | bytes 147464 | tf_op jit(solution)/shard_map/ppermute | solution.py:409
  40.2 1.3 %collective-permute-start.5 = (bf16[4,32,128]{2,1,0:T(8,128)(2,1)S(1)}, bf16[4,32,128]{2,1,0:T(8,128)(2,1)S(1)}, u32[]{:S(2)}, u32[]{:S(2)}) collective-permute-start(bf16[4,32,128]{2,1,0:T(8,128)(2,1)S(1)} %get-tuple-element.46), channel_id=1, source_target_pairs={{0,3},{2,5},{3,0},{4,7},{5,2},{6,9},{7,4},{8,11},{9,6},{10,13},{11... | collective-permute-start | bytes 98312 | tf_op jit(solution)/shard_map/ppermute | solution.py:409
  40.8 1.8 %collective-permute-start.3 = (bf16[32,128]{1,0:T(8,128)(2,1)S(1)}, bf16[32,128]{1,0:T(8,128)(2,1)S(1)}, u32[]{:S(2)}, u32[]{:S(2)}) collective-permute-start(bf16[32,128]{1,0:T(8,128)(2,1)S(1)} %get-tuple-element.41), channel_id=1, source_target_pairs={{0,0},{1,1},{2,2},{3,3},{4,4},{5,5},{6,6},{7,7},{8,8},{9,9},{10,10... | collective-permute-start | bytes 24584 | tf_op jit(solution)/shard_map/ppermute | solution.py:409

commit v3 on v2

--- a/solution.py
+++ b/solution.py
@@ -188,46 +188,46 @@
     return dot(joined, transfer).astype(BF).reshape(rows // 2, count, PROBES, RANK)
 
 
-def first_kernel(own, other, above, below, wide, up, sent, mine, beside, rim):
+def first_kernel(own, above, below, wide, up, pack, low, mine, rim):
     _, _, _, core = places()
-    transfer = up[0].reshape(4 * RANK, RANK)
-    kept = {}
-    for which, tile in ((core, own), (1 - core, other)):
-        coeffs = leaf_coeffs(tile[...], wide[...])
-        kept[tile is own] = coeffs
-        pairs = to_pairs(raise_pairs(coeffs, transfer)[0])
-        for peer in range(16):
-            sent[peer, pl.ds(2 * which, 2)] = pairs
-    mine[...] = kept[True]
+    coeffs = leaf_coeffs(own[...], wide[...])
+    pairs = to_pairs(raise_pairs(coeffs, up[0].reshape(4 * RANK, RANK))[0])
+    mine[...] = coeffs
     rim[pl.ds(0, 2)] = leaf_coeffs(above[...], wide[...])
     rim[pl.ds(2, 2)] = leaf_coeffs(below[...], wide[...])
-
-    for r in (0, 1):
-        beside[r] = other[r, 7 * core]
-
-        @pl.when(core == 0)
-        def _(r=r):
-            beside[2 + r] = kept[False][r, 0]
-
-        @pl.when(core == 1)
-        def _(r=r):
-            beside[2 + r] = kept[False][r, 3]
-
-
-def second_kernel(
-    gathered, own, mine, above, below, rim, up,
-    far_out, side_out, third_out, mate_out, level2, level3,
-    padded1, padded2,
-):
-    row, _, _, core = places()
+    low[...] = pairs
+
+    edge_pair = 3 - 3 * core
+    edge_col = 7 - 7 * core
+    pack[pl.ds(0, 2)] = pairs
+    pack[2] = mine[0, edge_pair]
+    pack[3] = mine[1, edge_pair]
+    pack[4] = own[0, edge_col]
+    pack[5] = own[1, edge_col]
+    pack[6] = above[1, edge_col]
+    pack[7] = below[0, edge_col]
+    for r in range(4):
+        pack[8 + r] = rim[r, edge_pair]
+
+
+def strip_kernel(low, packed, sent):
+    _, _, _, core = places()
+    for peer in range(16):
+        sent[peer, pl.ds(2 * core, 2)] = low[...]
+        sent[peer, pl.ds(2 - 2 * core, 2)] = packed[pl.ds(0, 2)]
+
+
+def second_kernel(gathered, up, far_out, level2, level3):
     pairs2 = to_pairs(raise_pairs(gathered[...], up[1].reshape(4 * RANK, RANK)))
     pairs3 = to_pairs(raise_pairs(pairs2, up[2].reshape(4 * RANK, RANK)))[:, 0]
     nodes4 = raise_pairs(pairs3[:, None], up[3].reshape(4 * RANK, RANK))
     far_out[...] = lanes([nodes4[0, 0], nodes4[1, 0]])
     level2[...] = pairs2
     level3[...] = pairs3
-    third_out[...] = pairs3
-
+
+
+def side_kernel(gathered, own, mine, above, below, rim, level2, level3, side_out, padded1, padded2):
+    row, _, _, core = places()
     edge_pair = 3 * core
     edge_col = 7 * core
     nothing = jnp.zeros((2, PROBES, 128), BF)
@@ -251,16 +251,12 @@
     side_out[9] = rim[3, edge_pair]
     side_out[pl.ds(10, 6)] = padded1[pl.ds(2 * (row // 2), 6)]
     side_out[pl.ds(16, 6)] = padded2[pl.ds(2 * (row // 4), 6)]
-    side_out[pl.ds(22, 4)] = pairs3
-    mate_out[0] = above[1, 7 - edge_col]
-    mate_out[1] = below[0, 7 - edge_col]
-    for r in range(4):
-        mate_out[2 + r] = rim[r, 3 - edge_pair]
+    side_out[pl.ds(22, 4)] = level3[...]
 
 
 def third_kernel(
-    own, above, below, mine, beside, rim, gathered, level2, level3,
-    side, third, mate, w0, w1, w2, w3, table,
+    own, above, below, mine, packed, rim, gathered, level2, level3,
+    side, third, w0, w1, w2, w3, table,
     near_sum, far0, far1, far2, far3, tag,
     near, window0, padded1, window1, padded2, window2, window3,
 ):
@@ -272,9 +268,9 @@
     for w in range(6):
         window0[w, 5 * core] = side[4 + w]
     for r in range(2):
-        window0[r, 5 - 5 * core] = mate[2 + r]
-        window0[2 + r, 5 - 5 * core] = beside[2 + r]
-        window0[4 + r, 5 - 5 * core] = mate[4 + r]
+        window0[r, 5 - 5 * core] = packed[8 + r]
+        window0[2 + r, 5 - 5 * core] = packed[2 + r]
+        window0[4 + r, 5 - 5 * core] = packed[10 + r]
     far0[...] = dot(
         lanes([window0[w, pl.ds(k, 4)].reshape(-1, 128) for w in range(6) for k in range(3)]),
         w0[...],
@@ -286,10 +282,10 @@
     near[3, pl.ds(1, 8)] = below[0]
     for r in range(4):
         near[r, 9 * core] = side[r]
-    near[0, 9 - 9 * core] = mate[0]
-    near[1, 9 - 9 * core] = beside[0]
-    near[2, 9 - 9 * core] = beside[1]
-    near[3, 9 - 9 * core] = mate[1]
+    near[0, 9 - 9 * core] = packed[6]
+    near[1, 9 - 9 * core] = packed[4]
+    near[2, 9 - 9 * core] = packed[5]
+    near[3, 9 - 9 * core] = packed[7]
     for e in (0, 1):
         joined = lanes([near[e + u, pl.ds(v, 8)].reshape(-1, 128) for u in range(3) for v in range(3)])
         near_sum[e] = dot(joined, table[...]).reshape(8, PROBES, 128)
@@ -408,7 +404,6 @@
     def move(value, rule):
         return lax.ppermute(value, both, route(rule, size_x, size_y))
 
-    other = move(probes, lambda a, b: (a, b ^ 1))
     above = move(probes, lambda a, b: (a + 1, b))
     below = move(probes, lambda a, b: (a - 1, b))
 
@@ -436,25 +431,28 @@
         ]
     )
 
-    sent, mine, beside, rim = call(
+    pack, low, mine, rim = call(
         first_kernel,
-        [array((16, 4) + block), array((2, 4) + block), array((4,) + block), array((4, 4) + block)],
-    )(own, other, above, below, wide, up)
+        [array((12,) + block), array((2,) + block), array((2, 4) + block), array((4, 4) + block)],
+    )(own, above, below, wide, up)
+    packed = move(pack, lambda a, b: (a, b ^ 1))
+    sent = call(strip_kernel, array((16, 4) + block))(low, packed)
     gathered = lax.all_to_all(sent, "gx", 0, 0)
 
-    far_out, side_out, third_out, mate_out, level2, level3 = call(
+    far_out, level2, level3 = call(
         second_kernel,
-        [
-            array(block), array((26,) + block), array((4,) + block), array((6,) + block),
-            array((8, 2) + block), array((4,) + block),
-        ],
+        [array(block), array((8, 2) + block), array((4,) + block)],
+    )(gathered, up)
+    side_out = call(
+        side_kernel,
+        array((26,) + block),
         scratch=[pltpu.VMEM((20,) + block, BF), pltpu.VMEM((12,) + block, BF)],
-    )(gathered, own, mine, above, below, rim, up)
+        flops=1 << 32,
+    )(gathered, own, mine, above, below, rim, level2, level3)
 
     chips = size_y // 2
     side = move(side_out, lambda a, b: (a, b + across(b % 2)))
-    third = move(third_out, lambda a, b: (a, b + 3 - 6 * (b % 2)))
-    mate = move(mate_out, lambda a, b: (a, b ^ 1))
+    third = move(level3, lambda a, b: (a, b + 3 - 6 * (b % 2)))
     top = move(far_out, lambda a, b: (a, 2 * ((b // 2 + a) % chips) + b % 2))
 
     near_sum, far0, far1, far2, far3, tag = call(
@@ -468,8 +466,10 @@
             pltpu.VMEM(lead + block, BF)
             for lead in ((4, 10), (6, 6), (20, 4), (6, 4), (12, 2), (6, 3), (4, 3))
         ],
+        flops=1,
+        read=1,
     )(
-        own, above, below, mine, beside, rim, gathered, level2, level3, side, third, mate,
+        own, above, below, mine, packed, rim, gathered, level2, level3, side, third,
         w0, w1, w2, w3, table,
     )
     copies = call(copies_kernel, array((16,) + block))(top, tag)

time: 72 us -> 70.4 us (0.978)
  the two profiles are of different devices: /device:TPU:1 before, /device:TPU:96 now
where the time goes in v3:
time: 70.4 us; the launch traced here: 70.1 us
  blocking collectives  42.9 us (61%)
  starting transfers between devices  17 us (24%)
  Pallas kernels  7.82 us (11%)
  waiting for transfers between devices  2.19 us (3%)
    all_to_all x1, blocking collectives, shards(): top = lax.all_to_all(copies, 'gx', 0, 0)  21.8 us
    all_to_all x1, blocking collectives, shards(): gathered = lax.all_to_all(sent, 'gx', 0, 0)  21.1 us
    ppermute x6, starting transfers between devices, move(): return lax.ppermute(value, both, route(rule, size_x, size_y))  17 us
    pallas_call x1, Pallas kernels, shards(): call(prepare_kernel, [array((36 * RANK, 256)), array((36 * RANK, 128)), a...  3.05 us
    pallas_call x1, Pallas kernels, shards(): call(fourth_kernel, array(probes.shape), scratch=[pltpu.VMEM((20,) + bloc...  2.53 us
    ppermute x6, waiting for transfers between devices, move(): return lax.ppermute(value, both, route(rule, size_x, size_y))  2.19 us
  transfers between devices with their start and end apart: 6, of which 2 were waited for; matrix products, arithmetic and copies ran while one was open for 0% of the time, Pallas kernels for 6%

profile of v3, /device:TPU:96, one launch (start us, length us, event | category | flops | bytes accessed | tf_op | source)
XLA Modules:
  0.0 70.1 jit_solution(3670908348538464790)
XLA Ops:
  0.0 1.3 %collective-permute-start.1 = (bf16[2,8,32,128]{3,2,1,0:T(8,128)(2,1)}, bf16[2,8,32,128]{3,2,1,0:T(8,128)(2,1)S(1)}, u32[]{:S(2)}, u32[]{:S(2)}) collective-permute-start(bf16[2,8,32,128]{3,2,1,0:T(8,128)(2,1)} %own_far.1), channel_id=1, source_target_pairs={{32,0},{33,1},{34,2},{35,3},{36,4},{37,5},{38,6},{39,7},{40,8},{41... | collective-permute-start | bytes 393224 | tf_op jit(solution)/shard_map/ppermute | solution.py:405
  1.3 4.6 %collective-permute-start = (bf16[2,8,32,128]{3,2,1,0:T(8,128)(2,1)}, bf16[2,8,32,128]{3,2,1,0:T(8,128)(2,1)S(1)}, u32[]{:S(2)}, u32[]{:S(2)}) collective-permute-start(bf16[2,8,32,128]{3,2,1,0:T(8,128)(2,1)} %own_far.1), channel_id=1, source_target_pairs={{0,32},{1,33},{2,34},{3,35},{4,36},{5,37},{6,38},{7,39},{8,40},{9,... | collective-permute-start | bytes 393224 | tf_op jit(solution)/shard_map/ppermute | solution.py:405
  5.8 3.1 %shard_map.64 = (bf16[2304,256]{1,0:T(8,128)(2,1)S(1)}, bf16[2304,128]{1,0:T(8,128)(2,1)S(1)}, bf16[2304,128]{1,0:T(8,128)(2,1)S(1)}, bf16[1536,64]{1,0:T(8,128)...) custom-call(s32[8,4,27]{2,1,0:T(4,128)} %ids_far.1, ...), custom_call_target="tpu_custom_call" | custom-call | flops 16777216 | bytes 2097152 | tf_op jit(solution)/shard_map/pallas_call | solution.py:412
  8.9 0.0 collective-permute-done.1.below
  8.9 0.0 collective-permute-done.above
  8.9 0.5 shard_map.65
  9.4 1.9 %collective-permute-start.2 = (bf16[12,32,128]{2,1,0:T(8,128)(2,1)S(1)}, bf16[12,32,128]{2,1,0:T(8,128)(2,1)S(1)}, u32[]{:S(2)}, u32[]{:S(2)}) collective-permute-start(bf16[12,32,128]{2,1,0:T(8,128)(2,1)S(1)} %get-tuple-element.36), channel_id=1, source_target_pairs={{0,1},{1,0},{2,3},{3,2},{4,5},{5,4},{6,7},{7,6},{8,9},{9,8},{10,11... | collective-permute-start | bytes 294920 | tf_op jit(solution)/shard_map/ppermute | solution.py:405
  11.3 1.3 %collective-permute-done.2.packed = bf16[12,32,128]{2,1,0:T(8,128)(2,1)S(1)} collective-permute-done((bf16[12,32,128]{2,1,0:T(8,128)(2,1)S(1)}, bf16[12,32,128]{2,1,0:T(8,128)(2,1)S(1)}, u32[]{:S(2)}, u32[]{:S(2)}) %collective-permute-start.2) | collective-permute-done | bytes 98336 | tf_op jit(solution)/shard_map/ppermute | solution.py:405
  12.6 0.1 shard_map.66
  12.7 21.1 %all_to_all.10.gathered = bf16[16,4,32,128]{3,2,1,0:T(8,128)(2,1)S(1)} all-to-all(bf16[16,4,32,128]{3,2,1,0:T(8,128)(2,1)S(1)} %shard_map.66), channel_id=1, replica_groups=mesh['gx'=16,'gy'=32] {'gx'}, dimensions={0} | all-to-all | bytes 1048576 | tf_op jit(solution)/shard_map/all_to_all | solution.py:440
  33.8 0.8 %shard_map.67 = (bf16[32,128]{1,0:T(8,128)(2,1)S(1)}, bf16[8,2,32,128]{3,2,1,0:T(8,128)(2,1)S(1)}, bf16[4,32,128]{2,1,0:T(8,128)(2,1)S(1)}) custom-call(bf16[16,4,32,128]{3,2,1,0:T(8,128)(2,1)S(1)} %all_to_all.10.gathered, bf16[7,4,64,64]{3,2,1,0:T(8,128)(2,1)S(1)} %get-tuple-element.34.up), custom_call_target="tpu_custom_call" | custom-call | flops 16777216 | bytes 2097152 | tf_op jit(solution)/shard_map/pallas_call | solution.py:442
  34.6 1.9 %collective-permute-start.4 = (bf16[26,32,128]{2,1,0:T(8,128)(2,1)S(1)}, bf16[26,32,128]{2,1,0:T(8,128)(2,1)S(1)}, u32[]{:S(2)}, u32[]{:S(2)}) collective-permute-start(bf16[26,32,128]{2,1,0:T(8,128)(2,1)S(1)} %shard_map.68), channel_id=1, source_target_pairs={{1,2},{2,1},{3,4},{4,3},{5,6},{6,5},{7,8},{8,7},{9,10},{10,9},{11,... | collective-permute-start | bytes 638984 | tf_op jit(solution)/shard_map/ppermute | solution.py:405
  36.6 6.7 %collective-permute-start.5 = (bf16[4,32,128]{2,1,0:T(8,128)(2,1)S(1)}, bf16[4,32,128]{2,1,0:T(8,128)(2,1)S(1)}, u32[]{:S(2)}, u32[]{:S(2)}) collective-permute-start(bf16[4,32,128]{2,1,0:T(8,128)(2,1)S(1)} %get-tuple-element.41.level3), channel_id=1, source_target_pairs={{0,3},{2,5},{3,0},{4,7},{5,2},{6,9},{7,4},{8,11},{9,6},{10,13},{11... | collective-permute-start | bytes 98312 | tf_op jit(solution)/shard_map/ppermute | solution.py:405
  43.2 0.7 collective-permute-start.3
  43.9 0.9 %collective-permute-done.5.third = bf16[4,32,128]{2,1,0:T(8,128)(2,1)S(1)} collective-permute-done((bf16[4,32,128]{2,1,0:T(8,128)(2,1)S(1)}, bf16[4,32,128]{2,1,0:T(8,128)(2,1)S(1)}, u32[]{:S(2)}, u32[]{:S(2)}) %collective-permute-start.5) | collective-permute-done | bytes 32800 | tf_op jit(solution)/shard_map/ppermute | solution.py:405
  44.8 0.0 collective-permute-done.4.side
  44.8 0.9 %shard_map.69 = (f32[2,8,32,128]{3,2,1,0:T(8,128)S(1)}, f32[128,256]{1,0:T(8,128)S(1)}, f32[64,128]{1,0:T(8,128)S(1)}, f32[32,128]{1,0:T(8,128)S(1)}, f32[32,64]{1,0:T(8,128)S(1)}, /*index=5*/f32[8,128]{1,0:T(8,128)S(1)}) custom-call(bf16[2,8,32,128]{3,2,1,0:T(8,128)(2,1)S(1)} %get-tuple-element.32.own, ...), custom_call_target="tpu_custom_call" | custom-call | flops 1 | bytes 1 | tf_op jit(solution)/shard_map/pallas_call | solution.py:458
  45.7 0.0 collective-permute-done.3.block
  45.7 21.8 %all_to_all.11.top = bf16[16,32,128]{2,1,0:T(8,128)(2,1)S(1)} all-to-all(bf16[16,32,128]{2,1,0:T(8,128)(2,1)S(1)} %shard_map.70), channel_id=1, replica_groups=mesh['gx'=16,'gy'=32] {'gx'}, dimensions={0} | all-to-all | bytes 262144 | tf_op jit(solution)/shard_map/all_to_all | solution.py:476
  67.5 2.5 %shard_map.71 = bf16[2,8,32,128]{3,2,1,0:T(8,128)(2,1)} custom-call(bf16[16,32,128]{2,1,0:T(8,128)(2,1)S(1)} %all_to_all.11.top, f32[2,8,32,128]{3,2,1,0:T(8,128)S(1)} %get-tuple-element.48.near_sum, f32[128,256]{1,0:T(8,128)S(1)} %get-tuple-element.49.far0, f32[64,128]{1,0:T(8,128)S(1)} %get-tuple-element.50.far1, f32[32,128]{1,0:T(8,128)S(1)} %get-tuple-element.51.far2, ...), custom_call_target="tpu_custom_call" | custom-call | flops 16777216 | bytes 2097152 | tf_op jit(solution)/shard_map/pallas_call | solution.py:478
  (2 shorter events, 0.1 us)
Async XLA Ops:
  0.0 8.9 %collective-permute-start.1 = (bf16[2,8,32,128]{3,2,1,0:T(8,128)(2,1)}, bf16[2,8,32,128]{3,2,1,0:T(8,128)(2,1)S(1)}, u32[]{:S(2)}, u32[]{:S(2)}) collective-permute-start(bf16[2,8,32,128]{3,2,1,0:T(8,128)(2,1)} %own_far.1), channel_id=1, source_target_pairs={{32,0},{33,1},{34,2},{35,3},{36,4},{37,5},{38,6},{39,7},{40,8},{41... | collective-permute-start | bytes 393224 | tf_op jit(solution)/shard_map/ppermute | solution.py:405
  1.3 7.6 %collective-permute-start = (bf16[2,8,32,128]{3,2,1,0:T(8,128)(2,1)}, bf16[2,8,32,128]{3,2,1,0:T(8,128)(2,1)S(1)}, u32[]{:S(2)}, u32[]{:S(2)}) collective-permute-start(bf16[2,8,32,128]{3,2,1,0:T(8,128)(2,1)} %own_far.1), channel_id=1, source_target_pairs={{0,32},{1,33},{2,34},{3,35},{4,36},{5,37},{6,38},{7,39},{8,40},{9,... | collective-permute-start | bytes 393224 | tf_op jit(solution)/shard_map/ppermute | solution.py:405
  9.4 3.2 %collective-permute-start.2 = (bf16[12,32,128]{2,1,0:T(8,128)(2,1)S(1)}, bf16[12,32,128]{2,1,0:T(8,128)(2,1)S(1)}, u32[]{:S(2)}, u32[]{:S(2)}) collective-permute-start(bf16[12,32,128]{2,1,0:T(8,128)(2,1)S(1)} %get-tuple-element.36), channel_id=1, source_target_pairs={{0,1},{1,0},{2,3},{3,2},{4,5},{5,4},{6,7},{7,6},{8,9},{9,8},{10,11... | collective-permute-start | bytes 294920 | tf_op jit(solution)/shard_map/ppermute | solution.py:405
  34.6 10.2 %collective-permute-start.4 = (bf16[26,32,128]{2,1,0:T(8,128)(2,1)S(1)}, bf16[26,32,128]{2,1,0:T(8,128)(2,1)S(1)}, u32[]{:S(2)}, u32[]{:S(2)}) collective-permute-start(bf16[26,32,128]{2,1,0:T(8,128)(2,1)S(1)} %shard_map.68), channel_id=1, source_target_pairs={{1,2},{2,1},{3,4},{4,3},{5,6},{6,5},{7,8},{8,7},{9,10},{10,9},{11,... | collective-permute-start | bytes 638984 | tf_op jit(solution)/shard_map/ppermute | solution.py:405
  36.6 8.3 %collective-permute-start.5 = (bf16[4,32,128]{2,1,0:T(8,128)(2,1)S(1)}, bf16[4,32,128]{2,1,0:T(8,128)(2,1)S(1)}, u32[]{:S(2)}, u32[]{:S(2)}) collective-permute-start(bf16[4,32,128]{2,1,0:T(8,128)(2,1)S(1)} %get-tuple-element.41.level3), channel_id=1, source_target_pairs={{0,3},{2,5},{3,0},{4,7},{5,2},{6,9},{7,4},{8,11},{9,6},{10,13},{11... | collective-permute-start | bytes 98312 | tf_op jit(solution)/shard_map/ppermute | solution.py:405
  43.2 2.5 %collective-permute-start.3 = (bf16[32,128]{1,0:T(8,128)(2,1)S(1)}, bf16[32,128]{1,0:T(8,128)(2,1)S(1)}, u32[]{:S(2)}, u32[]{:S(2)}) collective-permute-start(bf16[32,128]{1,0:T(8,128)(2,1)S(1)} %get-tuple-element.37), channel_id=1, source_target_pairs={{0,0},{1,1},{2,2},{3,3},{4,4},{5,5},{6,6},{7,7},{8,8},{9,9},{10,10... | collective-permute-start | bytes 24584 | tf_op jit(solution)/shard_map/ppermute | solution.py:405

commit v4 on v3

--- a/solution.py
+++ b/solution.py
@@ -256,8 +256,8 @@
 
 def third_kernel(
     own, above, below, mine, packed, rim, gathered, level2, level3,
-    side, third, w0, w1, w2, w3, table,
-    near_sum, far0, far1, far2, far3, tag,
+    side, third, far_out, w0, w1, w2, w3, table,
+    near_sum, far0, far1, far2, far3, copies,
     near, window0, padded1, window1, padded2, window2, window3,
 ):
     row, _, _, core = places()
@@ -318,12 +318,8 @@
         window3[r, 1] = level3[r]
         window3[r, 2 - 2 * core] = third[r]
     far3[...] = dot(lanes([window3[r, k] for r in range(4) for k in range(3)]), w3[...])
-    tag[...] = jnp.zeros_like(tag)
-
-
-def copies_kernel(block, tag, out):
     for peer in range(16):
-        out[peer] = block[...]
+        copies[peer] = far_out[...]
 
 
 def fourth_kernel(
@@ -337,7 +333,7 @@
     padded4[pl.ds(0, 2)] = blank
     padded4[pl.ds(18, 2)] = blank
     for c in range(16):
-        padded4[c + 2] = top[(chip - c + 16) % 16]
+        padded4[c + 2] = top[c]
     by_col = jnp.concatenate([up[4, 0], up[4, 2], up[4, 1], up[4, 3]], axis=0)
     all4 = padded4[pl.ds(2, 16)].reshape(8, 2, PROBES, 128)
     nodes5 = dot(lanes([all4[:, 0], all4[:, 1]]).reshape(-1, 256), by_col)
@@ -453,14 +449,13 @@
     chips = size_y // 2
     side = move(side_out, lambda a, b: (a, b + across(b % 2)))
     third = move(level3, lambda a, b: (a, b + 3 - 6 * (b % 2)))
-    top = move(far_out, lambda a, b: (a, 2 * ((b // 2 + a) % chips) + b % 2))
-
-    near_sum, far0, far1, far2, far3, tag = call(
+
+    near_sum, far0, far1, far2, far3, copies = call(
         third_kernel,
         [
             array((2, 8) + block, F32), array((4 * PROBES, 256), F32),
             array((2 * PROBES, 128), F32), array((PROBES, 128), F32), array((PROBES, RANK), F32),
-            array((8, 128), F32),
+            array((16,) + block),
         ],
         scratch=[
             pltpu.VMEM(lead + block, BF)
@@ -469,11 +464,11 @@
         flops=1,
         read=1,
     )(
-        own, above, below, mine, packed, rim, gathered, level2, level3, side, third,
+        own, above, below, mine, packed, rim, gathered, level2, level3, side, third, far_out,
         w0, w1, w2, w3, table,
     )
-    copies = call(copies_kernel, array((16,) + block))(top, tag)
-    top = lax.all_to_all(copies, "gx", 0, 0)
+    columns = [[2 * chip + core for chip in range(chips)] for core in (0, 1)]
+    top = lax.all_to_all(copies, "gy", 0, 0, axis_index_groups=columns)
 
     return call(
         fourth_kernel,

time: 70.4 us -> 76.5 us (1.087)
  the two profiles are of different devices: /device:TPU:96 before, /device:TPU:1 now
where the time goes in v4:
time: 76.5 us; the launch traced here: 76.2 us
  blocking collectives  44.1 us (58%)
  starting transfers between devices  20.5 us (27%)
  Pallas kernels  7.78 us (10%)
  waiting for transfers between devices  3.76 us (5%)
    all_to_all x1, blocking collectives, shards(): top = lax.all_to_all(copies, 'gy', 0, 0, axis_index_groups=columns)  29.7 us
    ppermute x5, starting transfers between devices, move(): return lax.ppermute(value, both, route(rule, size_x, size_y))  20.5 us
    all_to_all x1, blocking collectives, shards(): gathered = lax.all_to_all(sent, 'gx', 0, 0)  14.4 us
    ppermute x5, waiting for transfers between devices, move(): return lax.ppermute(value, both, route(rule, size_x, size_y))  3.76 us
    pallas_call x1, Pallas kernels, shards(): call(prepare_kernel, [array((36 * RANK, 256)), array((36 * RANK, 128)), a...  3.05 us
    pallas_call x1, Pallas kernels, shards(): call(fourth_kernel, array(probes.shape), scratch=[pltpu.VMEM((20,) + bloc...  2.51 us
  transfers between devices with their start and end apart: 5, of which 2 were waited for; matrix products, arithmetic and copies ran while one was open for 0% of the time, Pallas kernels for 4%

profile of v4, /device:TPU:1, one launch (start us, length us, event | category | flops | bytes accessed | tf_op | source)
XLA Modules:
  0.0 76.2 jit_solution(11810355184709066591)
XLA Ops:
  0.0 1.3 %collective-permute-start.1 = (bf16[2,8,32,128]{3,2,1,0:T(8,128)(2,1)}, bf16[2,8,32,128]{3,2,1,0:T(8,128)(2,1)S(1)}, u32[]{:S(2)}, u32[]{:S(2)}) collective-permute-start(bf16[2,8,32,128]{3,2,1,0:T(8,128)(2,1)} %own_far.1), channel_id=1, source_target_pairs={{32,0},{33,1},{34,2},{35,3},{36,4},{37,5},{38,6},{39,7},{40,8},{41... | collective-permute-start | bytes 393224 | tf_op jit(solution)/shard_map/ppermute | solution.py:401
  1.3 4.6 %collective-permute-start = (bf16[2,8,32,128]{3,2,1,0:T(8,128)(2,1)}, bf16[2,8,32,128]{3,2,1,0:T(8,128)(2,1)S(1)}, u32[]{:S(2)}, u32[]{:S(2)}) collective-permute-start(bf16[2,8,32,128]{3,2,1,0:T(8,128)(2,1)} %own_far.1), channel_id=1, source_target_pairs={{0,32},{1,33},{2,34},{3,35},{4,36},{5,37},{6,38},{7,39},{8,40},{9,... | collective-permute-start | bytes 393224 | tf_op jit(solution)/shard_map/ppermute | solution.py:401
  5.9 3.1 %shard_map.64 = (bf16[2304,256]{1,0:T(8,128)(2,1)S(1)}, bf16[2304,128]{1,0:T(8,128)(2,1)S(1)}, bf16[2304,128]{1,0:T(8,128)(2,1)S(1)}, bf16[1536,64]{1,0:T(8,128)...) custom-call(s32[8,4,27]{2,1,0:T(4,128)} %ids_far.1, ...), custom_call_target="tpu_custom_call" | custom-call | flops 16777216 | bytes 2097152 | tf_op jit(solution)/shard_map/pallas_call | solution.py:408
  8.9 0.0 collective-permute-done.1.below
  8.9 0.0 collective-permute-done.above
  9.0 0.4 shard_map.65
  9.4 8.8 %collective-permute-start.2 = (bf16[12,32,128]{2,1,0:T(8,128)(2,1)S(1)}, bf16[12,32,128]{2,1,0:T(8,128)(2,1)S(1)}, u32[]{:S(2)}, u32[]{:S(2)}) collective-permute-start(bf16[12,32,128]{2,1,0:T(8,128)(2,1)S(1)} %get-tuple-element.36), channel_id=1, source_target_pairs={{0,1},{1,0},{2,3},{3,2},{4,5},{5,4},{6,7},{7,6},{8,9},{9,8},{10,11... | collective-permute-start | bytes 294920 | tf_op jit(solution)/shard_map/ppermute | solution.py:401
  18.2 0.9 %collective-permute-done.2.packed = bf16[12,32,128]{2,1,0:T(8,128)(2,1)S(1)} collective-permute-done((bf16[12,32,128]{2,1,0:T(8,128)(2,1)S(1)}, bf16[12,32,128]{2,1,0:T(8,128)(2,1)S(1)}, u32[]{:S(2)}, u32[]{:S(2)}) %collective-permute-start.2) | collective-permute-done | bytes 98336 | tf_op jit(solution)/shard_map/ppermute | solution.py:401
  19.1 0.1 shard_map.66
  19.2 14.4 %all_to_all.10.gathered = bf16[16,4,32,128]{3,2,1,0:T(8,128)(2,1)S(1)} all-to-all(bf16[16,4,32,128]{3,2,1,0:T(8,128)(2,1)S(1)} %shard_map.66), channel_id=1, replica_groups=mesh['gx'=16,'gy'=32] {'gx'}, dimensions={0} | all-to-all | bytes 1048576 | tf_op jit(solution)/shard_map/all_to_all | solution.py:436
  33.5 0.8 %shard_map.67 = (bf16[32,128]{1,0:T(8,128)(2,1)S(1)}, bf16[8,2,32,128]{3,2,1,0:T(8,128)(2,1)S(1)}, bf16[4,32,128]{2,1,0:T(8,128)(2,1)S(1)}) custom-call(bf16[16,4,32,128]{3,2,1,0:T(8,128)(2,1)S(1)} %all_to_all.10.gathered, bf16[7,4,64,64]{3,2,1,0:T(8,128)(2,1)S(1)} %get-tuple-element.34.up), custom_call_target="tpu_custom_call" | custom-call | flops 16777216 | bytes 2097152 | tf_op jit(solution)/shard_map/pallas_call | solution.py:438
  34.4 5.2 %collective-permute-start.3 = (bf16[26,32,128]{2,1,0:T(8,128)(2,1)S(1)}, bf16[26,32,128]{2,1,0:T(8,128)(2,1)S(1)}, u32[]{:S(2)}, u32[]{:S(2)}) collective-permute-start(bf16[26,32,128]{2,1,0:T(8,128)(2,1)S(1)} %shard_map.68), channel_id=1, source_target_pairs={{1,2},{2,1},{3,4},{4,3},{5,6},{6,5},{7,8},{8,7},{9,10},{10,9},{11,... | collective-permute-start | bytes 638984 | tf_op jit(solution)/shard_map/ppermute | solution.py:401
  39.6 0.7 collective-permute-start.4
  40.2 0.0 collective-permute-done.4.third
  40.2 2.8 %collective-permute-done.3.side = bf16[26,32,128]{2,1,0:T(8,128)(2,1)S(1)} collective-permute-done((bf16[26,32,128]{2,1,0:T(8,128)(2,1)S(1)}, bf16[26,32,128]{2,1,0:T(8,128)(2,1)S(1)}, u32[]{:S(2)}, u32[]{:S(2)}) %collective-permute-start.3) | collective-permute-done | bytes 213024 | tf_op jit(solution)/shard_map/ppermute | solution.py:401
  43.1 0.9 %shard_map.69 = (f32[2,8,32,128]{3,2,1,0:T(8,128)S(1)}, f32[128,256]{1,0:T(8,128)S(1)}, f32[64,128]{1,0:T(8,128)S(1)}, f32[32,128]{1,0:T(8,128)S(1)}, f32[32,64]...) custom-call(bf16[2,8,32,128]{3,2,1,0:T(8,128)(2,1)S(1)} %get-tuple-element.32.own, ...), custom_call_target="tpu_custom_call" | custom-call | flops 1 | bytes 1 | tf_op jit(solution)/shard_map/pallas_call | solution.py:453
  44.0 29.7 %all_to_all.11.top = bf16[16,32,128]{2,1,0:T(8,128)(2,1)S(1)} all-to-all(bf16[16,32,128]{2,1,0:T(8,128)(2,1)S(1)} %get-tuple-element.47), channel_id=1, replica_groups={{0,2,4,6,8,10,12,14,16,18,20,22,24,26,28,30},{1,3,5,7,9,11,13,15,17,19,..., dimensions={0} | all-to-all | bytes 262144 | tf_op jit(solution)/shard_map/all_to_all | solution.py:471
  73.7 2.5 %shard_map.70 = bf16[2,8,32,128]{3,2,1,0:T(8,128)(2,1)} custom-call(bf16[16,32,128]{2,1,0:T(8,128)(2,1)S(1)} %all_to_all.11.top, f32[2,8,32,128]{3,2,1,0:T(8,128)S(1)} %get-tuple-element.48.near_sum, f32[128,256]{1,0:T(8,128)S(1)} %get-tuple-element.49.far0, f32[64,128]{1,0:T(8,128)S(1)} %get-tuple-element.50.far1, f32[32,128]{1,0:T(8,128)S(1)} %get-tuple-element.51.far2, ...), custom_call_target="tpu_custom_call" | custom-call | flops 16777216 | bytes 2097152 | tf_op jit(solution)/shard_map/pallas_call | solution.py:473
  (1 shorter events, 0.0 us)
Async XLA Ops:
  0.0 8.9 %collective-permute-start.1 = (bf16[2,8,32,128]{3,2,1,0:T(8,128)(2,1)}, bf16[2,8,32,128]{3,2,1,0:T(8,128)(2,1)S(1)}, u32[]{:S(2)}, u32[]{:S(2)}) collective-permute-start(bf16[2,8,32,128]{3,2,1,0:T(8,128)(2,1)} %own_far.1), channel_id=1, source_target_pairs={{32,0},{33,1},{34,2},{35,3},{36,4},{37,5},{38,6},{39,7},{40,8},{41... | collective-permute-start | bytes 393224 | tf_op jit(solution)/shard_map/ppermute | solution.py:401
  1.3 7.7 %collective-permute-start = (bf16[2,8,32,128]{3,2,1,0:T(8,128)(2,1)}, bf16[2,8,32,128]{3,2,1,0:T(8,128)(2,1)S(1)}, u32[]{:S(2)}, u32[]{:S(2)}) collective-permute-start(bf16[2,8,32,128]{3,2,1,0:T(8,128)(2,1)} %own_far.1), channel_id=1, source_target_pairs={{0,32},{1,33},{2,34},{3,35},{4,36},{5,37},{6,38},{7,39},{8,40},{9,... | collective-permute-start | bytes 393224 | tf_op jit(solution)/shard_map/ppermute | solution.py:401
  9.4 9.7 %collective-permute-start.2 = (bf16[12,32,128]{2,1,0:T(8,128)(2,1)S(1)}, bf16[12,32,128]{2,1,0:T(8,128)(2,1)S(1)}, u32[]{:S(2)}, u32[]{:S(2)}) collective-permute-start(bf16[12,32,128]{2,1,0:T(8,128)(2,1)S(1)} %get-tuple-element.36), channel_id=1, source_target_pairs={{0,1},{1,0},{2,3},{3,2},{4,5},{5,4},{6,7},{7,6},{8,9},{9,8},{10,11... | collective-permute-start | bytes 294920 | tf_op jit(solution)/shard_map/ppermute | solution.py:401
  34.4 8.7 %collective-permute-start.3 = (bf16[26,32,128]{2,1,0:T(8,128)(2,1)S(1)}, bf16[26,32,128]{2,1,0:T(8,128)(2,1)S(1)}, u32[]{:S(2)}, u32[]{:S(2)}) collective-permute-start(bf16[26,32,128]{2,1,0:T(8,128)(2,1)S(1)} %shard_map.68), channel_id=1, source_target_pairs={{1,2},{2,1},{3,4},{4,3},{5,6},{6,5},{7,8},{8,7},{9,10},{10,9},{11,... | collective-permute-start | bytes 638984 | tf_op jit(solution)/shard_map/ppermute | solution.py:401
  39.6 0.7 collective-permute-start.4

commit v5 on v4

--- a/solution.py
+++ b/solution.py
@@ -256,7 +256,7 @@
 
 def third_kernel(
     own, above, below, mine, packed, rim, gathered, level2, level3,
-    side, third, far_out, w0, w1, w2, w3, table,
+    side, third, arrived, w0, w1, w2, w3, table,
     near_sum, far0, far1, far2, far3, copies,
     near, window0, padded1, window1, padded2, window2, window3,
 ):
@@ -319,7 +319,11 @@
         window3[r, 2 - 2 * core] = third[r]
     far3[...] = dot(lanes([window3[r, k] for r in range(4) for k in range(3)]), w3[...])
     for peer in range(16):
-        copies[peer] = far_out[...]
+        copies[peer] = arrived[...]
+
+
+def arrival_kernel(block, out):
+    out[...] = block[...]
 
 
 def fourth_kernel(
@@ -333,7 +337,7 @@
     padded4[pl.ds(0, 2)] = blank
     padded4[pl.ds(18, 2)] = blank
     for c in range(16):
-        padded4[c + 2] = top[c]
+        padded4[c + 2] = top[(chip - c + 16) % 16]
     by_col = jnp.concatenate([up[4, 0], up[4, 2], up[4, 1], up[4, 3]], axis=0)
     all4 = padded4[pl.ds(2, 16)].reshape(8, 2, PROBES, 128)
     nodes5 = dot(lanes([all4[:, 0], all4[:, 1]]).reshape(-1, 256), by_col)
@@ -449,7 +453,9 @@
     chips = size_y // 2
     side = move(side_out, lambda a, b: (a, b + across(b % 2)))
     third = move(level3, lambda a, b: (a, b + 3 - 6 * (b % 2)))
-
+    top = move(far_out, lambda a, b: (a, 2 * ((b // 2 + a) % chips) + b % 2))
+
+    arrived = call(arrival_kernel, array(block), flops=1 << 36)(top)
     near_sum, far0, far1, far2, far3, copies = call(
         third_kernel,
         [
@@ -464,11 +470,10 @@
         flops=1,
         read=1,
     )(
-        own, above, below, mine, packed, rim, gathered, level2, level3, side, third, far_out,
+        own, above, below, mine, packed, rim, gathered, level2, level3, side, third, arrived,
         w0, w1, w2, w3, table,
     )
-    columns = [[2 * chip + core for chip in range(chips)] for core in (0, 1)]
-    top = lax.all_to_all(copies, "gy", 0, 0, axis_index_groups=columns)
+    top = lax.all_to_all(copies, "gx", 0, 0)
 
     return call(
         fourth_kernel,

time: 76.5 us -> 72.9 us (0.953)
  blocking collectives: 44.1 us -> 36.9 us
  starting transfers between devices: 20.5 us -> 22.6 us
    all_to_all x1, blocking collectives: 29.7 us -> 22.5 us  [shards(): top = lax.all_to_all(copies, 'gx', 0, 0)]
    ppermute x5 -> x6, starting transfers between devices: 20.5 us -> 22.6 us  [move(): return lax.ppermute(value, both, route(rule, size_x, size_y))]
    ppermute x5 -> x6, waiting for transfers between devices: 3.76 us -> 4.42 us  [move(): return lax.ppermute(value, both, route(rule, size_x, size_y))]
  transfers between devices with their start and end apart: 5 -> 6, of which waited for: 2 -> 2; matrix products, arithmetic and copies ran while one was open for 0% -> 0% of each run, Pallas kernels for 4% -> 4%
where the time goes in v5:
time: 72.9 us; the launch traced here: 71.9 us
  blocking collectives  36.9 us (51%)
  starting transfers between devices  22.6 us (31%)
  Pallas kernels  7.8 us (11%)
  waiting for transfers between devices  4.42 us (6%)
    ppermute x6, starting transfers between devices, move(): return lax.ppermute(value, both, route(rule, size_x, size_y))  22.6 us
    all_to_all x1, blocking collectives, shards(): top = lax.all_to_all(copies, 'gx', 0, 0)  22.5 us
    all_to_all x1, blocking collectives, shards(): gathered = lax.all_to_all(sent, 'gx', 0, 0)  14.4 us
    ppermute x6, waiting for transfers between devices, move(): return lax.ppermute(value, both, route(rule, size_x, size_y))  4.42 us
    pallas_call x1, Pallas kernels, shards(): call(prepare_kernel, [array((36 * RANK, 256)), array((36 * RANK, 128)), a...  3.05 us
    pallas_call x1, Pallas kernels, shards(): call(fourth_kernel, array(probes.shape), scratch=[pltpu.VMEM((20,) + bloc...  2.52 us
  transfers between devices with their start and end apart: 6, of which 2 were waited for; matrix products, arithmetic and copies ran while one was open for 0% of the time, Pallas kernels for 4%

profile of v5, /device:TPU:1, one launch (start us, length us, event | category | flops | bytes accessed | tf_op | source)
XLA Modules:
  0.0 71.9 jit_solution(9544234910593843537)
XLA Ops:
  0.0 1.3 %collective-permute-start.1 = (bf16[2,8,32,128]{3,2,1,0:T(8,128)(2,1)}, bf16[2,8,32,128]{3,2,1,0:T(8,128)(2,1)S(1)}, u32[]{:S(2)}, u32[]{:S(2)}) collective-permute-start(bf16[2,8,32,128]{3,2,1,0:T(8,128)(2,1)} %own_far.1), channel_id=1, source_target_pairs={{32,0},{33,1},{34,2},{35,3},{36,4},{37,5},{38,6},{39,7},{40,8},{41... | collective-permute-start | bytes 393224 | tf_op jit(solution)/shard_map/ppermute | solution.py:405
  1.3 4.6 %collective-permute-start = (bf16[2,8,32,128]{3,2,1,0:T(8,128)(2,1)}, bf16[2,8,32,128]{3,2,1,0:T(8,128)(2,1)S(1)}, u32[]{:S(2)}, u32[]{:S(2)}) collective-permute-start(bf16[2,8,32,128]{3,2,1,0:T(8,128)(2,1)} %own_far.1), channel_id=1, source_target_pairs={{0,32},{1,33},{2,34},{3,35},{4,36},{5,37},{6,38},{7,39},{8,40},{9,... | collective-permute-start | bytes 393224 | tf_op jit(solution)/shard_map/ppermute | solution.py:405
  5.9 3.1 %shard_map.64 = (bf16[2304,256]{1,0:T(8,128)(2,1)S(1)}, bf16[2304,128]{1,0:T(8,128)(2,1)S(1)}, bf16[2304,128]{1,0:T(8,128)(2,1)S(1)}, bf16[1536,64]{1,0:T(8,128)...) custom-call(s32[8,4,27]{2,1,0:T(4,128)} %ids_far.1, ...), custom_call_target="tpu_custom_call" | custom-call | flops 16777216 | bytes 2097152 | tf_op jit(solution)/shard_map/pallas_call | solution.py:412
  8.9 0.0 collective-permute-done.1.below
  8.9 0.0 collective-permute-done.above
  9.0 0.4 shard_map.65
  9.4 8.8 %collective-permute-start.2 = (bf16[12,32,128]{2,1,0:T(8,128)(2,1)S(1)}, bf16[12,32,128]{2,1,0:T(8,128)(2,1)S(1)}, u32[]{:S(2)}, u32[]{:S(2)}) collective-permute-start(bf16[12,32,128]{2,1,0:T(8,128)(2,1)S(1)} %get-tuple-element.36), channel_id=1, source_target_pairs={{0,1},{1,0},{2,3},{3,2},{4,5},{5,4},{6,7},{7,6},{8,9},{9,8},{10,11... | collective-permute-start | bytes 294920 | tf_op jit(solution)/shard_map/ppermute | solution.py:405
  18.2 0.9 %collective-permute-done.2.packed = bf16[12,32,128]{2,1,0:T(8,128)(2,1)S(1)} collective-permute-done((bf16[12,32,128]{2,1,0:T(8,128)(2,1)S(1)}, bf16[12,32,128]{2,1,0:T(8,128)(2,1)S(1)}, u32[]{:S(2)}, u32[]{:S(2)}) %collective-permute-start.2) | collective-permute-done | bytes 98336 | tf_op jit(solution)/shard_map/ppermute | solution.py:405
  19.1 0.1 shard_map.66
  19.2 14.4 %all_to_all.10.gathered = bf16[16,4,32,128]{3,2,1,0:T(8,128)(2,1)S(1)} all-to-all(bf16[16,4,32,128]{3,2,1,0:T(8,128)(2,1)S(1)} %shard_map.66), channel_id=1, replica_groups=mesh['gx'=16,'gy'=32] {'gx'}, dimensions={0} | all-to-all | bytes 1048576 | tf_op jit(solution)/shard_map/all_to_all | solution.py:440
  33.5 0.8 %shard_map.67 = (bf16[32,128]{1,0:T(8,128)(2,1)S(1)}, bf16[8,2,32,128]{3,2,1,0:T(8,128)(2,1)S(1)}, bf16[4,32,128]{2,1,0:T(8,128)(2,1)S(1)}) custom-call(bf16[16,4,32,128]{3,2,1,0:T(8,128)(2,1)S(1)} %all_to_all.10.gathered, bf16[7,4,64,64]{3,2,1,0:T(8,128)(2,1)S(1)} %get-tuple-element.34.up), custom_call_target="tpu_custom_call" | custom-call | flops 16777216 | bytes 2097152 | tf_op jit(solution)/shard_map/pallas_call | solution.py:442
  34.3 0.7 collective-permute-start.5
  35.0 0.7 collective-permute-start.4
  35.7 6.7 %collective-permute-start.3 = (bf16[26,32,128]{2,1,0:T(8,128)(2,1)S(1)}, bf16[26,32,128]{2,1,0:T(8,128)(2,1)S(1)}, u32[]{:S(2)}, u32[]{:S(2)}) collective-permute-start(bf16[26,32,128]{2,1,0:T(8,128)(2,1)S(1)} %shard_map.68), channel_id=1, source_target_pairs={{1,2},{2,1},{3,4},{4,3},{5,6},{6,5},{7,8},{8,7},{9,10},{10,9},{11,... | collective-permute-start | bytes 638984 | tf_op jit(solution)/shard_map/ppermute | solution.py:405
  42.4 0.0 collective-permute-done.5.block
  42.4 0.0 collective-permute-done.4.third
  42.5 3.5 %collective-permute-done.3.side = bf16[26,32,128]{2,1,0:T(8,128)(2,1)S(1)} collective-permute-done((bf16[26,32,128]{2,1,0:T(8,128)(2,1)S(1)}, bf16[26,32,128]{2,1,0:T(8,128)(2,1)S(1)}, u32[]{:S(2)}, u32[]{:S(2)}) %collective-permute-start.3) | collective-permute-done | bytes 213024 | tf_op jit(solution)/shard_map/ppermute | solution.py:405
  45.9 0.9 %shard_map.70 = (f32[2,8,32,128]{3,2,1,0:T(8,128)S(1)}, f32[128,256]{1,0:T(8,128)S(1)}, f32[64,128]{1,0:T(8,128)S(1)}, f32[32,128]{1,0:T(8,128)S(1)}, f32[32,64]...) custom-call(bf16[2,8,32,128]{3,2,1,0:T(8,128)(2,1)S(1)} %get-tuple-element.32.own, ...), custom_call_target="tpu_custom_call" | custom-call | flops 1 | bytes 1 | tf_op jit(solution)/shard_map/pallas_call | solution.py:459
  46.8 22.5 %all_to_all.11.top = bf16[16,32,128]{2,1,0:T(8,128)(2,1)S(1)} all-to-all(bf16[16,32,128]{2,1,0:T(8,128)(2,1)S(1)} %get-tuple-element.47), channel_id=1, replica_groups=mesh['gx'=16,'gy'=32] {'gx'}, dimensions={0} | all-to-all | bytes 262144 | tf_op jit(solution)/shard_map/all_to_all | solution.py:476
  69.3 2.5 %shard_map.71 = bf16[2,8,32,128]{3,2,1,0:T(8,128)(2,1)} custom-call(bf16[16,32,128]{2,1,0:T(8,128)(2,1)S(1)} %all_to_all.11.top, f32[2,8,32,128]{3,2,1,0:T(8,128)S(1)} %get-tuple-element.48.near_sum, f32[128,256]{1,0:T(8,128)S(1)} %get-tuple-element.49.far0, f32[64,128]{1,0:T(8,128)S(1)} %get-tuple-element.50.far1, f32[32,128]{1,0:T(8,128)S(1)} %get-tuple-element.51.far2, ...), custom_call_target="tpu_custom_call" | custom-call | flops 16777216 | bytes 2097152 | tf_op jit(solution)/shard_map/pallas_call | solution.py:478
  (2 shorter events, 0.0 us)
Async XLA Ops:
  0.0 8.9 %collective-permute-start.1 = (bf16[2,8,32,128]{3,2,1,0:T(8,128)(2,1)}, bf16[2,8,32,128]{3,2,1,0:T(8,128)(2,1)S(1)}, u32[]{:S(2)}, u32[]{:S(2)}) collective-permute-start(bf16[2,8,32,128]{3,2,1,0:T(8,128)(2,1)} %own_far.1), channel_id=1, source_target_pairs={{32,0},{33,1},{34,2},{35,3},{36,4},{37,5},{38,6},{39,7},{40,8},{41... | collective-permute-start | bytes 393224 | tf_op jit(solution)/shard_map/ppermute | solution.py:405
  1.3 7.7 %collective-permute-start = (bf16[2,8,32,128]{3,2,1,0:T(8,128)(2,1)}, bf16[2,8,32,128]{3,2,1,0:T(8,128)(2,1)S(1)}, u32[]{:S(2)}, u32[]{:S(2)}) collective-permute-start(bf16[2,8,32,128]{3,2,1,0:T(8,128)(2,1)} %own_far.1), channel_id=1, source_target_pairs={{0,32},{1,33},{2,34},{3,35},{4,36},{5,37},{6,38},{7,39},{8,40},{9,... | collective-permute-start | bytes 393224 | tf_op jit(solution)/shard_map/ppermute | solution.py:405
  9.4 9.7 %collective-permute-start.2 = (bf16[12,32,128]{2,1,0:T(8,128)(2,1)S(1)}, bf16[12,32,128]{2,1,0:T(8,128)(2,1)S(1)}, u32[]{:S(2)}, u32[]{:S(2)}) collective-permute-start(bf16[12,32,128]{2,1,0:T(8,128)(2,1)S(1)} %get-tuple-element.36), channel_id=1, source_target_pairs={{0,1},{1,0},{2,3},{3,2},{4,5},{5,4},{6,7},{7,6},{8,9},{9,8},{10,11... | collective-permute-start | bytes 294920 | tf_op jit(solution)/shard_map/ppermute | solution.py:405
  34.3 8.1 %collective-permute-start.5 = (bf16[32,128]{1,0:T(8,128)(2,1)S(1)}, bf16[32,128]{1,0:T(8,128)(2,1)S(1)}, u32[]{:S(2)}, u32[]{:S(2)}) collective-permute-start(bf16[32,128]{1,0:T(8,128)(2,1)S(1)} %get-tuple-element.41), channel_id=1, source_target_pairs={{0,0},{1,1},{2,2},{3,3},{4,4},{5,5},{6,6},{7,7},{8,8},{9,9},{10,10... | collective-permute-start | bytes 24584 | tf_op jit(solution)/shard_map/ppermute | solution.py:405
  35.0 7.5 %collective-permute-start.4 = (bf16[4,32,128]{2,1,0:T(8,128)(2,1)S(1)}, bf16[4,32,128]{2,1,0:T(8,128)(2,1)S(1)}, u32[]{:S(2)}, u32[]{:S(2)}) collective-permute-start(bf16[4,32,128]{2,1,0:T(8,128)(2,1)S(1)} %get-tuple-element.40.level3), channel_id=1, source_target_pairs={{0,3},{2,5},{3,0},{4,7},{5,2},{6,9},{7,4},{8,11},{9,6},{10,13},{11... | collective-permute-start | bytes 98312 | tf_op jit(solution)/shard_map/ppermute | solution.py:405
  35.7 10.2 %collective-permute-start.3 = (bf16[26,32,128]{2,1,0:T(8,128)(2,1)S(1)}, bf16[26,32,128]{2,1,0:T(8,128)(2,1)S(1)}, u32[]{:S(2)}, u32[]{:S(2)}) collective-permute-start(bf16[26,32,128]{2,1,0:T(8,128)(2,1)S(1)} %shard_map.68), channel_id=1, source_target_pairs={{1,2},{2,1},{3,4},{4,3},{5,6},{6,5},{7,8},{8,7},{9,10},{10,9},{11,... | collective-permute-start | bytes 638984 | tf_op jit(solution)/shard_map/ppermute | solution.py:405

commit v6 on v3

--- a/solution.py
+++ b/solution.py
@@ -39,30 +39,21 @@
     return row, col, col // 2, col % 2
 
 
-def prepare_kernel(
-    ids_far, coupling_far, up_far, down_far, basis_far, own_far,
-    w0, w1, w2, w3, w4, w5, table, wide, up, down0, down1, down2, down3, own,
-    ids, coupling, down, basis, ids_sem, level_sems, sems,
+def build_weights(
+    ids_far, coupling_far, down_far, w0, w1, w2, w3, w4, w5, table, down0, down1, down2, down3,
+    ids, coupling, down, sems,
 ):
     row, col, _, _ = places()
-    first = pltpu.make_async_copy(ids_far, ids, ids_sem)
+    first = pltpu.make_async_copy(ids_far, ids, sems.at[8])
     first.start()
     levels = []
     for level in range(8):
         levels.append(
-            pltpu.make_async_copy(coupling_far.at[level], coupling.at[level], level_sems.at[level])
+            pltpu.make_async_copy(coupling_far.at[level], coupling.at[level], sems.at[level])
         )
-    levels[0].start()
-    small = [
-        pltpu.make_async_copy(source, target, sems.at[at])
-        for at, (source, target) in enumerate(
-            ((basis_far, basis), (own_far, own), (up_far, up), (down_far, down))
-        )
-    ]
-    for copy in small:
-        copy.start()
-    for copy in levels[1:]:
-        copy.start()
+        levels[-1].start()
+    other = pltpu.make_async_copy(down_far, down, sems.at[9])
+    other.start()
 
     size = LEAF_ROWS * LEAF_COLS
     theirs = lax.broadcasted_iota(jnp.int32, (size, size), 0)
@@ -132,10 +123,7 @@
                 level, jnp.int32(0), f, jnp.int32(2), wc
             )
 
-    for copy in small:
-        copy.wait()
-    blank = jnp.zeros_like(basis)
-    wide[...] = jnp.concatenate([lanes([basis[...], blank]), lanes([blank, basis[...]])], axis=0)
+    other.wait()
     all0 = lanes([down[0, k] for k in range(4)])
     none0 = jnp.zeros_like(all0)
     down0[...] = jnp.concatenate([lanes([all0, none0]), lanes([none0, all0])], axis=0)
@@ -150,6 +138,48 @@
         down3[level - 3] = down[level, 2 * e + f]
 
 
+EARLY_PLANES = 7
+
+
+def start_kernel(
+    ids_far, coupling_far, down_far, up_far, basis_far, own_far,
+    wide, up, own, mine, low,
+    w0, w1, w2, w3, w4, w5, table, down0, down1, down2, down3,
+    ids, coupling, down, basis, sems, small_sems,
+):
+    _, _, chip, _ = places()
+    small = [
+        pltpu.make_async_copy(source, target, small_sems.at[at])
+        for at, (source, target) in enumerate(((basis_far, basis), (own_far, own), (up_far, up)))
+    ]
+    for copy in small:
+        copy.start()
+    for copy in small:
+        copy.wait()
+    blank = jnp.zeros_like(basis)
+    wide[...] = jnp.concatenate([lanes([basis[...], blank]), lanes([blank, basis[...]])], axis=0)
+    coeffs = leaf_coeffs(own[...], wide[...])
+    mine[...] = coeffs
+    low[...] = to_pairs(raise_pairs(coeffs, up[0].reshape(4 * RANK, RANK))[0])
+
+    @pl.when(chip < EARLY_PLANES)
+    def _():
+        build_weights(
+            ids_far, coupling_far, down_far,
+            w0, w1, w2, w3, w4, w5, table, down0, down1, down2, down3,
+            ids, coupling, down, sems,
+        )
+
+
+def later_kernel(ids_far, coupling_far, down_far, tag, *refs):
+    _, _, chip, _ = places()
+    weights, scratch = refs[11:22], refs[22:]
+
+    @pl.when(chip >= EARLY_PLANES)
+    def _():
+        build_weights(ids_far, coupling_far, down_far, *weights, *scratch)
+
+
 def array(shape, kind=BF):
     return jax.ShapeDtypeStruct(shape, kind)
 
@@ -188,57 +218,77 @@
     return dot(joined, transfer).astype(BF).reshape(rows // 2, count, PROBES, RANK)
 
 
-def first_kernel(own, above, below, wide, up, pack, low, mine, rim):
-    _, _, _, core = places()
-    coeffs = leaf_coeffs(own[...], wide[...])
-    pairs = to_pairs(raise_pairs(coeffs, up[0].reshape(4 * RANK, RANK))[0])
-    mine[...] = coeffs
+def rim_kernel(above, below, wide, low, rim, sent):
     rim[pl.ds(0, 2)] = leaf_coeffs(above[...], wide[...])
     rim[pl.ds(2, 2)] = leaf_coeffs(below[...], wide[...])
-    low[...] = pairs
-
+    for peer in range(16):
+        sent[peer] = low[...]
+
+
+def strip_kernel(gathered, own, mine, above, below, rim, up, pack, level2, level3, padded1, padded2):
+    row, _, _, core = places()
+    pairs2 = to_pairs(raise_pairs(gathered[...], up[1].reshape(4 * RANK, RANK)))
+    nodes3 = raise_pairs(pairs2, up[2].reshape(4 * RANK, RANK))[:, 0]
+    level2[...] = pairs2[:, 0]
+    level3[...] = nodes3
+    nothing = jnp.zeros((2, PROBES, 128), BF)
+    padded1[pl.ds(0, 2)] = nothing
+    padded1[pl.ds(18, 2)] = nothing
+    padded2[pl.ds(0, 2)] = nothing
+    padded2[pl.ds(2, 8)] = pairs2[:, 0]
+    padded2[pl.ds(10, 2)] = nothing
+    for r in range(16):
+        padded1[r + 2] = gathered[r, 1 - core]
     edge_pair = 3 - 3 * core
     edge_col = 7 - 7 * core
-    pack[pl.ds(0, 2)] = pairs
-    pack[2] = mine[0, edge_pair]
-    pack[3] = mine[1, edge_pair]
-    pack[4] = own[0, edge_col]
-    pack[5] = own[1, edge_col]
-    pack[6] = above[1, edge_col]
-    pack[7] = below[0, edge_col]
+    pack[pl.ds(0, 6)] = padded1[pl.ds(2 * (row // 2), 6)]
+    pack[pl.ds(6, 6)] = padded2[pl.ds(2 * (row // 4), 6)]
+    pack[12] = lanes([nodes3[0], nodes3[1]])
+    pack[13] = lanes([nodes3[2], nodes3[3]])
+    pack[14] = mine[0, edge_pair]
+    pack[15] = mine[1, edge_pair]
+    pack[16] = own[0, edge_col]
+    pack[17] = own[1, edge_col]
+    pack[18] = above[1, edge_col]
+    pack[19] = below[0, edge_col]
     for r in range(4):
-        pack[8 + r] = rim[r, edge_pair]
-
-
-def strip_kernel(low, packed, sent):
-    _, _, _, core = places()
-    for peer in range(16):
-        sent[peer, pl.ds(2 * core, 2)] = low[...]
-        sent[peer, pl.ds(2 - 2 * core, 2)] = packed[pl.ds(0, 2)]
-
-
-def second_kernel(gathered, up, far_out, level2, level3):
-    pairs2 = to_pairs(raise_pairs(gathered[...], up[1].reshape(4 * RANK, RANK)))
-    pairs3 = to_pairs(raise_pairs(pairs2, up[2].reshape(4 * RANK, RANK)))[:, 0]
+        pack[20 + r] = rim[r, edge_pair]
+
+
+def second_kernel(
+    packed, gathered, level2, level3_own, own, mine, above, below, rim, up,
+    far_out, side_out, level3, padded1, padded2,
+):
+    row, _, _, core = places()
+    theirs = []
+    for at in (12, 13):
+        block = packed[at]
+        theirs += [block[:, :RANK], block[:, RANK:]]
+
+    @pl.when(core == 0)
+    def _():
+        for r in range(4):
+            level3[r] = lanes([level3_own[r], theirs[r]])
+
+    @pl.when(core == 1)
+    def _():
+        for r in range(4):
+            level3[r] = lanes([theirs[r], level3_own[r]])
+
+    pairs3 = level3[...]
     nodes4 = raise_pairs(pairs3[:, None], up[3].reshape(4 * RANK, RANK))
     far_out[...] = lanes([nodes4[0, 0], nodes4[1, 0]])
-    level2[...] = pairs2
-    level3[...] = pairs3
-
-
-def side_kernel(gathered, own, mine, above, below, rim, level2, level3, side_out, padded1, padded2):
-    row, _, _, core = places()
+
     edge_pair = 3 * core
     edge_col = 7 * core
     nothing = jnp.zeros((2, PROBES, 128), BF)
     padded1[pl.ds(0, 2)] = nothing
     padded1[pl.ds(18, 2)] = nothing
     padded2[pl.ds(0, 2)] = nothing
+    padded2[pl.ds(2, 8)] = level2[...]
     padded2[pl.ds(10, 2)] = nothing
     for r in range(16):
-        padded1[r + 2] = gathered[r, edge_pair]
-    for r in range(8):
-        padded2[r + 2] = level2[r, core]
+        padded1[r + 2] = gathered[r, core]
     side_out[0] = above[1, edge_col]
     side_out[1] = own[0, edge_col]
     side_out[2] = own[1, edge_col]
@@ -251,7 +301,7 @@
     side_out[9] = rim[3, edge_pair]
     side_out[pl.ds(10, 6)] = padded1[pl.ds(2 * (row // 2), 6)]
     side_out[pl.ds(16, 6)] = padded2[pl.ds(2 * (row // 4), 6)]
-    side_out[pl.ds(22, 4)] = level3[...]
+    side_out[pl.ds(22, 4)] = pairs3
 
 
 def third_kernel(
@@ -268,9 +318,9 @@
     for w in range(6):
         window0[w, 5 * core] = side[4 + w]
     for r in range(2):
-        window0[r, 5 - 5 * core] = packed[8 + r]
-        window0[2 + r, 5 - 5 * core] = packed[2 + r]
-        window0[4 + r, 5 - 5 * core] = packed[10 + r]
+        window0[r, 5 - 5 * core] = packed[20 + r]
+        window0[2 + r, 5 - 5 * core] = packed[14 + r]
+        window0[4 + r, 5 - 5 * core] = packed[22 + r]
     far0[...] = dot(
         lanes([window0[w, pl.ds(k, 4)].reshape(-1, 128) for w in range(6) for k in range(3)]),
         w0[...],
@@ -282,34 +332,34 @@
     near[3, pl.ds(1, 8)] = below[0]
     for r in range(4):
         near[r, 9 * core] = side[r]
-    near[0, 9 - 9 * core] = packed[6]
-    near[1, 9 - 9 * core] = packed[4]
-    near[2, 9 - 9 * core] = packed[5]
-    near[3, 9 - 9 * core] = packed[7]
+    near[0, 9 - 9 * core] = packed[18]
+    near[1, 9 - 9 * core] = packed[16]
+    near[2, 9 - 9 * core] = packed[17]
+    near[3, 9 - 9 * core] = packed[19]
     for e in (0, 1):
         joined = lanes([near[e + u, pl.ds(v, 8)].reshape(-1, 128) for u in range(3) for v in range(3)])
         near_sum[e] = dot(joined, table[...]).reshape(8, PROBES, 128)
 
-    empty1 = jnp.zeros((2, 4, PROBES, 128), BF)
+    empty1 = jnp.zeros((2, 2, PROBES, 128), BF)
     padded1[pl.ds(0, 2)] = empty1
     padded1[pl.ds(2, 16)] = gathered[...]
     padded1[pl.ds(18, 2)] = empty1
+    window1[:, pl.ds(1, 2)] = padded1[pl.ds(2 * (row // 2), 6)]
     for w in range(6):
-        for k in range(3):
-            window1[w, k + 1 - core] = padded1[2 * (row // 2) + w, k + core]
+        window1[w, 3 - 3 * core] = packed[w]
         window1[w, 3 * core] = side[10 + w]
     far1[...] = dot(
         lanes([window1[w, pl.ds(k, 2)].reshape(-1, 128) for w in range(6) for k in range(3)]),
         w1[...],
     )
 
-    empty2 = jnp.zeros((2, 2, PROBES, 128), BF)
+    empty2 = jnp.zeros((2, PROBES, 128), BF)
     padded2[pl.ds(0, 2)] = empty2
     padded2[pl.ds(2, 8)] = level2[...]
     padded2[pl.ds(10, 2)] = empty2
+    window2[:, 1] = padded2[pl.ds(2 * (row // 4), 6)]
     for w in range(6):
-        for k in range(2):
-            window2[w, k + 1 - core] = padded2[2 * (row // 4) + w, k]
+        window2[w, 2 - 2 * core] = packed[6 + w]
         window2[w, 2 * core] = side[16 + w]
     far2[...] = dot(lanes([window2[w, k] for w in range(6) for k in range(3)]), w2[...])
 
@@ -408,52 +458,67 @@
     below = move(probes, lambda a, b: (a - 1, b))
 
     hbm = pl.BlockSpec(memory_space=pltpu.MemorySpace.HBM)
+    whole = pl.BlockSpec(memory_space=pltpu.VMEM)
     block = (PROBES, 128)
-    w0, w1, w2, w3, w4, w5, table, wide, up, down0, down1, down2, down3, own = call(
-        prepare_kernel,
+    far_inputs = [
+        pltpu.with_memory_space_constraint(value, pltpu.MemorySpace.HBM)
+        for value in (far_ids, coupling, down_transfer, up_transfer, leaf_basis.T, probes)
+    ]
+    weight_shapes = [
+        array((36 * RANK, 256)), array((36 * RANK, 128)), array((36 * RANK, 128)),
+        array((24 * RANK, RANK)), array((12 * RANK, RANK)), array((3, 6 * RANK, RANK)),
+        array((9 * 128, 128)), array((128, 512)), array((128, 256)), array((RANK, 128)),
+        array((4, RANK, RANK)),
+    ]
+    build_scratch = [
+        pltpu.SMEM(far_ids.shape, jnp.int32), pltpu.VMEM(coupling.shape, BF),
+        pltpu.VMEM(down_transfer.shape, BF),
+    ]
+    wide, up, own, mine, low, *weights = call(
+        start_kernel,
         [
-            array((36 * RANK, 256)), array((36 * RANK, 128)), array((36 * RANK, 128)),
-            array((24 * RANK, RANK)), array((12 * RANK, RANK)), array((3, 6 * RANK, RANK)),
-            array((9 * 128, 128)), array((128, 256)), array(up_transfer.shape),
-            array((128, 512)), array((128, 256)), array((RANK, 128)), array((4, RANK, RANK)),
-            array(probes.shape),
+            array((128, 256)), array(up_transfer.shape), array(probes.shape),
+            array((2, 4) + block), array((2,) + block),
+        ]
+        + weight_shapes,
+        in_specs=[hbm] * 6,
+        scratch=build_scratch
+        + [
+            pltpu.VMEM(leaf_basis.shape[::-1], BF), pltpu.SemaphoreType.DMA((10,)),
+            pltpu.SemaphoreType.DMA((3,)),
         ],
-        in_specs=[hbm] * 6,
-        scratch=[
-            pltpu.SMEM(far_ids.shape, jnp.int32), pltpu.VMEM(coupling.shape, BF),
-            pltpu.VMEM(down_transfer.shape, BF), pltpu.VMEM(leaf_basis.shape[::-1], BF),
-            pltpu.SemaphoreType.DMA, pltpu.SemaphoreType.DMA((8,)), pltpu.SemaphoreType.DMA((4,)),
-        ],
-    )(
-        *[
-            pltpu.with_memory_space_constraint(value, pltpu.MemorySpace.HBM)
-            for value in (far_ids, coupling, up_transfer, down_transfer, leaf_basis.T, probes)
-        ]
-    )
-
-    pack, low, mine, rim = call(
-        first_kernel,
-        [array((12,) + block), array((2,) + block), array((2, 4) + block), array((4, 4) + block)],
-    )(own, above, below, wide, up)
+    )(*far_inputs)
+
+    rim, sent = call(rim_kernel, [array((4, 4) + block), array((16, 2) + block)])(
+        above, below, wide, low
+    )
+    gathered = lax.all_to_all(sent, "gx", 0, 0)
+
+    pack, level2, level3_own = call(
+        strip_kernel,
+        [array((24,) + block), array((8,) + block), array((4, PROBES, RANK))],
+        scratch=[pltpu.VMEM((20,) + block, BF), pltpu.VMEM((12,) + block, BF)],
+    )(gathered, own, mine, above, below, rim, up)
     packed = move(pack, lambda a, b: (a, b ^ 1))
-    sent = call(strip_kernel, array((16, 4) + block))(low, packed)
-    gathered = lax.all_to_all(sent, "gx", 0, 0)
-
-    far_out, level2, level3 = call(
+    far_out, side_out, level3 = call(
         second_kernel,
-        [array(block), array((8, 2) + block), array((4,) + block)],
-    )(gathered, up)
-    side_out = call(
-        side_kernel,
-        array((26,) + block),
+        [array(block), array((26,) + block), array((4,) + block)],
         scratch=[pltpu.VMEM((20,) + block, BF), pltpu.VMEM((12,) + block, BF)],
-        flops=1 << 32,
-    )(gathered, own, mine, above, below, rim, level2, level3)
+    )(packed, gathered, level2, level3_own, own, mine, above, below, rim, up)
 
     chips = size_y // 2
     side = move(side_out, lambda a, b: (a, b + across(b % 2)))
     third = move(level3, lambda a, b: (a, b + 3 - 6 * (b % 2)))
     top = move(far_out, lambda a, b: (a, 2 * ((b // 2 + a) % chips) + b % 2))
+
+    weights = call(
+        later_kernel,
+        weight_shapes,
+        in_specs=[hbm] * 3 + [whole] * 12,
+        input_output_aliases={4 + at: at for at in range(11)},
+        scratch=build_scratch + [pltpu.SemaphoreType.DMA((10,))],
+    )(*far_inputs[:3], third, *weights)
+    w0, w1, w2, w3, w4, w5, table, down0, down1, down2, down3 = weights
 
     near_sum, far0, far1, far2, far3, tag = call(
         third_kernel,
@@ -464,7 +529,7 @@
         ],
         scratch=[
             pltpu.VMEM(lead + block, BF)
-            for lead in ((4, 10), (6, 6), (20, 4), (6, 4), (12, 2), (6, 3), (4, 3))
+            for lead in ((4, 10), (6, 6), (20, 2), (6, 4), (12,), (6, 3), (4, 3))
         ],
         flops=1,
         read=1,

time: 70.4 us -> 67.8 us (0.963)
  the two profiles are of different devices: /device:TPU:96 before, /device:TPU:64 now
where the time goes in v6:
time: 67.8 us; the launch traced here: 67.3 us
  blocking collectives  38.8 us (57%)
  starting transfers between devices  15.8 us (23%)
  Pallas kernels  8.85 us (13%)
  waiting for transfers between devices  3.75 us (6%)
    all_to_all x1, blocking collectives, shards(): top = lax.all_to_all(copies, 'gx', 0, 0)  21.7 us
    all_to_all x1, blocking collectives, shards(): gathered = lax.all_to_all(sent, 'gx', 0, 0)  17.1 us
    ppermute x6, starting transfers between devices, move(): return lax.ppermute(value, both, route(rule, size_x, size_y))  15.8 us
    pallas_call x1, Pallas kernels, shards(): call(start_kernel, [array((128, 256)), array(up_transfer.shape), array(pr...  4.34 us
    ppermute x6, waiting for transfers between devices, move(): return lax.ppermute(value, both, route(rule, size_x, size_y))  3.75 us
    pallas_call x1, Pallas kernels, shards(): call(fourth_kernel, array(probes.shape), scratch=[pltpu.VMEM((20,) + bloc...  2.53 us
  transfers between devices with their start and end apart: 6, of which 3 were waited for; matrix products, arithmetic and copies ran while one was open for 0% of the time, Pallas kernels for 8%

profile of v6, /device:TPU:64, one launch (start us, length us, event | category | flops | bytes accessed | tf_op | source)
XLA Modules:
  0.0 67.3 jit_solution(16053348849609492776)
XLA Ops:
  0.0 3.4 %collective-permute-start = (bf16[2,8,32,128]{3,2,1,0:T(8,128)(2,1)}, bf16[2,8,32,128]{3,2,1,0:T(8,128)(2,1)S(1)}, u32[]{:S(2)}, u32[]{:S(2)}) collective-permute-start(bf16[2,8,32,128]{3,2,1,0:T(8,128)(2,1)} %own_far.1), channel_id=1, source_target_pairs={{0,32},{1,33},{2,34},{3,35},{4,36},{5,37},{6,38},{7,39},{8,40},{9,... | collective-permute-start | bytes 393224 | tf_op jit(solution)/shard_map/ppermute | solution.py:455
  3.4 1.3 %collective-permute-start.1 = (bf16[2,8,32,128]{3,2,1,0:T(8,128)(2,1)}, bf16[2,8,32,128]{3,2,1,0:T(8,128)(2,1)S(1)}, u32[]{:S(2)}, u32[]{:S(2)}) collective-permute-start(bf16[2,8,32,128]{3,2,1,0:T(8,128)(2,1)} %own_far.1), channel_id=1, source_target_pairs={{32,0},{33,1},{34,2},{35,3},{36,4},{37,5},{38,6},{39,7},{40,8},{41... | collective-permute-start | bytes 393224 | tf_op jit(solution)/shard_map/ppermute | solution.py:455
  4.7 4.3 %shard_map.64 = (bf16[128,256]{1,0:T(8,128)(2,1)S(1)}, bf16[7,4,64,64]{3,2,1,0:T(8,128)(2,1)S(1)}, bf16[2,8,32,128]{3,2,1,0:T(8,128)(2,1)S(1)}, bf16[2,4,32,128]...) custom-call(s32[8,4,27]{2,1,0:T(4,128)} %ids_far.3, ...), custom_call_target="tpu_custom_call" | custom-call | flops 16777216 | bytes 2097152 | tf_op jit(solution)/shard_map/pallas_call | solution.py:477
  9.0 0.0 collective-permute-done.above
  9.1 1.4 %collective-permute-done.1.below = bf16[2,8,32,128]{3,2,1,0:T(8,128)(2,1)S(1)} collective-permute-done((bf16[2,8,32,128]{3,2,1,0:T(8,128)(2,1)}, bf16[2,8,32,128]{3,2,1,0:T(8,128)(2,1)S(1)}, u32[]{:S(2)}, u32[]{:S(2)}) %collective-permute-start.1) | collective-permute-done | bytes 131104 | tf_op jit(solution)/shard_map/ppermute | solution.py:455
  10.5 0.2 shard_map.65
  10.7 17.1 %all_to_all.10.gathered = bf16[16,2,32,128]{3,2,1,0:T(8,128)(2,1)S(1)} all-to-all(bf16[16,2,32,128]{3,2,1,0:T(8,128)(2,1)S(1)} %get-tuple-element.48), channel_id=1, replica_groups=mesh['gx'=16,'gy'=32] {'gx'}, dimensions={0} | all-to-all | bytes 524288 | tf_op jit(solution)/shard_map/all_to_all | solution.py:495
  27.8 0.5 shard_map.66
  28.3 1.9 %collective-permute-start.2 = (bf16[24,32,128]{2,1,0:T(8,128)(2,1)S(1)}, bf16[24,32,128]{2,1,0:T(8,128)(2,1)S(1)}, u32[]{:S(2)}, u32[]{:S(2)}) collective-permute-start(bf16[24,32,128]{2,1,0:T(8,128)(2,1)S(1)} %get-tuple-element.53), channel_id=1, source_target_pairs={{0,1},{1,0},{2,3},{3,2},{4,5},{5,4},{6,7},{7,6},{8,9},{9,8},{10,11... | collective-permute-start | bytes 589832 | tf_op jit(solution)/shard_map/ppermute | solution.py:455
  30.2 1.4 %collective-permute-done.2.packed = bf16[24,32,128]{2,1,0:T(8,128)(2,1)S(1)} collective-permute-done((bf16[24,32,128]{2,1,0:T(8,128)(2,1)S(1)}, bf16[24,32,128]{2,1,0:T(8,128)(2,1)S(1)}, u32[]{:S(2)}, u32[]{:S(2)}) %collective-permute-start.2) | collective-permute-done | bytes 196640 | tf_op jit(solution)/shard_map/ppermute | solution.py:455
  31.6 0.3 shard_map.67
  31.9 1.9 %collective-permute-start.4 = (bf16[26,32,128]{2,1,0:T(8,128)(2,1)S(1)}, bf16[26,32,128]{2,1,0:T(8,128)(2,1)S(1)}, u32[]{:S(2)}, u32[]{:S(2)}) collective-permute-start(bf16[26,32,128]{2,1,0:T(8,128)(2,1)S(1)} %get-tuple-element.58), channel_id=1, source_target_pairs={{1,2},{2,1},{3,4},{4,3},{5,6},{6,5},{7,8},{8,7},{9,10},{10,9},{11,... | collective-permute-start | bytes 638984 | tf_op jit(solution)/shard_map/ppermute | solution.py:455
  33.8 6.7 %collective-permute-start.5 = (bf16[4,32,128]{2,1,0:T(8,128)(2,1)S(1)}, bf16[4,32,128]{2,1,0:T(8,128)(2,1)S(1)}, u32[]{:S(2)}, u32[]{:S(2)}) collective-permute-start(bf16[4,32,128]{2,1,0:T(8,128)(2,1)S(1)} %get-tuple-element.57.level3), channel_id=1, source_target_pairs={{0,3},{2,5},{3,0},{4,7},{5,2},{6,9},{7,4},{8,11},{9,6},{10,13},{11... | collective-permute-start | bytes 98312 | tf_op jit(solution)/shard_map/ppermute | solution.py:455
  40.5 0.7 collective-permute-start.3
  41.1 0.9 %collective-permute-done.5.tag.third = bf16[4,32,128]{2,1,0:T(8,128)(2,1)S(1)} collective-permute-done((bf16[4,32,128]{2,1,0:T(8,128)(2,1)S(1)}, bf16[4,32,128]{2,1,0:T(8,128)(2,1)S(1)}, u32[]{:S(2)}, u32[]{:S(2)}) %collective-permute-start.5) | collective-permute-done | bytes 32800 | tf_op jit(solution)/shard_map/ppermute | solution.py:455
  42.1 0.1 shard_map.68
  42.2 0.0 collective-permute-done.4.side
  42.2 0.9 %shard_map.69 = (f32[2,8,32,128]{3,2,1,0:T(8,128)S(1)}, f32[128,256]{1,0:T(8,128)S(1)}, f32[64,128]{1,0:T(8,128)S(1)}, f32[32,128]{1,0:T(8,128)S(1)}, f32[32,64]{1,0:T(8,128)S(1)}, /*index=5*/f32[8,128]{1,0:T(8,128)S(1)}) custom-call(bf16[2,8,32,128]{3,2,1,0:T(8,128)(2,1)S(1)} %get-tuple-element.49.own, ...), custom_call_target="tpu_custom_call" | custom-call | flops 1 | bytes 1 | tf_op jit(solution)/shard_map/pallas_call | solution.py:523
  43.1 0.0 collective-permute-done.3.block
  43.1 21.7 %all_to_all.11.top = bf16[16,32,128]{2,1,0:T(8,128)(2,1)S(1)} all-to-all(bf16[16,32,128]{2,1,0:T(8,128)(2,1)S(1)} %shard_map.70), channel_id=1, replica_groups=mesh['gx'=16,'gy'=32] {'gx'}, dimensions={0} | all-to-all | bytes 262144 | tf_op jit(solution)/shard_map/all_to_all | solution.py:541
  64.8 2.5 %shard_map.71 = bf16[2,8,32,128]{3,2,1,0:T(8,128)(2,1)} custom-call(bf16[16,32,128]{2,1,0:T(8,128)(2,1)S(1)} %all_to_all.11.top, f32[2,8,32,128]{3,2,1,0:T(8,128)S(1)} %get-tuple-element.76.near_sum, f32[128,256]{1,0:T(8,128)S(1)} %get-tuple-element.77.far0, f32[64,128]{1,0:T(8,128)S(1)} %get-tuple-element.78.far1, f32[32,128]{1,0:T(8,128)S(1)} %get-tuple-element.79.far2, ...), custom_call_target="tpu_custom_call" | custom-call | flops 16777216 | bytes 2097152 | tf_op jit(solution)/shard_map/pallas_call | solution.py:543
  (1 shorter events, 0.0 us)
Async XLA Ops:
  0.0 9.0 %collective-permute-start = (bf16[2,8,32,128]{3,2,1,0:T(8,128)(2,1)}, bf16[2,8,32,128]{3,2,1,0:T(8,128)(2,1)S(1)}, u32[]{:S(2)}, u32[]{:S(2)}) collective-permute-start(bf16[2,8,32,128]{3,2,1,0:T(8,128)(2,1)} %own_far.1), channel_id=1, source_target_pairs={{0,32},{1,33},{2,34},{3,35},{4,36},{5,37},{6,38},{7,39},{8,40},{9,... | collective-permute-start | bytes 393224 | tf_op jit(solution)/shard_map/ppermute | solution.py:455
  3.4 7.1 %collective-permute-start.1 = (bf16[2,8,32,128]{3,2,1,0:T(8,128)(2,1)}, bf16[2,8,32,128]{3,2,1,0:T(8,128)(2,1)S(1)}, u32[]{:S(2)}, u32[]{:S(2)}) collective-permute-start(bf16[2,8,32,128]{3,2,1,0:T(8,128)(2,1)} %own_far.1), channel_id=1, source_target_pairs={{32,0},{33,1},{34,2},{35,3},{36,4},{37,5},{38,6},{39,7},{40,8},{41... | collective-permute-start | bytes 393224 | tf_op jit(solution)/shard_map/ppermute | solution.py:455
  28.3 3.3 %collective-permute-start.2 = (bf16[24,32,128]{2,1,0:T(8,128)(2,1)S(1)}, bf16[24,32,128]{2,1,0:T(8,128)(2,1)S(1)}, u32[]{:S(2)}, u32[]{:S(2)}) collective-permute-start(bf16[24,32,128]{2,1,0:T(8,128)(2,1)S(1)} %get-tuple-element.53), channel_id=1, source_target_pairs={{0,1},{1,0},{2,3},{3,2},{4,5},{5,4},{6,7},{7,6},{8,9},{9,8},{10,11... | collective-permute-start | bytes 589832 | tf_op jit(solution)/shard_map/ppermute | solution.py:455
  31.9 10.3 %collective-permute-start.4 = (bf16[26,32,128]{2,1,0:T(8,128)(2,1)S(1)}, bf16[26,32,128]{2,1,0:T(8,128)(2,1)S(1)}, u32[]{:S(2)}, u32[]{:S(2)}) collective-permute-start(bf16[26,32,128]{2,1,0:T(8,128)(2,1)S(1)} %get-tuple-element.58), channel_id=1, source_target_pairs={{1,2},{2,1},{3,4},{4,3},{5,6},{6,5},{7,8},{8,7},{9,10},{10,9},{11,... | collective-permute-start | bytes 638984 | tf_op jit(solution)/shard_map/ppermute | solution.py:455
  33.8 8.3 %collective-permute-start.5 = (bf16[4,32,128]{2,1,0:T(8,128)(2,1)S(1)}, bf16[4,32,128]{2,1,0:T(8,128)(2,1)S(1)}, u32[]{:S(2)}, u32[]{:S(2)}) collective-permute-start(bf16[4,32,128]{2,1,0:T(8,128)(2,1)S(1)} %get-tuple-element.57.level3), channel_id=1, source_target_pairs={{0,3},{2,5},{3,0},{4,7},{5,2},{6,9},{7,4},{8,11},{9,6},{10,13},{11... | collective-permute-start | bytes 98312 | tf_op jit(solution)/shard_map/ppermute | solution.py:455
  40.5 2.6 %collective-permute-start.3 = (bf16[32,128]{1,0:T(8,128)(2,1)S(1)}, bf16[32,128]{1,0:T(8,128)(2,1)S(1)}, u32[]{:S(2)}, u32[]{:S(2)}) collective-permute-start(bf16[32,128]{1,0:T(8,128)(2,1)S(1)} %get-tuple-element.56), channel_id=1, source_target_pairs={{0,0},{1,1},{2,2},{3,3},{4,4},{5,5},{6,6},{7,7},{8,8},{9,9},{10,10... | collective-permute-start | bytes 24584 | tf_op jit(solution)/shard_map/ppermute | solution.py:455

commit v7 on v6

--- a/solution.py
+++ b/solution.py
@@ -40,7 +40,8 @@
 
 
 def build_weights(
-    ids_far, coupling_far, down_far, w0, w1, w2, w3, w4, w5, table, down0, down1, down2, down3,
+    ids_far, coupling_far, down_far, wide, up,
+    w0, w1, w2, w3, table, down0, down1, down2, up5, up6, up7, top_far, top_leaf,
     ids, coupling, down, sems,
 ):
     row, col, _, _ = places()
@@ -110,20 +111,31 @@
     for r in range(4):
         for wc in range(6):
             w3[pl.ds((6 * r + wc) * RANK, RANK), :] = single(3, e3, f3, r + first3, wc)
-    levels[4].wait()
-    e4, f4 = row // 8, (col // 2) % 2
-    for wc in range(6):
-        for r in range(2):
-            w4[pl.ds((2 * wc + r) * RANK, RANK), :] = single(4, e4, f4, jnp.int32(2 + r), wc)
-    for level in (5, 6, 7):
+
+    other.wait()
+    chain = None
+    first_row = 0
+    for level in (4, 5, 6, 7):
         levels[level].wait()
+        e = (row // (1 << (level - 1))) % 2
         f = (col // (1 << (level - 3))) % 2
-        for wc in range(6):
-            w5[level - 5, pl.ds(wc * RANK, RANK), :] = single(
-                level, jnp.int32(0), f, jnp.int32(2), wc
-            )
-
-    other.wait()
+        e_up = (row // (1 << (level - 2))) % 2
+        f_up = (col // (1 << (level - 4))) % 2
+        step = down[level - 1, 2 * e_up + f_up]
+        chain = step if chain is None else dot(step, chain).astype(BF)
+        rows = 2 if level == 4 else 1
+        blocks = [
+            single(level, e, f, jnp.int32(2 + r), wc) for wc in range(6) for r in range(rows)
+        ]
+        stacked = dot(jnp.concatenate(blocks, axis=0), chain).astype(BF)
+        top_far[pl.ds(first_row, stacked.shape[0]), :] = stacked
+        first_row += stacked.shape[0]
+    from4 = jnp.concatenate([up[4, 0], up[4, 2], up[4, 1], up[4, 3]], axis=0)
+    from5 = jnp.concatenate([dot(from4, up[5, f]).astype(BF) for f in (0, 1)], axis=0)
+    up5[...] = from4
+    up6[...] = from5
+    up7[...] = jnp.concatenate([dot(from5, up[6, f]).astype(BF) for f in (0, 1)], axis=0)
+
     all0 = lanes([down[0, k] for k in range(4)])
     none0 = jnp.zeros_like(all0)
     down0[...] = jnp.concatenate([lanes([all0, none0]), lanes([none0, all0])], axis=0)
@@ -132,10 +144,15 @@
     none1 = jnp.zeros_like(both1)
     down1[...] = jnp.concatenate([lanes([both1, none1]), lanes([none1, both1])], axis=0)
     down2[...] = lanes([down[2, 2 * e2], down[2, 2 * e2 + 1]])
-    for level in (3, 4, 5, 6):
-        e = (row // (1 << (level - 1))) % 2
-        f = (col // (1 << (level - 3))) % 2
-        down3[level - 3] = down[level, 2 * e + f]
+
+    node1 = dot(down2[...], down1[...]).astype(BF)
+    for t in (0, 1):
+        node0 = dot(node1[:, 128 * t : 128 * t + 128], down0[...]).astype(BF)
+        for q in (0, 1):
+            for e in (0, 1):
+                at = 256 * q + 128 * e
+                leaves = dot(node0[:, at : at + 128], wide[...]).astype(BF)
+                top_leaf[:, pl.ds(256 * (4 * e + 2 * t + q), 256)] = leaves
 
 
 EARLY_PLANES = 7
@@ -144,7 +161,7 @@
 def start_kernel(
     ids_far, coupling_far, down_far, up_far, basis_far, own_far,
     wide, up, own, mine, low,
-    w0, w1, w2, w3, w4, w5, table, down0, down1, down2, down3,
+    w0, w1, w2, w3, table, down0, down1, down2, up5, up6, up7, top_far, top_leaf,
     ids, coupling, down, basis, sems, small_sems,
 ):
     _, _, chip, _ = places()
@@ -165,19 +182,19 @@
     @pl.when(chip < EARLY_PLANES)
     def _():
         build_weights(
-            ids_far, coupling_far, down_far,
-            w0, w1, w2, w3, w4, w5, table, down0, down1, down2, down3,
+            ids_far, coupling_far, down_far, wide, up,
+            w0, w1, w2, w3, table, down0, down1, down2, up5, up6, up7, top_far, top_leaf,
             ids, coupling, down, sems,
         )
 
 
-def later_kernel(ids_far, coupling_far, down_far, tag, *refs):
+def later_kernel(ids_far, coupling_far, down_far, wide, up, tag, *refs):
     _, _, chip, _ = places()
-    weights, scratch = refs[11:22], refs[22:]
+    weights, scratch = refs[13:26], refs[26:]
 
     @pl.when(chip >= EARLY_PLANES)
     def _():
-        build_weights(ids_far, coupling_far, down_far, *weights, *scratch)
+        build_weights(ids_far, coupling_far, down_far, wide, up, *weights, *scratch)
 
 
 def array(shape, kind=BF):
@@ -228,14 +245,13 @@
 def strip_kernel(gathered, own, mine, above, below, rim, up, pack, level2, level3, padded1, padded2):
     row, _, _, core = places()
     pairs2 = to_pairs(raise_pairs(gathered[...], up[1].reshape(4 * RANK, RANK)))
-    nodes3 = raise_pairs(pairs2, up[2].reshape(4 * RANK, RANK))[:, 0]
     level2[...] = pairs2[:, 0]
-    level3[...] = nodes3
+    level3[...] = raise_pairs(pairs2, up[2].reshape(4 * RANK, RANK))[:, 0]
     nothing = jnp.zeros((2, PROBES, 128), BF)
     padded1[pl.ds(0, 2)] = nothing
     padded1[pl.ds(18, 2)] = nothing
     padded2[pl.ds(0, 2)] = nothing
-    padded2[pl.ds(2, 8)] = pairs2[:, 0]
+    padded2[pl.ds(2, 8)] = level2[...]
     padded2[pl.ds(10, 2)] = nothing
     for r in range(16):
         padded1[r + 2] = gathered[r, 1 - core]
@@ -243,8 +259,8 @@
     edge_col = 7 - 7 * core
     pack[pl.ds(0, 6)] = padded1[pl.ds(2 * (row // 2), 6)]
     pack[pl.ds(6, 6)] = padded2[pl.ds(2 * (row // 4), 6)]
-    pack[12] = lanes([nodes3[0], nodes3[1]])
-    pack[13] = lanes([nodes3[2], nodes3[3]])
+    pack[12] = lanes([level3[0], level3[1]])
+    pack[13] = lanes([level3[2], level3[3]])
     pack[14] = mine[0, edge_pair]
     pack[15] = mine[1, edge_pair]
     pack[16] = own[0, edge_col]
@@ -305,10 +321,9 @@
 
 
 def third_kernel(
-    own, above, below, mine, packed, rim, gathered, level2, level3,
-    side, third, w0, w1, w2, w3, table,
-    near_sum, far0, far1, far2, far3, tag,
-    near, window0, padded1, window1, padded2, window2, window3,
+    own, above, below, mine, packed, rim, gathered, level2, side, w0, w1, w2, table,
+    near_sum, far0, far1, far2,
+    near, window0, padded1, window1, padded2, window2,
 ):
     row, _, _, core = places()
 
@@ -363,62 +378,17 @@
         window2[w, 2 * core] = side[16 + w]
     far2[...] = dot(lanes([window2[w, k] for w in range(6) for k in range(3)]), w2[...])
 
+
+def lower_kernel(
+    side, third, level3, w3, near_sum, far0, far1, far2, down0, down1, down2, wide, partial, window3
+):
+    _, _, _, core = places()
     for r in range(4):
         window3[r, 2 * core] = side[22 + r]
         window3[r, 1] = level3[r]
         window3[r, 2 - 2 * core] = third[r]
-    far3[...] = dot(lanes([window3[r, k] for r in range(4) for k in range(3)]), w3[...])
-    tag[...] = jnp.zeros_like(tag)
-
-
-def copies_kernel(block, tag, out):
-    for peer in range(16):
-        out[peer] = block[...]
-
-
-def fourth_kernel(
-    top, near_sum, far0, far1, far2, far3, w4, w5, wide, up, down0, down1, down2, down3,
-    out,
-    padded4, padded5, padded6, padded7,
-):
-    _, col, chip, _ = places()
-
-    blank = jnp.zeros((2, PROBES, 128), BF)
-    padded4[pl.ds(0, 2)] = blank
-    padded4[pl.ds(18, 2)] = blank
-    for c in range(16):
-        padded4[c + 2] = top[(chip - c + 16) % 16]
-    by_col = jnp.concatenate([up[4, 0], up[4, 2], up[4, 1], up[4, 3]], axis=0)
-    all4 = padded4[pl.ds(2, 16)].reshape(8, 2, PROBES, 128)
-    nodes5 = dot(lanes([all4[:, 0], all4[:, 1]]).reshape(-1, 256), by_col)
-    nodes5 = nodes5.astype(BF).reshape(8, PROBES, RANK)
-
-    def raise_row(nodes, level):
-        pairs = to_pairs(nodes).reshape(-1, 128)
-        both = jnp.concatenate([up[level, 0], up[level, 1]], axis=0)
-        return dot(pairs, both).astype(BF).reshape(-1, PROBES, RANK)
-
-    nodes6 = raise_row(nodes5, 5)
-    nodes7 = raise_row(nodes6, 6)
-    gap = jnp.zeros((2, PROBES, RANK), BF)
-    for padded, nodes in ((padded5, nodes5), (padded6, nodes6), (padded7, nodes7)):
-        count = nodes.shape[0]
-        padded[pl.ds(0, 2)] = gap
-        padded[pl.ds(2, count)] = nodes
-        padded[pl.ds(2 + count, 2)] = gap
-
-    def far_row(padded, level):
-        start = 2 * (col // (1 << (level - 2)))
-        return dot(lanes([padded[start + k] for k in range(6)]), w5[level - 5])
-
-    start4 = 2 * (chip // 2)
-    far4 = dot(lanes([padded4[start4 + k] for k in range(6)]), w4[...])
-    local = far_row(padded7, 7).astype(BF)
-    local = (far_row(padded6, 6) + dot(local, down3[3])).astype(BF)
-    local = (far_row(padded5, 5) + dot(local, down3[2])).astype(BF)
-    local = (far4 + dot(local, down3[1])).astype(BF)
-    local = (far3[...] + dot(local, down3[0])).astype(BF)
-    local2 = (far2[...] + dot(local, down2[...])).astype(BF)
+    far3 = dot(lanes([window3[r, k] for r in range(4) for k in range(3)]), w3[...])
+    local2 = (far2[...] + dot(far3.astype(BF), down2[...])).astype(BF)
     spread1 = dot(local2, down1[...])
     spread1 = jnp.concatenate([spread1[:, :128], spread1[:, 128:]], axis=0)
     local1 = (far1[...] + spread1).astype(BF)
@@ -430,7 +400,42 @@
         for q in range(4):
             for f in (0, 1):
                 part = far_sum[q, :, 128 * f : 128 * f + 128]
-                out[e, 2 * q + f] = (near_sum[e, 2 * q + f] + part).astype(BF)
+                partial[e, 2 * q + f] = near_sum[e, 2 * q + f] + part
+
+
+def copies_kernel(block, partial, out):
+    for peer in range(16):
+        out[peer] = block[...]
+
+
+def fourth_kernel(
+    top, partial, up5, up6, up7, top_far, top_leaf, out, padded4, padded5, padded6, padded7
+):
+    _, col, chip, _ = places()
+    blank = jnp.zeros((2, PROBES, 128), BF)
+    padded4[pl.ds(0, 2)] = blank
+    padded4[pl.ds(18, 2)] = blank
+    for c in range(16):
+        padded4[c + 2] = top[(chip - c + 16) % 16]
+    gap = jnp.zeros((2, PROBES, RANK), BF)
+    for padded, transfer, count in ((padded5, up5, 8), (padded6, up6, 4), (padded7, up7, 2)):
+        children = padded4[pl.ds(2, 16)].reshape(count, 16 // count, PROBES, 128)
+        joined = lanes([children[:, k] for k in range(16 // count)])
+        nodes = dot(joined.reshape(count * PROBES, -1), transfer[...])
+        padded[pl.ds(0, 2)] = gap
+        padded[pl.ds(2, count)] = nodes.astype(BF).reshape(count, PROBES, RANK)
+        padded[pl.ds(2 + count, 2)] = gap
+    start4 = 2 * (chip // 2)
+    window = [padded4[start4 + k] for k in range(6)]
+    for padded, level in ((padded5, 5), (padded6, 6), (padded7, 7)):
+        start = 2 * (col // (1 << (level - 2)))
+        window += [padded[start + k] for k in range(6)]
+    local = dot(lanes(window), top_far[...]).astype(BF)
+    spread = dot(local, top_leaf[...])
+    for e in (0, 1):
+        for c in range(8):
+            at = 128 * (8 * e + c)
+            out[e, c] = (partial[e, c] + spread[:, at : at + 128]).astype(BF)
 
 
 def route(rule, size_x, size_y):
@@ -466,9 +471,9 @@
     ]
     weight_shapes = [
         array((36 * RANK, 256)), array((36 * RANK, 128)), array((36 * RANK, 128)),
-        array((24 * RANK, RANK)), array((12 * RANK, RANK)), array((3, 6 * RANK, RANK)),
-        array((9 * 128, 128)), array((128, 512)), array((128, 256)), array((RANK, 128)),
-        array((4, RANK, RANK)),
+        array((24 * RANK, RANK)), array((9 * 128, 128)), array((128, 512)), array((128, 256)),
+        array((RANK, 128)), array((256, RANK)), array((512, RANK)), array((1024, RANK)),
+        array((30 * RANK, RANK)), array((RANK, 16 * 128)),
     ]
     build_scratch = [
         pltpu.SMEM(far_ids.shape, jnp.int32), pltpu.VMEM(coupling.shape, BF),
@@ -488,7 +493,6 @@
             pltpu.SemaphoreType.DMA((3,)),
         ],
     )(*far_inputs)
-
     rim, sent = call(rim_kernel, [array((4, 4) + block), array((16, 2) + block)])(
         above, below, wide, low
     )
@@ -511,41 +515,41 @@
     third = move(level3, lambda a, b: (a, b + 3 - 6 * (b % 2)))
     top = move(far_out, lambda a, b: (a, 2 * ((b // 2 + a) % chips) + b % 2))
 
+    count = len(weight_shapes)
     weights = call(
         later_kernel,
         weight_shapes,
-        in_specs=[hbm] * 3 + [whole] * 12,
-        input_output_aliases={4 + at: at for at in range(11)},
+        in_specs=[hbm] * 3 + [whole] * (3 + count),
+        input_output_aliases={6 + at: at for at in range(count)},
         scratch=build_scratch + [pltpu.SemaphoreType.DMA((10,))],
-    )(*far_inputs[:3], third, *weights)
-    w0, w1, w2, w3, w4, w5, table, down0, down1, down2, down3 = weights
-
-    near_sum, far0, far1, far2, far3, tag = call(
+    )(*far_inputs[:3], wide, up, side, *weights)
+    w0, w1, w2, w3, table, down0, down1, down2, up5, up6, up7, top_far, top_leaf = weights
+
+    near_sum, far0, far1, far2 = call(
         third_kernel,
         [
             array((2, 8) + block, F32), array((4 * PROBES, 256), F32),
-            array((2 * PROBES, 128), F32), array((PROBES, 128), F32), array((PROBES, RANK), F32),
-            array((8, 128), F32),
+            array((2 * PROBES, 128), F32), array((PROBES, 128), F32),
         ],
         scratch=[
             pltpu.VMEM(lead + block, BF)
-            for lead in ((4, 10), (6, 6), (20, 2), (6, 4), (12,), (6, 3), (4, 3))
+            for lead in ((4, 10), (6, 6), (20, 2), (6, 4), (12,), (6, 3))
         ],
-        flops=1,
-        read=1,
-    )(
-        own, above, below, mine, packed, rim, gathered, level2, level3, side, third,
-        w0, w1, w2, w3, table,
-    )
-    copies = call(copies_kernel, array((16,) + block))(top, tag)
+    )(own, above, below, mine, packed, rim, gathered, level2, side, w0, w1, w2, table)
+    partial = call(
+        lower_kernel,
+        array((2, 8) + block, F32),
+        scratch=[pltpu.VMEM((4, 3) + block, BF)],
+    )(side, third, level3, w3, near_sum, far0, far1, far2, down0, down1, down2, wide)
+    copies = call(copies_kernel, array((16,) + block))(top, partial)
     top = lax.all_to_all(copies, "gx", 0, 0)
 
     return call(
         fourth_kernel,
         array(probes.shape),
         scratch=[pltpu.VMEM((20,) + block, BF)]
-        + [pltpu.VMEM((count + 4, PROBES, RANK), BF) for count in (8, 4, 2)],
-    )(top, near_sum, far0, far1, far2, far3, w4, w5, wide, up, down0, down1, down2, down3)
+        + [pltpu.VMEM((nodes + 4, PROBES, RANK), BF) for nodes in (8, 4, 2)],
+    )(top, partial, up5, up6, up7, top_far, top_leaf)
 
 
 def solution(mesh):

time: 67.8 us -> 66.6 us (0.982)
  the two profiles are of different devices: /device:TPU:64 before, /device:TPU:1 now
where the time goes in v7:
time: 66.6 us; the launch traced here: 65.7 us
  blocking collectives  37.5 us (56%)
  starting transfers between devices  15 us (23%)
  Pallas kernels  9.83 us (15%)
  waiting for transfers between devices  3.23 us (5%)
    all_to_all x1, blocking collectives, shards(): top = lax.all_to_all(copies, 'gx', 0, 0)  22.4 us
    all_to_all x1, blocking collectives, shards(): gathered = lax.all_to_all(sent, 'gx', 0, 0)  15.1 us
    ppermute x6, starting transfers between devices, move(): return lax.ppermute(value, both, route(rule, size_x, size_y))  15 us
    pallas_call x1, Pallas kernels, shards(): call(start_kernel, [array((128, 256)), array(up_transfer.shape), array(pr...  5.92 us
    ppermute x6, waiting for transfers between devices, move(): return lax.ppermute(value, both, route(rule, size_x, size_y))  3.23 us
  transfers between devices with their start and end apart: 6, of which 2 were waited for; matrix products, arithmetic and copies ran while one was open for 0% of the time, Pallas kernels for 11%

profile of v7, /device:TPU:1, one launch (start us, length us, event | category | flops | bytes accessed | tf_op | source)
XLA Modules:
  0.0 65.7 jit_solution(17309185276602101809)
XLA Ops:
  0.0 3.9 %collective-permute-start = (bf16[2,8,32,128]{3,2,1,0:T(8,128)(2,1)}, bf16[2,8,32,128]{3,2,1,0:T(8,128)(2,1)S(1)}, u32[]{:S(2)}, u32[]{:S(2)}) collective-permute-start(bf16[2,8,32,128]{3,2,1,0:T(8,128)(2,1)} %own_far.1), channel_id=1, source_target_pairs={{0,32},{1,33},{2,34},{3,35},{4,36},{5,37},{6,38},{7,39},{8,40},{9,... | collective-permute-start | bytes 393224 | tf_op jit(solution)/shard_map/ppermute | solution.py:460
  3.9 1.3 %collective-permute-start.1 = (bf16[2,8,32,128]{3,2,1,0:T(8,128)(2,1)}, bf16[2,8,32,128]{3,2,1,0:T(8,128)(2,1)S(1)}, u32[]{:S(2)}, u32[]{:S(2)}) collective-permute-start(bf16[2,8,32,128]{3,2,1,0:T(8,128)(2,1)} %own_far.1), channel_id=1, source_target_pairs={{32,0},{33,1},{34,2},{35,3},{36,4},{37,5},{38,6},{39,7},{40,8},{41... | collective-permute-start | bytes 393224 | tf_op jit(solution)/shard_map/ppermute | solution.py:460
  5.2 5.9 %shard_map.64 = (bf16[128,256]{1,0:T(8,128)(2,1)S(1)}, bf16[7,4,64,64]{3,2,1,0:T(8,128)(2,1)S(1)}, bf16[2,8,32,128]{3,2,1,0:T(8,128)(2,1)S(1)}, bf16[2,4,32,128]...) custom-call(s32[8,4,27]{2,1,0:T(4,128)} %ids_far.3, ...), custom_call_target="tpu_custom_call" | custom-call | flops 16777216 | bytes 2097152 | tf_op jit(solution)/shard_map/pallas_call | solution.py:482
  11.2 0.0 collective-permute-done.above
  11.2 0.0 collective-permute-done.1.below
  11.2 0.2 shard_map.65
  11.4 15.1 %all_to_all.10.gathered = bf16[16,2,32,128]{3,2,1,0:T(8,128)(2,1)S(1)} all-to-all(bf16[16,2,32,128]{3,2,1,0:T(8,128)(2,1)S(1)} %get-tuple-element.50), channel_id=1, replica_groups=mesh['gx'=16,'gy'=32] {'gx'}, dimensions={0} | all-to-all | bytes 524288 | tf_op jit(solution)/shard_map/all_to_all | solution.py:499
  26.6 0.5 shard_map.66
  27.1 4.6 %collective-permute-start.2 = (bf16[24,32,128]{2,1,0:T(8,128)(2,1)S(1)}, bf16[24,32,128]{2,1,0:T(8,128)(2,1)S(1)}, u32[]{:S(2)}, u32[]{:S(2)}) collective-permute-start(bf16[24,32,128]{2,1,0:T(8,128)(2,1)S(1)} %get-tuple-element.55), channel_id=1, source_target_pairs={{0,1},{1,0},{2,3},{3,2},{4,5},{5,4},{6,7},{7,6},{8,9},{9,8},{10,11... | collective-permute-start | bytes 589832 | tf_op jit(solution)/shard_map/ppermute | solution.py:460
  31.7 1.0 %collective-permute-done.2.packed = bf16[24,32,128]{2,1,0:T(8,128)(2,1)S(1)} collective-permute-done((bf16[24,32,128]{2,1,0:T(8,128)(2,1)S(1)}, bf16[24,32,128]{2,1,0:T(8,128)(2,1)S(1)}, u32[]{:S(2)}, u32[]{:S(2)}) %collective-permute-start.2) | collective-permute-done | bytes 196640 | tf_op jit(solution)/shard_map/ppermute | solution.py:460
  32.8 0.3 shard_map.67
  33.0 3.8 %collective-permute-start.4 = (bf16[26,32,128]{2,1,0:T(8,128)(2,1)S(1)}, bf16[26,32,128]{2,1,0:T(8,128)(2,1)S(1)}, u32[]{:S(2)}, u32[]{:S(2)}) collective-permute-start(bf16[26,32,128]{2,1,0:T(8,128)(2,1)S(1)} %get-tuple-element.59), channel_id=1, source_target_pairs={{1,2},{2,1},{3,4},{4,3},{5,6},{6,5},{7,8},{8,7},{9,10},{10,9},{11,... | collective-permute-start | bytes 638984 | tf_op jit(solution)/shard_map/ppermute | solution.py:460
  36.8 0.7 %collective-permute-start.5 = (bf16[4,32,128]{2,1,0:T(8,128)(2,1)S(1)}, bf16[4,32,128]{2,1,0:T(8,128)(2,1)S(1)}, u32[]{:S(2)}, u32[]{:S(2)}) collective-permute-start(bf16[4,32,128]{2,1,0:T(8,128)(2,1)S(1)} %get-tuple-element.60.level3), channel_id=1, source_target_pairs={{0,3},{2,5},{3,0},{4,7},{5,2},{6,9},{7,4},{8,11},{9,6},{10,13},{11... | collective-permute-start | bytes 98312 | tf_op jit(solution)/shard_map/ppermute | solution.py:460
  37.5 0.7 %collective-permute-start.3 = (bf16[32,128]{1,0:T(8,128)(2,1)S(1)}, bf16[32,128]{1,0:T(8,128)(2,1)S(1)}, u32[]{:S(2)}, u32[]{:S(2)}) collective-permute-start(bf16[32,128]{1,0:T(8,128)(2,1)S(1)} %get-tuple-element.58), channel_id=1, source_target_pairs={{0,0},{1,1},{2,2},{3,3},{4,4},{5,5},{6,6},{7,7},{8,8},{9,9},{10,10... | collective-permute-start | bytes 24584 | tf_op jit(solution)/shard_map/ppermute | solution.py:460
  38.2 2.2 %collective-permute-done.4.tag.side = bf16[26,32,128]{2,1,0:T(8,128)(2,1)S(1)} collective-permute-done((bf16[26,32,128]{2,1,0:T(8,128)(2,1)S(1)}, bf16[26,32,128]{2,1,0:T(8,128)(2,1)S(1)}, u32[]{:S(2)}, u32[]{:S(2)}) %collective-permute-start.4) | collective-permute-done | bytes 213024 | tf_op jit(solution)/shard_map/ppermute | solution.py:460
  40.4 0.1 shard_map.68
  40.5 0.8 %shard_map.69 = (f32[2,8,32,128]{3,2,1,0:T(8,128)S(1)}, f32[128,256]{1,0:T(8,128)S(1)}, f32[64,128]{1,0:T(8,128)S(1)}, f32[32,128]{1,0:T(8,128)S(1)}) custom-call(bf16[2,8,32,128]{3,2,1,0:T(8,128)(2,1)S(1)} %get-tuple-element.51.own, bf16[2,8,32,128]{3,2,1,0:T(8,128)(2,1)S(1)} %collective-permute-done.above, ...), custom_call_target="tpu_custom_call" | custom-call | flops 16777216 | bytes 2097152 | tf_op jit(solution)/shard_map/pallas_call | solution.py:528
  41.2 0.0 collective-permute-done.5.third
  41.2 0.7 %shard_map.70.partial = f32[2,8,32,128]{3,2,1,0:T(8,128)S(1)} custom-call(bf16[26,32,128]{2,1,0:T(8,128)(2,1)S(1)} %collective-permute-done.4.tag.side, bf16[4,32,128]{2,1,0:T(8,128)(2,1)S(1)} %collective-permute-done.5.third, bf16[4,32,128]{2,1,0:T(8,128)(2,1)S(1)} %get-tuple-element.60.level3, bf16[1536,64]{1,0:T(8,128)(2,1)S(1)} %get-tuple-element.74.w3, ...), custom_call_target="tpu_custom_call" | custom-call | flops 16777216 | bytes 2097152 | tf_op jit(solution)/shard_map/pallas_call | solution.py:539
  42.0 0.0 collective-permute-done.3.block
  42.0 22.4 %all_to_all.11.top = bf16[16,32,128]{2,1,0:T(8,128)(2,1)S(1)} all-to-all(bf16[16,32,128]{2,1,0:T(8,128)(2,1)S(1)} %shard_map.71), channel_id=1, replica_groups=mesh['gx'=16,'gy'=32] {'gx'}, dimensions={0} | all-to-all | bytes 262144 | tf_op jit(solution)/shard_map/all_to_all | solution.py:545
  64.4 1.3 %shard_map.72 = bf16[2,8,32,128]{3,2,1,0:T(8,128)(2,1)} custom-call(bf16[16,32,128]{2,1,0:T(8,128)(2,1)S(1)} %all_to_all.11.top, f32[2,8,32,128]{3,2,1,0:T(8,128)S(1)} %shard_map.70.partial, bf16[256,64]{1,0:T(8,128)(2,1)S(1)} %get-tuple-element.86.up5, bf16[512,64]{1,0:T(8,128)(2,1)S(1)} %get-tuple-element.87.up6, ...), custom_call_target="tpu_custom_call" | custom-call | flops 16777216 | bytes 2097152 | tf_op jit(solution)/shard_map/pallas_call | solution.py:547
  (1 shorter events, 0.0 us)
Async XLA Ops:
  0.0 11.2 %collective-permute-start = (bf16[2,8,32,128]{3,2,1,0:T(8,128)(2,1)}, bf16[2,8,32,128]{3,2,1,0:T(8,128)(2,1)S(1)}, u32[]{:S(2)}, u32[]{:S(2)}) collective-permute-start(bf16[2,8,32,128]{3,2,1,0:T(8,128)(2,1)} %own_far.1), channel_id=1, source_target_pairs={{0,32},{1,33},{2,34},{3,35},{4,36},{5,37},{6,38},{7,39},{8,40},{9,... | collective-permute-start | bytes 393224 | tf_op jit(solution)/shard_map/ppermute | solution.py:460
  3.9 7.2 %collective-permute-start.1 = (bf16[2,8,32,128]{3,2,1,0:T(8,128)(2,1)}, bf16[2,8,32,128]{3,2,1,0:T(8,128)(2,1)S(1)}, u32[]{:S(2)}, u32[]{:S(2)}) collective-permute-start(bf16[2,8,32,128]{3,2,1,0:T(8,128)(2,1)} %own_far.1), channel_id=1, source_target_pairs={{32,0},{33,1},{34,2},{35,3},{36,4},{37,5},{38,6},{39,7},{40,8},{41... | collective-permute-start | bytes 393224 | tf_op jit(solution)/shard_map/ppermute | solution.py:460
  27.1 5.7 %collective-permute-start.2 = (bf16[24,32,128]{2,1,0:T(8,128)(2,1)S(1)}, bf16[24,32,128]{2,1,0:T(8,128)(2,1)S(1)}, u32[]{:S(2)}, u32[]{:S(2)}) collective-permute-start(bf16[24,32,128]{2,1,0:T(8,128)(2,1)S(1)} %get-tuple-element.55), channel_id=1, source_target_pairs={{0,1},{1,0},{2,3},{3,2},{4,5},{5,4},{6,7},{7,6},{8,9},{9,8},{10,11... | collective-permute-start | bytes 589832 | tf_op jit(solution)/shard_map/ppermute | solution.py:460
  33.0 7.3 %collective-permute-start.4 = (bf16[26,32,128]{2,1,0:T(8,128)(2,1)S(1)}, bf16[26,32,128]{2,1,0:T(8,128)(2,1)S(1)}, u32[]{:S(2)}, u32[]{:S(2)}) collective-permute-start(bf16[26,32,128]{2,1,0:T(8,128)(2,1)S(1)} %get-tuple-element.59), channel_id=1, source_target_pairs={{1,2},{2,1},{3,4},{4,3},{5,6},{6,5},{7,8},{8,7},{9,10},{10,9},{11,... | collective-permute-start | bytes 638984 | tf_op jit(solution)/shard_map/ppermute | solution.py:460
  36.8 4.4 %collective-permute-start.5 = (bf16[4,32,128]{2,1,0:T(8,128)(2,1)S(1)}, bf16[4,32,128]{2,1,0:T(8,128)(2,1)S(1)}, u32[]{:S(2)}, u32[]{:S(2)}) collective-permute-start(bf16[4,32,128]{2,1,0:T(8,128)(2,1)S(1)} %get-tuple-element.60.level3), channel_id=1, source_target_pairs={{0,3},{2,5},{3,0},{4,7},{5,2},{6,9},{7,4},{8,11},{9,6},{10,13},{11... | collective-permute-start | bytes 98312 | tf_op jit(solution)/shard_map/ppermute | solution.py:460
  37.5 4.4 %collective-permute-start.3 = (bf16[32,128]{1,0:T(8,128)(2,1)S(1)}, bf16[32,128]{1,0:T(8,128)(2,1)S(1)}, u32[]{:S(2)}, u32[]{:S(2)}) collective-permute-start(bf16[32,128]{1,0:T(8,128)(2,1)S(1)} %get-tuple-element.58), channel_id=1, source_target_pairs={{0,0},{1,1},{2,2},{3,3},{4,4},{5,5},{6,6},{7,7},{8,8},{9,9},{10,10... | collective-permute-start | bytes 24584 | tf_op jit(solution)/shard_map/ppermute | solution.py:460

commit v8 on v7

--- a/solution.py
+++ b/solution.py
@@ -41,7 +41,7 @@
 
 def build_weights(
     ids_far, coupling_far, down_far, wide, up,
-    w0, w1, w2, w3, table, down0, down1, down2, up5, up6, up7, top_far, top_leaf,
+    w0, w1, w2, w3, table, down0, down1, down2, up5, up6, up7, top_far, top_leaf, wx,
     ids, coupling, down, sems,
 ):
     row, col, _, _ = places()
@@ -111,6 +111,16 @@
     for r in range(4):
         for wc in range(6):
             w3[pl.ds((6 * r + wc) * RANK, RANK), :] = single(3, e3, f3, r + first3, wc)
+
+    @pl.when(row == 0)
+    def _():
+        for r in range(4):
+            for k in (0, 1):
+                wc = k + 4 - 4 * f3
+                for p in (0, 1):
+                    wx[pl.ds((2 * r + k) * RANK, RANK), pl.ds(128 * p, 128)] = lanes(
+                        [single(3, e, f3, jnp.int32(r + 2 - 2 * p), wc) for e in (0, 1)]
+                    )
 
     other.wait()
     chain = None
@@ -161,7 +171,7 @@
 def start_kernel(
     ids_far, coupling_far, down_far, up_far, basis_far, own_far,
     wide, up, own, mine, low,
-    w0, w1, w2, w3, table, down0, down1, down2, up5, up6, up7, top_far, top_leaf,
+    w0, w1, w2, w3, table, down0, down1, down2, up5, up6, up7, top_far, top_leaf, wx,
     ids, coupling, down, basis, sems, small_sems,
 ):
     _, _, chip, _ = places()
@@ -183,14 +193,14 @@
     def _():
         build_weights(
             ids_far, coupling_far, down_far, wide, up,
-            w0, w1, w2, w3, table, down0, down1, down2, up5, up6, up7, top_far, top_leaf,
+            w0, w1, w2, w3, table, down0, down1, down2, up5, up6, up7, top_far, top_leaf, wx,
             ids, coupling, down, sems,
         )
 
 
 def later_kernel(ids_far, coupling_far, down_far, wide, up, tag, *refs):
     _, _, chip, _ = places()
-    weights, scratch = refs[13:26], refs[26:]
+    weights, scratch = refs[14:28], refs[28:]
 
     @pl.when(chip >= EARLY_PLANES)
     def _():
@@ -380,13 +390,13 @@
 
 
 def lower_kernel(
-    side, third, level3, w3, near_sum, far0, far1, far2, down0, down1, down2, wide, partial, window3
+    side, level3, w3, near_sum, far0, far1, far2, down0, down1, down2, wide, partial, window3
 ):
     _, _, _, core = places()
     for r in range(4):
         window3[r, 2 * core] = side[22 + r]
         window3[r, 1] = level3[r]
-        window3[r, 2 - 2 * core] = third[r]
+        window3[r, 2 - 2 * core] = jnp.zeros((PROBES, 128), BF)
     far3 = dot(lanes([window3[r, k] for r in range(4) for k in range(3)]), w3[...])
     local2 = (far2[...] + dot(far3.astype(BF), down2[...])).astype(BF)
     spread1 = dot(local2, down1[...])
@@ -403,9 +413,24 @@
                 partial[e, 2 * q + f] = near_sum[e, 2 * q + f] + part
 
 
-def copies_kernel(block, partial, out):
+def copies_kernel(block, third, wx, partial, out):
+    row, _, _, _ = places()
     for peer in range(16):
-        out[peer] = block[...]
+        out[peer, pl.ds(0, PROBES)] = block[...]
+
+    @pl.when(row == 0)
+    def _():
+        parts = dot(lanes([third[r] for r in range(4)]), wx[...]).astype(BF)
+        for node in range(4):
+            part = parts[:, RANK * node : RANK * node + RANK]
+            packed = lanes([part[: PROBES // 2], part[PROBES // 2 :]])
+            for peer in range(4 * node, 4 * node + 4):
+                out[peer, pl.ds(PROBES, PROBES // 2)] = packed
+
+    @pl.when(row != 0)
+    def _():
+        for peer in range(16):
+            out[peer, pl.ds(PROBES, PROBES // 2)] = jnp.zeros((PROBES // 2, 128), BF)
 
 
 def fourth_kernel(
@@ -416,7 +441,7 @@
     padded4[pl.ds(0, 2)] = blank
     padded4[pl.ds(18, 2)] = blank
     for c in range(16):
-        padded4[c + 2] = top[(chip - c + 16) % 16]
+        padded4[c + 2] = top[(chip - c + 16) % 16, pl.ds(0, PROBES)]
     gap = jnp.zeros((2, PROBES, RANK), BF)
     for padded, transfer, count in ((padded5, up5, 8), (padded6, up6, 4), (padded7, up7, 2)):
         children = padded4[pl.ds(2, 16)].reshape(count, 16 // count, PROBES, 128)
@@ -430,7 +455,9 @@
     for padded, level in ((padded5, 5), (padded6, 6), (padded7, 7)):
         start = 2 * (col // (1 << (level - 2)))
         window += [padded[start + k] for k in range(6)]
-    local = dot(lanes(window), top_far[...]).astype(BF)
+    packed = top[0, pl.ds(PROBES, PROBES // 2)].astype(F32)
+    beyond = jnp.concatenate([packed[:, :RANK], packed[:, RANK:]], axis=0)
+    local = (dot(lanes(window), top_far[...]) + beyond).astype(BF)
     spread = dot(local, top_leaf[...])
     for e in (0, 1):
         for c in range(8):
@@ -473,7 +500,7 @@
         array((36 * RANK, 256)), array((36 * RANK, 128)), array((36 * RANK, 128)),
         array((24 * RANK, RANK)), array((9 * 128, 128)), array((128, 512)), array((128, 256)),
         array((RANK, 128)), array((256, RANK)), array((512, RANK)), array((1024, RANK)),
-        array((30 * RANK, RANK)), array((RANK, 16 * 128)),
+        array((30 * RANK, RANK)), array((RANK, 16 * 128)), array((8 * RANK, 4 * RANK)),
     ]
     build_scratch = [
         pltpu.SMEM(far_ids.shape, jnp.int32), pltpu.VMEM(coupling.shape, BF),
@@ -512,7 +539,7 @@
 
     chips = size_y // 2
     side = move(side_out, lambda a, b: (a, b + across(b % 2)))
-    third = move(level3, lambda a, b: (a, b + 3 - 6 * (b % 2)))
+    third = move(level3, lambda a, b: (a, b + 3 - 6 * (b % 2)) if a == 0 else (-1, -1))
     top = move(far_out, lambda a, b: (a, 2 * ((b // 2 + a) % chips) + b % 2))
 
     count = len(weight_shapes)
@@ -523,7 +550,7 @@
         input_output_aliases={6 + at: at for at in range(count)},
         scratch=build_scratch + [pltpu.SemaphoreType.DMA((10,))],
     )(*far_inputs[:3], wide, up, side, *weights)
-    w0, w1, w2, w3, table, down0, down1, down2, up5, up6, up7, top_far, top_leaf = weights
+    w0, w1, w2, w3, table, down0, down1, down2, up5, up6, up7, top_far, top_leaf, wx = weights
 
     near_sum, far0, far1, far2 = call(
         third_kernel,
@@ -540,8 +567,8 @@
         lower_kernel,
         array((2, 8) + block, F32),
         scratch=[pltpu.VMEM((4, 3) + block, BF)],
-    )(side, third, level3, w3, near_sum, far0, far1, far2, down0, down1, down2, wide)
-    copies = call(copies_kernel, array((16,) + block))(top, partial)
+    )(side, level3, w3, near_sum, far0, far1, far2, down0, down1, down2, wide)
+    copies = call(copies_kernel, array((16, PROBES + PROBES // 2, 128)))(top, third, wx, partial)
     top = lax.all_to_all(copies, "gx", 0, 0)
 
     return call(

time: 66.6 us -> 64.5 us (0.968)
  blocking collectives: 37.5 us -> 35.6 us
    all_to_all x1, blocking collectives: 22.4 us -> 20.5 us  [shards(): top = lax.all_to_all(copies, 'gx', 0, 0)]
  transfers between devices with their start and end apart: 6 -> 6, of which waited for: 2 -> 2; matrix products, arithmetic and copies ran while one was open for 0% -> 0% of each run, Pallas kernels for 11% -> 12%
where the time goes in v8:
time: 64.5 us; the launch traced here: 64 us
  blocking collectives  35.6 us (55%)
  starting transfers between devices  15 us (23%)
  Pallas kernels  10.1 us (16%)
  waiting for transfers between devices  3.23 us (5%)
    all_to_all x1, blocking collectives, shards(): top = lax.all_to_all(copies, 'gx', 0, 0)  20.5 us
    all_to_all x1, blocking collectives, shards(): gathered = lax.all_to_all(sent, 'gx', 0, 0)  15.1 us
    ppermute x6, starting transfers between devices, move(): return lax.ppermute(value, both, route(rule, size_x, size_y))  15 us
    pallas_call x1, Pallas kernels, shards(): call(start_kernel, [array((128, 256)), array(up_transfer.shape), array(pr...  5.92 us
    ppermute x6, waiting for transfers between devices, move(): return lax.ppermute(value, both, route(rule, size_x, size_y))  3.23 us
    pallas_call x1, Pallas kernels, shards(): call(fourth_kernel, array(probes.shape), scratch=[pltpu.VMEM((20,) + bloc...  1.29 us
  transfers between devices with their start and end apart: 6, of which 2 were waited for; matrix products, arithmetic and copies ran while one was open for 0% of the time, Pallas kernels for 12%

profile of v8, /device:TPU:1, one launch (start us, length us, event | category | flops | bytes accessed | tf_op | source)
XLA Modules:
  0.0 64.0 jit_solution(3188127291074451253)
XLA Ops:
  0.0 3.9 %collective-permute-start = (bf16[2,8,32,128]{3,2,1,0:T(8,128)(2,1)}, bf16[2,8,32,128]{3,2,1,0:T(8,128)(2,1)S(1)}, u32[]{:S(2)}, u32[]{:S(2)}) collective-permute-start(bf16[2,8,32,128]{3,2,1,0:T(8,128)(2,1)} %own_far.1), channel_id=1, source_target_pairs={{0,32},{1,33},{2,34},{3,35},{4,36},{5,37},{6,38},{7,39},{8,40},{9,... | collective-permute-start | bytes 393224 | tf_op jit(solution)/shard_map/ppermute | solution.py:487
  3.9 1.3 %collective-permute-start.1 = (bf16[2,8,32,128]{3,2,1,0:T(8,128)(2,1)}, bf16[2,8,32,128]{3,2,1,0:T(8,128)(2,1)S(1)}, u32[]{:S(2)}, u32[]{:S(2)}) collective-permute-start(bf16[2,8,32,128]{3,2,1,0:T(8,128)(2,1)} %own_far.1), channel_id=1, source_target_pairs={{32,0},{33,1},{34,2},{35,3},{36,4},{37,5},{38,6},{39,7},{40,8},{41... | collective-permute-start | bytes 393224 | tf_op jit(solution)/shard_map/ppermute | solution.py:487
  5.2 5.9 %shard_map.64 = (bf16[128,256]{1,0:T(8,128)(2,1)S(1)}, bf16[7,4,64,64]{3,2,1,0:T(8,128)(2,1)S(1)}, bf16[2,8,32,128]{3,2,1,0:T(8,128)(2,1)S(1)}, bf16[2,4,32,128]...) custom-call(s32[8,4,27]{2,1,0:T(4,128)} %ids_far.3, ...), custom_call_target="tpu_custom_call" | custom-call | flops 16777216 | bytes 2097152 | tf_op jit(solution)/shard_map/pallas_call | solution.py:509
  11.2 0.0 collective-permute-done.above
  11.2 0.0 collective-permute-done.1.below
  11.2 0.2 shard_map.65
  11.4 15.1 %all_to_all.10.gathered = bf16[16,2,32,128]{3,2,1,0:T(8,128)(2,1)S(1)} all-to-all(bf16[16,2,32,128]{3,2,1,0:T(8,128)(2,1)S(1)} %get-tuple-element.52), channel_id=1, replica_groups=mesh['gx'=16,'gy'=32] {'gx'}, dimensions={0} | all-to-all | bytes 524288 | tf_op jit(solution)/shard_map/all_to_all | solution.py:526
  26.6 0.5 shard_map.66
  27.1 4.6 %collective-permute-start.2 = (bf16[24,32,128]{2,1,0:T(8,128)(2,1)S(1)}, bf16[24,32,128]{2,1,0:T(8,128)(2,1)S(1)}, u32[]{:S(2)}, u32[]{:S(2)}) collective-permute-start(bf16[24,32,128]{2,1,0:T(8,128)(2,1)S(1)} %get-tuple-element.57), channel_id=1, source_target_pairs={{0,1},{1,0},{2,3},{3,2},{4,5},{5,4},{6,7},{7,6},{8,9},{9,8},{10,11... | collective-permute-start | bytes 589832 | tf_op jit(solution)/shard_map/ppermute | solution.py:487
  31.7 1.0 %collective-permute-done.2.packed = bf16[24,32,128]{2,1,0:T(8,128)(2,1)S(1)} collective-permute-done((bf16[24,32,128]{2,1,0:T(8,128)(2,1)S(1)}, bf16[24,32,128]{2,1,0:T(8,128)(2,1)S(1)}, u32[]{:S(2)}, u32[]{:S(2)}) %collective-permute-start.2) | collective-permute-done | bytes 196640 | tf_op jit(solution)/shard_map/ppermute | solution.py:487
  32.8 0.3 shard_map.67
  33.0 3.8 %collective-permute-start.5 = (bf16[26,32,128]{2,1,0:T(8,128)(2,1)S(1)}, bf16[26,32,128]{2,1,0:T(8,128)(2,1)S(1)}, u32[]{:S(2)}, u32[]{:S(2)}) collective-permute-start(bf16[26,32,128]{2,1,0:T(8,128)(2,1)S(1)} %get-tuple-element.62), channel_id=1, source_target_pairs={{1,2},{2,1},{3,4},{4,3},{5,6},{6,5},{7,8},{8,7},{9,10},{10,9},{11,... | collective-permute-start | bytes 638984 | tf_op jit(solution)/shard_map/ppermute | solution.py:487
  36.8 0.7 %collective-permute-start.4 = (bf16[4,32,128]{2,1,0:T(8,128)(2,1)S(1)}, bf16[4,32,128]{2,1,0:T(8,128)(2,1)S(1)}, u32[]{:S(2)}, u32[]{:S(2)}) collective-permute-start(bf16[4,32,128]{2,1,0:T(8,128)(2,1)S(1)} %get-tuple-element.61.level3), channel_id=1, source_target_pairs={{0,3},{2,5},{3,0},{4,7},{5,2},{6,9},{7,4},{8,11},{9,6},{10,13},{11... | collective-permute-start | bytes 98312 | tf_op jit(solution)/shard_map/ppermute | solution.py:487
  37.5 0.7 %collective-permute-start.3 = (bf16[32,128]{1,0:T(8,128)(2,1)S(1)}, bf16[32,128]{1,0:T(8,128)(2,1)S(1)}, u32[]{:S(2)}, u32[]{:S(2)}) collective-permute-start(bf16[32,128]{1,0:T(8,128)(2,1)S(1)} %get-tuple-element.60), channel_id=1, source_target_pairs={{0,0},{1,1},{2,2},{3,3},{4,4},{5,5},{6,6},{7,7},{8,8},{9,9},{10,10... | collective-permute-start | bytes 24584 | tf_op jit(solution)/shard_map/ppermute | solution.py:487
  38.2 2.2 %collective-permute-done.5.tag.side = bf16[26,32,128]{2,1,0:T(8,128)(2,1)S(1)} collective-permute-done((bf16[26,32,128]{2,1,0:T(8,128)(2,1)S(1)}, bf16[26,32,128]{2,1,0:T(8,128)(2,1)S(1)}, u32[]{:S(2)}, u32[]{:S(2)}) %collective-permute-start.5) | collective-permute-done | bytes 213024 | tf_op jit(solution)/shard_map/ppermute | solution.py:487
  40.4 0.1 shard_map.68
  40.5 0.8 %shard_map.69 = (f32[2,8,32,128]{3,2,1,0:T(8,128)S(1)}, f32[128,256]{1,0:T(8,128)S(1)}, f32[64,128]{1,0:T(8,128)S(1)}, f32[32,128]{1,0:T(8,128)S(1)}) custom-call(bf16[2,8,32,128]{3,2,1,0:T(8,128)(2,1)S(1)} %get-tuple-element.53.own, bf16[2,8,32,128]{3,2,1,0:T(8,128)(2,1)S(1)} %collective-permute-done.above, ...), custom_call_target="tpu_custom_call" | custom-call | flops 16777216 | bytes 2097152 | tf_op jit(solution)/shard_map/pallas_call | solution.py:555
  41.2 0.7 %shard_map.70.partial = f32[2,8,32,128]{3,2,1,0:T(8,128)S(1)} custom-call(bf16[26,32,128]{2,1,0:T(8,128)(2,1)S(1)} %collective-permute-done.5.tag.side, bf16[4,32,128]{2,1,0:T(8,128)(2,1)S(1)} %get-tuple-element.61.level3, bf16[1536,64]{1,0:T(8,128)(2,1)S(1)} %get-tuple-element.78.w3, f32[2,8,32,128]{3,2,1,0:T(8,128)S(1)} %get-tuple-element.83.near_sum, ...), custom_call_target="tpu_custom_call" | custom-call | flops 16777216 | bytes 2097152 | tf_op jit(solution)/shard_map/pallas_call | solution.py:566
  41.9 0.0 collective-permute-done.3.block
  42.0 0.0 collective-permute-done.4.third
  42.0 0.2 shard_map.71
  42.2 20.5 %all_to_all.11.top = bf16[16,48,128]{2,1,0:T(8,128)(2,1)S(1)} all-to-all(bf16[16,48,128]{2,1,0:T(8,128)(2,1)S(1)} %shard_map.71), channel_id=1, replica_groups=mesh['gx'=16,'gy'=32] {'gx'}, dimensions={0} | all-to-all | bytes 393216 | tf_op jit(solution)/shard_map/all_to_all | solution.py:572
  62.7 1.3 %shard_map.72 = bf16[2,8,32,128]{3,2,1,0:T(8,128)(2,1)} custom-call(bf16[16,48,128]{2,1,0:T(8,128)(2,1)S(1)} %all_to_all.11.top, f32[2,8,32,128]{3,2,1,0:T(8,128)S(1)} %shard_map.70.partial, bf16[256,64]{1,0:T(8,128)(2,1)S(1)} %get-tuple-element.90.up5, bf16[512,64]{1,0:T(8,128)(2,1)S(1)} %get-tuple-element.91.up6, ...), custom_call_target="tpu_custom_call" | custom-call | flops 16777216 | bytes 2097152 | tf_op jit(solution)/shard_map/pallas_call | solution.py:574
Async XLA Ops:
  0.0 11.2 %collective-permute-start = (bf16[2,8,32,128]{3,2,1,0:T(8,128)(2,1)}, bf16[2,8,32,128]{3,2,1,0:T(8,128)(2,1)S(1)}, u32[]{:S(2)}, u32[]{:S(2)}) collective-permute-start(bf16[2,8,32,128]{3,2,1,0:T(8,128)(2,1)} %own_far.1), channel_id=1, source_target_pairs={{0,32},{1,33},{2,34},{3,35},{4,36},{5,37},{6,38},{7,39},{8,40},{9,... | collective-permute-start | bytes 393224 | tf_op jit(solution)/shard_map/ppermute | solution.py:487
  3.9 7.2 %collective-permute-start.1 = (bf16[2,8,32,128]{3,2,1,0:T(8,128)(2,1)}, bf16[2,8,32,128]{3,2,1,0:T(8,128)(2,1)S(1)}, u32[]{:S(2)}, u32[]{:S(2)}) collective-permute-start(bf16[2,8,32,128]{3,2,1,0:T(8,128)(2,1)} %own_far.1), channel_id=1, source_target_pairs={{32,0},{33,1},{34,2},{35,3},{36,4},{37,5},{38,6},{39,7},{40,8},{41... | collective-permute-start | bytes 393224 | tf_op jit(solution)/shard_map/ppermute | solution.py:487
  27.1 5.7 %collective-permute-start.2 = (bf16[24,32,128]{2,1,0:T(8,128)(2,1)S(1)}, bf16[24,32,128]{2,1,0:T(8,128)(2,1)S(1)}, u32[]{:S(2)}, u32[]{:S(2)}) collective-permute-start(bf16[24,32,128]{2,1,0:T(8,128)(2,1)S(1)} %get-tuple-element.57), channel_id=1, source_target_pairs={{0,1},{1,0},{2,3},{3,2},{4,5},{5,4},{6,7},{7,6},{8,9},{9,8},{10,11... | collective-permute-start | bytes 589832 | tf_op jit(solution)/shard_map/ppermute | solution.py:487
  33.0 7.3 %collective-permute-start.5 = (bf16[26,32,128]{2,1,0:T(8,128)(2,1)S(1)}, bf16[26,32,128]{2,1,0:T(8,128)(2,1)S(1)}, u32[]{:S(2)}, u32[]{:S(2)}) collective-permute-start(bf16[26,32,128]{2,1,0:T(8,128)(2,1)S(1)} %get-tuple-element.62), channel_id=1, source_target_pairs={{1,2},{2,1},{3,4},{4,3},{5,6},{6,5},{7,8},{8,7},{9,10},{10,9},{11,... | collective-permute-start | bytes 638984 | tf_op jit(solution)/shard_map/ppermute | solution.py:487
  36.8 5.1 %collective-permute-start.4 = (bf16[4,32,128]{2,1,0:T(8,128)(2,1)S(1)}, bf16[4,32,128]{2,1,0:T(8,128)(2,1)S(1)}, u32[]{:S(2)}, u32[]{:S(2)}) collective-permute-start(bf16[4,32,128]{2,1,0:T(8,128)(2,1)S(1)} %get-tuple-element.61.level3), channel_id=1, source_target_pairs={{0,3},{2,5},{3,0},{4,7},{5,2},{6,9},{7,4},{8,11},{9,6},{10,13},{11... | collective-permute-start | bytes 98312 | tf_op jit(solution)/shard_map/ppermute | solution.py:487
  37.5 4.4 %collective-permute-start.3 = (bf16[32,128]{1,0:T(8,128)(2,1)S(1)}, bf16[32,128]{1,0:T(8,128)(2,1)S(1)}, u32[]{:S(2)}, u32[]{:S(2)}) collective-permute-start(bf16[32,128]{1,0:T(8,128)(2,1)S(1)} %get-tuple-element.60), channel_id=1, source_target_pairs={{0,0},{1,1},{2,2},{3,3},{4,4},{5,5},{6,6},{7,7},{8,8},{9,9},{10,10... | collective-permute-start | bytes 24584 | tf_op jit(solution)/shard_map/ppermute | solution.py:487

commit v9 on v8

--- a/solution.py
+++ b/solution.py
@@ -41,7 +41,7 @@
 
 def build_weights(
     ids_far, coupling_far, down_far, wide, up,
-    w0, w1, w2, w3, table, down0, down1, down2, up5, up6, up7, top_far, top_leaf, wx,
+    w0, w1, w2, w3, table, down0, down1, down2, top_leaf, wt, wx,
     ids, coupling, down, sems,
 ):
     row, col, _, _ = places()
@@ -123,28 +123,32 @@
                     )
 
     other.wait()
-    chain = None
-    first_row = 0
+    chip = col // 2
+    plane = (chip - row + 16) % 16
+
+    def coupled(level, e, wr, height):
+        levels_up = plane // (1 << height), chip // (1 << height)
+        f = levels_up[1] % 2
+        wc = levels_up[0] - levels_up[1] + 2 + f
+        inside = jnp.where(jnp.logical_and(wc >= 0, wc <= 5), 1.0, 0.0)
+        block = single(level, e, f, jnp.int32(wr), jnp.clip(wc, 0, 5))
+        return block.astype(F32) * jnp.full((RANK, RANK), inside, F32)
+
     for level in (4, 5, 6, 7):
         levels[level].wait()
-        e = (row // (1 << (level - 1))) % 2
-        f = (col // (1 << (level - 3))) % 2
-        e_up = (row // (1 << (level - 2))) % 2
-        f_up = (col // (1 << (level - 4))) % 2
-        step = down[level - 1, 2 * e_up + f_up]
-        chain = step if chain is None else dot(step, chain).astype(BF)
-        rows = 2 if level == 4 else 1
-        blocks = [
-            single(level, e, f, jnp.int32(2 + r), wc) for wc in range(6) for r in range(rows)
-        ]
-        stacked = dot(jnp.concatenate(blocks, axis=0), chain).astype(BF)
-        top_far[pl.ds(first_row, stacked.shape[0]), :] = stacked
-        first_row += stacked.shape[0]
-    from4 = jnp.concatenate([up[4, 0], up[4, 2], up[4, 1], up[4, 3]], axis=0)
-    from5 = jnp.concatenate([dot(from4, up[5, f]).astype(BF) for f in (0, 1)], axis=0)
-    up5[...] = from4
-    up6[...] = from5
-    up7[...] = jnp.concatenate([dot(from5, up[6, f]).astype(BF) for f in (0, 1)], axis=0)
+    zero = jnp.int32(0)
+    inner = coupled(7, zero, 2, 3).astype(BF)
+    inner = dot(dot(up[6, (plane // 4) % 2], inner).astype(BF), down[6, (chip // 4) % 2])
+    inner = (inner + coupled(6, zero, 2, 2)).astype(BF)
+    inner = dot(dot(up[5, (plane // 2) % 2], inner).astype(BF), down[5, (chip // 2) % 2])
+    inner = (inner + coupled(5, zero, 2, 1)).astype(BF)
+    for source in (0, 1):
+        raised = dot(up[4, 2 * source + plane % 2], inner).astype(BF)
+        for target in (0, 1):
+            local4 = dot(raised, down[4, 2 * target + chip % 2])
+            local4 = (local4 + coupled(4, jnp.int32(target), source + 2, 0)).astype(BF)
+            nodes = lanes([dot(local4, down[3, 2 * e + f3]).astype(BF) for e in (0, 1)])
+            wt[pl.ds(RANK * source, RANK), pl.ds(128 * target, 128)] = nodes
 
     all0 = lanes([down[0, k] for k in range(4)])
     none0 = jnp.zeros_like(all0)
@@ -171,7 +175,7 @@
 def start_kernel(
     ids_far, coupling_far, down_far, up_far, basis_far, own_far,
     wide, up, own, mine, low,
-    w0, w1, w2, w3, table, down0, down1, down2, up5, up6, up7, top_far, top_leaf, wx,
+    w0, w1, w2, w3, table, down0, down1, down2, top_leaf, wt, wx,
     ids, coupling, down, basis, sems, small_sems,
 ):
     _, _, chip, _ = places()
@@ -193,14 +197,14 @@
     def _():
         build_weights(
             ids_far, coupling_far, down_far, wide, up,
-            w0, w1, w2, w3, table, down0, down1, down2, up5, up6, up7, top_far, top_leaf, wx,
+            w0, w1, w2, w3, table, down0, down1, down2, top_leaf, wt, wx,
             ids, coupling, down, sems,
         )
 
 
 def later_kernel(ids_far, coupling_far, down_far, wide, up, tag, *refs):
     _, _, chip, _ = places()
-    weights, scratch = refs[14:28], refs[28:]
+    weights, scratch = refs[11:22], refs[22:]
 
     @pl.when(chip >= EARLY_PLANES)
     def _():
@@ -413,51 +417,24 @@
                 partial[e, 2 * q + f] = near_sum[e, 2 * q + f] + part
 
 
-def copies_kernel(block, third, wx, partial, out):
+def share_kernel(block, third, wt, wx, partial, out, parts):
     row, _, _, _ = places()
-    for peer in range(16):
-        out[peer, pl.ds(0, PROBES)] = block[...]
+    parts[...] = dot(block[...], wt[...])
 
     @pl.when(row == 0)
     def _():
-        parts = dot(lanes([third[r] for r in range(4)]), wx[...]).astype(BF)
-        for node in range(4):
-            part = parts[:, RANK * node : RANK * node + RANK]
-            packed = lanes([part[: PROBES // 2], part[PROBES // 2 :]])
-            for peer in range(4 * node, 4 * node + 4):
-                out[peer, pl.ds(PROBES, PROBES // 2)] = packed
-
-    @pl.when(row != 0)
-    def _():
-        for peer in range(16):
-            out[peer, pl.ds(PROBES, PROBES // 2)] = jnp.zeros((PROBES // 2, 128), BF)
-
-
-def fourth_kernel(
-    top, partial, up5, up6, up7, top_far, top_leaf, out, padded4, padded5, padded6, padded7
-):
-    _, col, chip, _ = places()
-    blank = jnp.zeros((2, PROBES, 128), BF)
-    padded4[pl.ds(0, 2)] = blank
-    padded4[pl.ds(18, 2)] = blank
-    for c in range(16):
-        padded4[c + 2] = top[(chip - c + 16) % 16, pl.ds(0, PROBES)]
-    gap = jnp.zeros((2, PROBES, RANK), BF)
-    for padded, transfer, count in ((padded5, up5, 8), (padded6, up6, 4), (padded7, up7, 2)):
-        children = padded4[pl.ds(2, 16)].reshape(count, 16 // count, PROBES, 128)
-        joined = lanes([children[:, k] for k in range(16 // count)])
-        nodes = dot(joined.reshape(count * PROBES, -1), transfer[...])
-        padded[pl.ds(0, 2)] = gap
-        padded[pl.ds(2, count)] = nodes.astype(BF).reshape(count, PROBES, RANK)
-        padded[pl.ds(2 + count, 2)] = gap
-    start4 = 2 * (chip // 2)
-    window = [padded4[start4 + k] for k in range(6)]
-    for padded, level in ((padded5, 5), (padded6, 6), (padded7, 7)):
-        start = 2 * (col // (1 << (level - 2)))
-        window += [padded[start + k] for k in range(6)]
-    packed = top[0, pl.ds(PROBES, PROBES // 2)].astype(F32)
-    beyond = jnp.concatenate([packed[:, :RANK], packed[:, RANK:]], axis=0)
-    local = (dot(lanes(window), top_far[...]) + beyond).astype(BF)
+        parts[...] += dot(lanes([third[r] for r in range(4)]), wx[...])
+
+    for node in range(4):
+        part = parts[:, RANK * node : RANK * node + RANK].astype(BF)
+        packed = lanes([part[: PROBES // 2], part[PROBES // 2 :]])
+        for peer in range(4 * node, 4 * node + 4):
+            out[peer] = packed
+
+
+def fourth_kernel(top, partial, top_leaf, out):
+    packed = jnp.sum(top[...].astype(F32), axis=0)
+    local = jnp.concatenate([packed[:, :RANK], packed[:, RANK:]], axis=0).astype(BF)
     spread = dot(local, top_leaf[...])
     for e in (0, 1):
         for c in range(8):
@@ -499,8 +476,8 @@
     weight_shapes = [
         array((36 * RANK, 256)), array((36 * RANK, 128)), array((36 * RANK, 128)),
         array((24 * RANK, RANK)), array((9 * 128, 128)), array((128, 512)), array((128, 256)),
-        array((RANK, 128)), array((256, RANK)), array((512, RANK)), array((1024, RANK)),
-        array((30 * RANK, RANK)), array((RANK, 16 * 128)), array((8 * RANK, 4 * RANK)),
+        array((RANK, 128)), array((RANK, 16 * 128)), array((2 * RANK, 4 * RANK)),
+        array((8 * RANK, 4 * RANK)),
     ]
     build_scratch = [
         pltpu.SMEM(far_ids.shape, jnp.int32), pltpu.VMEM(coupling.shape, BF),
@@ -550,7 +527,7 @@
         input_output_aliases={6 + at: at for at in range(count)},
         scratch=build_scratch + [pltpu.SemaphoreType.DMA((10,))],
     )(*far_inputs[:3], wide, up, side, *weights)
-    w0, w1, w2, w3, table, down0, down1, down2, up5, up6, up7, top_far, top_leaf, wx = weights
+    w0, w1, w2, w3, table, down0, down1, down2, top_leaf, wt, wx = weights
 
     near_sum, far0, far1, far2 = call(
         third_kernel,
@@ -568,15 +545,14 @@
         array((2, 8) + block, F32),
         scratch=[pltpu.VMEM((4, 3) + block, BF)],
     )(side, level3, w3, near_sum, far0, far1, far2, down0, down1, down2, wide)
-    copies = call(copies_kernel, array((16, PROBES + PROBES // 2, 128)))(top, third, wx, partial)
-    top = lax.all_to_all(copies, "gx", 0, 0)
-
-    return call(
-        fourth_kernel,
-        array(probes.shape),
-        scratch=[pltpu.VMEM((20,) + block, BF)]
-        + [pltpu.VMEM((nodes + 4, PROBES, RANK), BF) for nodes in (8, 4, 2)],
-    )(top, partial, up5, up6, up7, top_far, top_leaf)
+    shares = call(
+        share_kernel,
+        array((16, PROBES // 2, 128)),
+        scratch=[pltpu.VMEM((PROBES, 4 * RANK), F32)],
+    )(top, third, wt, wx, partial)
+    top = lax.all_to_all(shares, "gx", 0, 0)
+
+    return call(fourth_kernel, array(probes.shape))(top, partial, top_leaf)
 
 
 def solution(mesh):

time: 64.5 us -> 63.6 us (0.986)
  blocking collectives: 35.6 us -> 34.9 us
where the time goes in v9:
time: 63.6 us; the launch traced here: 63.1 us
  blocking collectives  34.9 us (55%)
  starting transfers between devices  14.9 us (23%)
  Pallas kernels  9.97 us (16%)
  waiting for transfers between devices  3.23 us (5%)
    all_to_all x1, blocking collectives, shards(): top = lax.all_to_all(shares, 'gx', 0, 0)  19.9 us
    all_to_all x1, blocking collectives, shards(): gathered = lax.all_to_all(sent, 'gx', 0, 0)  15 us
    ppermute x6, starting transfers between devices, move(): return lax.ppermute(value, both, route(rule, size_x, size_y))  14.9 us
    pallas_call x1, Pallas kernels, shards(): call(start_kernel, [array((128, 256)), array(up_transfer.shape), array(pr...  6.11 us
    ppermute x6, waiting for transfers between devices, move(): return lax.ppermute(value, both, route(rule, size_x, size_y))  3.23 us
  transfers between devices with their start and end apart: 6, of which 2 were waited for; matrix products, arithmetic and copies ran while one was open for 0% of the time, Pallas kernels for 12%

profile of v9, /device:TPU:1, one launch (start us, length us, event | category | flops | bytes accessed | tf_op | source)
XLA Modules:
  0.0 63.1 jit_solution(6127010134198011693)
XLA Ops:
  0.0 3.9 %collective-permute-start = (bf16[2,8,32,128]{3,2,1,0:T(8,128)(2,1)}, bf16[2,8,32,128]{3,2,1,0:T(8,128)(2,1)S(1)}, u32[]{:S(2)}, u32[]{:S(2)}) collective-permute-start(bf16[2,8,32,128]{3,2,1,0:T(8,128)(2,1)} %own_far.1), channel_id=1, source_target_pairs={{0,32},{1,33},{2,34},{3,35},{4,36},{5,37},{6,38},{7,39},{8,40},{9,... | collective-permute-start | bytes 393224 | tf_op jit(solution)/shard_map/ppermute | solution.py:464
  3.9 1.3 %collective-permute-start.1 = (bf16[2,8,32,128]{3,2,1,0:T(8,128)(2,1)}, bf16[2,8,32,128]{3,2,1,0:T(8,128)(2,1)S(1)}, u32[]{:S(2)}, u32[]{:S(2)}) collective-permute-start(bf16[2,8,32,128]{3,2,1,0:T(8,128)(2,1)} %own_far.1), channel_id=1, source_target_pairs={{32,0},{33,1},{34,2},{35,3},{36,4},{37,5},{38,6},{39,7},{40,8},{41... | collective-permute-start | bytes 393224 | tf_op jit(solution)/shard_map/ppermute | solution.py:464
  5.2 6.1 %shard_map.64 = (bf16[128,256]{1,0:T(8,128)(2,1)S(1)}, bf16[7,4,64,64]{3,2,1,0:T(8,128)(2,1)S(1)}, bf16[2,8,32,128]{3,2,1,0:T(8,128)(2,1)S(1)}, bf16[2,4,32,128]...) custom-call(s32[8,4,27]{2,1,0:T(4,128)} %ids_far.3, ...), custom_call_target="tpu_custom_call" | custom-call | flops 16777216 | bytes 2097152 | tf_op jit(solution)/shard_map/pallas_call | solution.py:486
  11.4 0.0 collective-permute-done.above
  11.4 0.0 collective-permute-done.1.below
  11.4 0.2 shard_map.65
  11.6 15.0 %all_to_all.10.gathered = bf16[16,2,32,128]{3,2,1,0:T(8,128)(2,1)S(1)} all-to-all(bf16[16,2,32,128]{3,2,1,0:T(8,128)(2,1)S(1)} %get-tuple-element.46), channel_id=1, replica_groups=mesh['gx'=16,'gy'=32] {'gx'}, dimensions={0} | all-to-all | bytes 524288 | tf_op jit(solution)/shard_map/all_to_all | solution.py:503
  26.6 0.5 shard_map.66
  27.1 4.6 %collective-permute-start.2 = (bf16[24,32,128]{2,1,0:T(8,128)(2,1)S(1)}, bf16[24,32,128]{2,1,0:T(8,128)(2,1)S(1)}, u32[]{:S(2)}, u32[]{:S(2)}) collective-permute-start(bf16[24,32,128]{2,1,0:T(8,128)(2,1)S(1)} %get-tuple-element.51), channel_id=1, source_target_pairs={{0,1},{1,0},{2,3},{3,2},{4,5},{5,4},{6,7},{7,6},{8,9},{9,8},{10,11... | collective-permute-start | bytes 589832 | tf_op jit(solution)/shard_map/ppermute | solution.py:464
  31.7 1.0 %collective-permute-done.2.packed = bf16[24,32,128]{2,1,0:T(8,128)(2,1)S(1)} collective-permute-done((bf16[24,32,128]{2,1,0:T(8,128)(2,1)S(1)}, bf16[24,32,128]{2,1,0:T(8,128)(2,1)S(1)}, u32[]{:S(2)}, u32[]{:S(2)}) %collective-permute-start.2) | collective-permute-done | bytes 196640 | tf_op jit(solution)/shard_map/ppermute | solution.py:464
  32.8 0.3 shard_map.67
  33.0 3.8 %collective-permute-start.5 = (bf16[26,32,128]{2,1,0:T(8,128)(2,1)S(1)}, bf16[26,32,128]{2,1,0:T(8,128)(2,1)S(1)}, u32[]{:S(2)}, u32[]{:S(2)}) collective-permute-start(bf16[26,32,128]{2,1,0:T(8,128)(2,1)S(1)} %get-tuple-element.56), channel_id=1, source_target_pairs={{1,2},{2,1},{3,4},{4,3},{5,6},{6,5},{7,8},{8,7},{9,10},{10,9},{11,... | collective-permute-start | bytes 638984 | tf_op jit(solution)/shard_map/ppermute | solution.py:464
  36.8 0.7 %collective-permute-start.4 = (bf16[4,32,128]{2,1,0:T(8,128)(2,1)S(1)}, bf16[4,32,128]{2,1,0:T(8,128)(2,1)S(1)}, u32[]{:S(2)}, u32[]{:S(2)}) collective-permute-start(bf16[4,32,128]{2,1,0:T(8,128)(2,1)S(1)} %get-tuple-element.55.level3), channel_id=1, source_target_pairs={{0,3},{2,5},{3,0},{4,7},{5,2},{6,9},{7,4},{8,11},{9,6},{10,13},{11... | collective-permute-start | bytes 98312 | tf_op jit(solution)/shard_map/ppermute | solution.py:464
  37.5 0.7 %collective-permute-start.3 = (bf16[32,128]{1,0:T(8,128)(2,1)S(1)}, bf16[32,128]{1,0:T(8,128)(2,1)S(1)}, u32[]{:S(2)}, u32[]{:S(2)}) collective-permute-start(bf16[32,128]{1,0:T(8,128)(2,1)S(1)} %get-tuple-element.54), channel_id=1, source_target_pairs={{0,0},{1,1},{2,2},{3,3},{4,4},{5,5},{6,6},{7,7},{8,8},{9,9},{10,10... | collective-permute-start | bytes 24584 | tf_op jit(solution)/shard_map/ppermute | solution.py:464
  38.2 2.2 %collective-permute-done.5.tag.side = bf16[26,32,128]{2,1,0:T(8,128)(2,1)S(1)} collective-permute-done((bf16[26,32,128]{2,1,0:T(8,128)(2,1)S(1)}, bf16[26,32,128]{2,1,0:T(8,128)(2,1)S(1)}, u32[]{:S(2)}, u32[]{:S(2)}) %collective-permute-start.5) | collective-permute-done | bytes 213024 | tf_op jit(solution)/shard_map/ppermute | solution.py:464
  40.4 0.1 shard_map.68
  40.5 0.8 %shard_map.69 = (f32[2,8,32,128]{3,2,1,0:T(8,128)S(1)}, f32[128,256]{1,0:T(8,128)S(1)}, f32[64,128]{1,0:T(8,128)S(1)}, f32[32,128]{1,0:T(8,128)S(1)}) custom-call(bf16[2,8,32,128]{3,2,1,0:T(8,128)(2,1)S(1)} %get-tuple-element.47.own, bf16[2,8,32,128]{3,2,1,0:T(8,128)(2,1)S(1)} %collective-permute-done.above, ...), custom_call_target="tpu_custom_call" | custom-call | flops 16777216 | bytes 2097152 | tf_op jit(solution)/shard_map/pallas_call | solution.py:532
  41.2 0.7 %shard_map.70.partial = f32[2,8,32,128]{3,2,1,0:T(8,128)S(1)} custom-call(bf16[26,32,128]{2,1,0:T(8,128)(2,1)S(1)} %collective-permute-done.5.tag.side, bf16[4,32,128]{2,1,0:T(8,128)(2,1)S(1)} %get-tuple-element.55.level3, bf16[1536,64]{1,0:T(8,128)(2,1)S(1)} %get-tuple-element.70.w3, f32[2,8,32,128]{3,2,1,0:T(8,128)S(1)} %get-tuple-element.75.near_sum, ...), custom_call_target="tpu_custom_call" | custom-call | flops 16777216 | bytes 2097152 | tf_op jit(solution)/shard_map/pallas_call | solution.py:543
  42.0 0.0 collective-permute-done.3.block
  42.0 0.0 collective-permute-done.4.third
  42.0 0.3 shard_map.71
  42.3 19.9 %all_to_all.11.top = bf16[16,16,128]{2,1,0:T(8,128)(2,1)S(1)} all-to-all(bf16[16,16,128]{2,1,0:T(8,128)(2,1)S(1)} %shard_map.71), channel_id=1, replica_groups=mesh['gx'=16,'gy'=32] {'gx'}, dimensions={0} | all-to-all | bytes 131072 | tf_op jit(solution)/shard_map/all_to_all | solution.py:553
  62.2 0.9 %shard_map.72 = bf16[2,8,32,128]{3,2,1,0:T(8,128)(2,1)} custom-call(bf16[16,16,128]{2,1,0:T(8,128)(2,1)S(1)} %all_to_all.11.top, f32[2,8,32,128]{3,2,1,0:T(8,128)S(1)} %shard_map.70.partial, bf16[64,2048]{1,0:T(8,128)(2,1)S(1)} %get-tuple-element.82.top_leaf), custom_call_target="tpu_custom_call" | custom-call | flops 16777216 | bytes 2097152 | tf_op jit(solution)/shard_map/pallas_call | solution.py:555
Async XLA Ops:
  0.0 11.4 %collective-permute-start = (bf16[2,8,32,128]{3,2,1,0:T(8,128)(2,1)}, bf16[2,8,32,128]{3,2,1,0:T(8,128)(2,1)S(1)}, u32[]{:S(2)}, u32[]{:S(2)}) collective-permute-start(bf16[2,8,32,128]{3,2,1,0:T(8,128)(2,1)} %own_far.1), channel_id=1, source_target_pairs={{0,32},{1,33},{2,34},{3,35},{4,36},{5,37},{6,38},{7,39},{8,40},{9,... | collective-permute-start | bytes 393224 | tf_op jit(solution)/shard_map/ppermute | solution.py:464
  3.9 7.4 %collective-permute-start.1 = (bf16[2,8,32,128]{3,2,1,0:T(8,128)(2,1)}, bf16[2,8,32,128]{3,2,1,0:T(8,128)(2,1)S(1)}, u32[]{:S(2)}, u32[]{:S(2)}) collective-permute-start(bf16[2,8,32,128]{3,2,1,0:T(8,128)(2,1)} %own_far.1), channel_id=1, source_target_pairs={{32,0},{33,1},{34,2},{35,3},{36,4},{37,5},{38,6},{39,7},{40,8},{41... | collective-permute-start | bytes 393224 | tf_op jit(solution)/shard_map/ppermute | solution.py:464
  27.1 5.7 %collective-permute-start.2 = (bf16[24,32,128]{2,1,0:T(8,128)(2,1)S(1)}, bf16[24,32,128]{2,1,0:T(8,128)(2,1)S(1)}, u32[]{:S(2)}, u32[]{:S(2)}) collective-permute-start(bf16[24,32,128]{2,1,0:T(8,128)(2,1)S(1)} %get-tuple-element.51), channel_id=1, source_target_pairs={{0,1},{1,0},{2,3},{3,2},{4,5},{5,4},{6,7},{7,6},{8,9},{9,8},{10,11... | collective-permute-start | bytes 589832 | tf_op jit(solution)/shard_map/ppermute | solution.py:464
  33.0 7.3 %collective-permute-start.5 = (bf16[26,32,128]{2,1,0:T(8,128)(2,1)S(1)}, bf16[26,32,128]{2,1,0:T(8,128)(2,1)S(1)}, u32[]{:S(2)}, u32[]{:S(2)}) collective-permute-start(bf16[26,32,128]{2,1,0:T(8,128)(2,1)S(1)} %get-tuple-element.56), channel_id=1, source_target_pairs={{1,2},{2,1},{3,4},{4,3},{5,6},{6,5},{7,8},{8,7},{9,10},{10,9},{11,... | collective-permute-start | bytes 638984 | tf_op jit(solution)/shard_map/ppermute | solution.py:464
  36.8 5.1 %collective-permute-start.4 = (bf16[4,32,128]{2,1,0:T(8,128)(2,1)S(1)}, bf16[4,32,128]{2,1,0:T(8,128)(2,1)S(1)}, u32[]{:S(2)}, u32[]{:S(2)}) collective-permute-start(bf16[4,32,128]{2,1,0:T(8,128)(2,1)S(1)} %get-tuple-element.55.level3), channel_id=1, source_target_pairs={{0,3},{2,5},{3,0},{4,7},{5,2},{6,9},{7,4},{8,11},{9,6},{10,13},{11... | collective-permute-start | bytes 98312 | tf_op jit(solution)/shard_map/ppermute | solution.py:464
  37.5 4.5 %collective-permute-start.3 = (bf16[32,128]{1,0:T(8,128)(2,1)S(1)}, bf16[32,128]{1,0:T(8,128)(2,1)S(1)}, u32[]{:S(2)}, u32[]{:S(2)}) collective-permute-start(bf16[32,128]{1,0:T(8,128)(2,1)S(1)} %get-tuple-element.54), channel_id=1, source_target_pairs={{0,0},{1,1},{2,2},{3,3},{4,4},{5,5},{6,6},{7,7},{8,8},{9,9},{10,10... | collective-permute-start | bytes 24584 | tf_op jit(solution)/shard_map/ppermute | solution.py:464

commit v10 on v9

--- a/solution.py
+++ b/solution.py
@@ -415,6 +415,10 @@
             for f in (0, 1):
                 part = far_sum[q, :, 128 * f : 128 * f + 128]
                 partial[e, 2 * q + f] = near_sum[e, 2 * q + f] + part
+
+
+def arrival_kernel(block, partial, out):
+    out[...] = block[...]
 
 
 def share_kernel(block, third, wt, wx, partial, out, parts):
@@ -545,11 +549,12 @@
         array((2, 8) + block, F32),
         scratch=[pltpu.VMEM((4, 3) + block, BF)],
     )(side, level3, w3, near_sum, far0, far1, far2, down0, down1, down2, wide)
+    arrived = call(arrival_kernel, array(block), flops=1 << 36)(top, partial)
     shares = call(
         share_kernel,
         array((16, PROBES // 2, 128)),
         scratch=[pltpu.VMEM((PROBES, 4 * RANK), F32)],
-    )(top, third, wt, wx, partial)
+    )(arrived, third, wt, wx, partial)
     top = lax.all_to_all(shares, "gx", 0, 0)
 
     return call(fourth_kernel, array(probes.shape))(top, partial, top_leaf)

time: 63.6 us -> 63.6 us (level)
  no operation moved by 1% of the time
where the time goes in v10:
time: 63.6 us; the launch traced here: 63.1 us
  blocking collectives  34.9 us (55%)
  starting transfers between devices  14.9 us (23%)
  Pallas kernels  9.97 us (16%)
  waiting for transfers between devices  3.23 us (5%)
    all_to_all x1, blocking collectives, shards(): top = lax.all_to_all(shares, 'gx', 0, 0)  19.9 us
    all_to_all x1, blocking collectives, shards(): gathered = lax.all_to_all(sent, 'gx', 0, 0)  15 us
    ppermute x6, starting transfers between devices, move(): return lax.ppermute(value, both, route(rule, size_x, size_y))  14.9 us
    pallas_call x1, Pallas kernels, shards(): call(start_kernel, [array((128, 256)), array(up_transfer.shape), array(pr...  6.11 us
    ppermute x6, waiting for transfers between devices, move(): return lax.ppermute(value, both, route(rule, size_x, size_y))  3.23 us
  transfers between devices with their start and end apart: 6, of which 2 were waited for; matrix products, arithmetic and copies ran while one was open for 0% of the time, Pallas kernels for 12%

profile of v10, /device:TPU:1, one launch (start us, length us, event | category | flops | bytes accessed | tf_op | source)
XLA Modules:
  0.0 63.1 jit_solution(4045669892458129355)
XLA Ops:
  0.0 3.9 %collective-permute-start = (bf16[2,8,32,128]{3,2,1,0:T(8,128)(2,1)}, bf16[2,8,32,128]{3,2,1,0:T(8,128)(2,1)S(1)}, u32[]{:S(2)}, u32[]{:S(2)}) collective-permute-start(bf16[2,8,32,128]{3,2,1,0:T(8,128)(2,1)} %own_far.1), channel_id=1, source_target_pairs={{0,32},{1,33},{2,34},{3,35},{4,36},{5,37},{6,38},{7,39},{8,40},{9,... | collective-permute-start | bytes 393224 | tf_op jit(solution)/shard_map/ppermute | solution.py:468
  3.9 1.3 %collective-permute-start.1 = (bf16[2,8,32,128]{3,2,1,0:T(8,128)(2,1)}, bf16[2,8,32,128]{3,2,1,0:T(8,128)(2,1)S(1)}, u32[]{:S(2)}, u32[]{:S(2)}) collective-permute-start(bf16[2,8,32,128]{3,2,1,0:T(8,128)(2,1)} %own_far.1), channel_id=1, source_target_pairs={{32,0},{33,1},{34,2},{35,3},{36,4},{37,5},{38,6},{39,7},{40,8},{41... | collective-permute-start | bytes 393224 | tf_op jit(solution)/shard_map/ppermute | solution.py:468
  5.2 6.1 %shard_map.64 = (bf16[128,256]{1,0:T(8,128)(2,1)S(1)}, bf16[7,4,64,64]{3,2,1,0:T(8,128)(2,1)S(1)}, bf16[2,8,32,128]{3,2,1,0:T(8,128)(2,1)S(1)}, bf16[2,4,32,128]...) custom-call(s32[8,4,27]{2,1,0:T(4,128)} %ids_far.3, ...), custom_call_target="tpu_custom_call" | custom-call | flops 16777216 | bytes 2097152 | tf_op jit(solution)/shard_map/pallas_call | solution.py:490
  11.4 0.0 collective-permute-done.above
  11.4 0.0 collective-permute-done.1.below
  11.4 0.2 shard_map.65
  11.6 15.0 %all_to_all.10.gathered = bf16[16,2,32,128]{3,2,1,0:T(8,128)(2,1)S(1)} all-to-all(bf16[16,2,32,128]{3,2,1,0:T(8,128)(2,1)S(1)} %get-tuple-element.46), channel_id=1, replica_groups=mesh['gx'=16,'gy'=32] {'gx'}, dimensions={0} | all-to-all | bytes 524288 | tf_op jit(solution)/shard_map/all_to_all | solution.py:507
  26.6 0.5 shard_map.66
  27.1 4.6 %collective-permute-start.2 = (bf16[24,32,128]{2,1,0:T(8,128)(2,1)S(1)}, bf16[24,32,128]{2,1,0:T(8,128)(2,1)S(1)}, u32[]{:S(2)}, u32[]{:S(2)}) collective-permute-start(bf16[24,32,128]{2,1,0:T(8,128)(2,1)S(1)} %get-tuple-element.51), channel_id=1, source_target_pairs={{0,1},{1,0},{2,3},{3,2},{4,5},{5,4},{6,7},{7,6},{8,9},{9,8},{10,11... | collective-permute-start | bytes 589832 | tf_op jit(solution)/shard_map/ppermute | solution.py:468
  31.7 1.0 %collective-permute-done.2.packed = bf16[24,32,128]{2,1,0:T(8,128)(2,1)S(1)} collective-permute-done((bf16[24,32,128]{2,1,0:T(8,128)(2,1)S(1)}, bf16[24,32,128]{2,1,0:T(8,128)(2,1)S(1)}, u32[]{:S(2)}, u32[]{:S(2)}) %collective-permute-start.2) | collective-permute-done | bytes 196640 | tf_op jit(solution)/shard_map/ppermute | solution.py:468
  32.8 0.3 shard_map.67
  33.0 3.8 %collective-permute-start.4 = (bf16[26,32,128]{2,1,0:T(8,128)(2,1)S(1)}, bf16[26,32,128]{2,1,0:T(8,128)(2,1)S(1)}, u32[]{:S(2)}, u32[]{:S(2)}) collective-permute-start(bf16[26,32,128]{2,1,0:T(8,128)(2,1)S(1)} %get-tuple-element.55), channel_id=1, source_target_pairs={{1,2},{2,1},{3,4},{4,3},{5,6},{6,5},{7,8},{8,7},{9,10},{10,9},{11,... | collective-permute-start | bytes 638984 | tf_op jit(solution)/shard_map/ppermute | solution.py:468
  36.8 0.7 %collective-permute-start.3 = (bf16[32,128]{1,0:T(8,128)(2,1)S(1)}, bf16[32,128]{1,0:T(8,128)(2,1)S(1)}, u32[]{:S(2)}, u32[]{:S(2)}) collective-permute-start(bf16[32,128]{1,0:T(8,128)(2,1)S(1)} %get-tuple-element.54), channel_id=1, source_target_pairs={{0,0},{1,1},{2,2},{3,3},{4,4},{5,5},{6,6},{7,7},{8,8},{9,9},{10,10... | collective-permute-start | bytes 24584 | tf_op jit(solution)/shard_map/ppermute | solution.py:468
  37.5 0.7 %collective-permute-start.5 = (bf16[4,32,128]{2,1,0:T(8,128)(2,1)S(1)}, bf16[4,32,128]{2,1,0:T(8,128)(2,1)S(1)}, u32[]{:S(2)}, u32[]{:S(2)}) collective-permute-start(bf16[4,32,128]{2,1,0:T(8,128)(2,1)S(1)} %get-tuple-element.56.level3), channel_id=1, source_target_pairs={{0,3},{2,5},{3,0},{4,7},{5,2},{6,9},{7,4},{8,11},{9,6},{10,13},{11... | collective-permute-start | bytes 98312 | tf_op jit(solution)/shard_map/ppermute | solution.py:468
  38.2 2.2 %collective-permute-done.4.tag.side = bf16[26,32,128]{2,1,0:T(8,128)(2,1)S(1)} collective-permute-done((bf16[26,32,128]{2,1,0:T(8,128)(2,1)S(1)}, bf16[26,32,128]{2,1,0:T(8,128)(2,1)S(1)}, u32[]{:S(2)}, u32[]{:S(2)}) %collective-permute-start.4) | collective-permute-done | bytes 213024 | tf_op jit(solution)/shard_map/ppermute | solution.py:468
  40.4 0.1 shard_map.68
  40.5 0.8 %shard_map.69 = (f32[2,8,32,128]{3,2,1,0:T(8,128)S(1)}, f32[128,256]{1,0:T(8,128)S(1)}, f32[64,128]{1,0:T(8,128)S(1)}, f32[32,128]{1,0:T(8,128)S(1)}) custom-call(bf16[2,8,32,128]{3,2,1,0:T(8,128)(2,1)S(1)} %get-tuple-element.47.own, bf16[2,8,32,128]{3,2,1,0:T(8,128)(2,1)S(1)} %collective-permute-done.above, ...), custom_call_target="tpu_custom_call" | custom-call | flops 16777216 | bytes 2097152 | tf_op jit(solution)/shard_map/pallas_call | solution.py:536
  41.2 0.7 %shard_map.70.partial = f32[2,8,32,128]{3,2,1,0:T(8,128)S(1)} custom-call(bf16[26,32,128]{2,1,0:T(8,128)(2,1)S(1)} %collective-permute-done.4.tag.side, bf16[4,32,128]{2,1,0:T(8,128)(2,1)S(1)} %get-tuple-element.56.level3, bf16[1536,64]{1,0:T(8,128)(2,1)S(1)} %get-tuple-element.68.w3, f32[2,8,32,128]{3,2,1,0:T(8,128)S(1)} %get-tuple-element.73.near_sum, ...), custom_call_target="tpu_custom_call" | custom-call | flops 16777216 | bytes 2097152 | tf_op jit(solution)/shard_map/pallas_call | solution.py:547
  42.0 0.0 collective-permute-done.3.block
  42.0 0.0 collective-permute-done.5.third
  42.0 0.3 shard_map.72
  42.3 19.9 %all_to_all.11.top = bf16[16,16,128]{2,1,0:T(8,128)(2,1)S(1)} all-to-all(bf16[16,16,128]{2,1,0:T(8,128)(2,1)S(1)} %shard_map.72), channel_id=1, replica_groups=mesh['gx'=16,'gy'=32] {'gx'}, dimensions={0} | all-to-all | bytes 131072 | tf_op jit(solution)/shard_map/all_to_all | solution.py:558
  62.2 0.9 %shard_map.73 = bf16[2,8,32,128]{3,2,1,0:T(8,128)(2,1)} custom-call(bf16[16,16,128]{2,1,0:T(8,128)(2,1)S(1)} %all_to_all.11.top, f32[2,8,32,128]{3,2,1,0:T(8,128)S(1)} %shard_map.70.partial, bf16[64,2048]{1,0:T(8,128)(2,1)S(1)} %get-tuple-element.82.top_leaf), custom_call_target="tpu_custom_call" | custom-call | flops 16777216 | bytes 2097152 | tf_op jit(solution)/shard_map/pallas_call | solution.py:560
  (1 shorter events, 0.0 us)
Async XLA Ops:
  0.0 11.4 %collective-permute-start = (bf16[2,8,32,128]{3,2,1,0:T(8,128)(2,1)}, bf16[2,8,32,128]{3,2,1,0:T(8,128)(2,1)S(1)}, u32[]{:S(2)}, u32[]{:S(2)}) collective-permute-start(bf16[2,8,32,128]{3,2,1,0:T(8,128)(2,1)} %own_far.1), channel_id=1, source_target_pairs={{0,32},{1,33},{2,34},{3,35},{4,36},{5,37},{6,38},{7,39},{8,40},{9,... | collective-permute-start | bytes 393224 | tf_op jit(solution)/shard_map/ppermute | solution.py:468
  3.9 7.4 %collective-permute-start.1 = (bf16[2,8,32,128]{3,2,1,0:T(8,128)(2,1)}, bf16[2,8,32,128]{3,2,1,0:T(8,128)(2,1)S(1)}, u32[]{:S(2)}, u32[]{:S(2)}) collective-permute-start(bf16[2,8,32,128]{3,2,1,0:T(8,128)(2,1)} %own_far.1), channel_id=1, source_target_pairs={{32,0},{33,1},{34,2},{35,3},{36,4},{37,5},{38,6},{39,7},{40,8},{41... | collective-permute-start | bytes 393224 | tf_op jit(solution)/shard_map/ppermute | solution.py:468
  27.1 5.7 %collective-permute-start.2 = (bf16[24,32,128]{2,1,0:T(8,128)(2,1)S(1)}, bf16[24,32,128]{2,1,0:T(8,128)(2,1)S(1)}, u32[]{:S(2)}, u32[]{:S(2)}) collective-permute-start(bf16[24,32,128]{2,1,0:T(8,128)(2,1)S(1)} %get-tuple-element.51), channel_id=1, source_target_pairs={{0,1},{1,0},{2,3},{3,2},{4,5},{5,4},{6,7},{7,6},{8,9},{9,8},{10,11... | collective-permute-start | bytes 589832 | tf_op jit(solution)/shard_map/ppermute | solution.py:468
  33.0 7.3 %collective-permute-start.4 = (bf16[26,32,128]{2,1,0:T(8,128)(2,1)S(1)}, bf16[26,32,128]{2,1,0:T(8,128)(2,1)S(1)}, u32[]{:S(2)}, u32[]{:S(2)}) collective-permute-start(bf16[26,32,128]{2,1,0:T(8,128)(2,1)S(1)} %get-tuple-element.55), channel_id=1, source_target_pairs={{1,2},{2,1},{3,4},{4,3},{5,6},{6,5},{7,8},{8,7},{9,10},{10,9},{11,... | collective-permute-start | bytes 638984 | tf_op jit(solution)/shard_map/ppermute | solution.py:468
  36.8 5.1 %collective-permute-start.3 = (bf16[32,128]{1,0:T(8,128)(2,1)S(1)}, bf16[32,128]{1,0:T(8,128)(2,1)S(1)}, u32[]{:S(2)}, u32[]{:S(2)}) collective-permute-start(bf16[32,128]{1,0:T(8,128)(2,1)S(1)} %get-tuple-element.54), channel_id=1, source_target_pairs={{0,0},{1,1},{2,2},{3,3},{4,4},{5,5},{6,6},{7,7},{8,8},{9,9},{10,10... | collective-permute-start | bytes 24584 | tf_op jit(solution)/shard_map/ppermute | solution.py:468
  37.5 4.5 %collective-permute-start.5 = (bf16[4,32,128]{2,1,0:T(8,128)(2,1)S(1)}, bf16[4,32,128]{2,1,0:T(8,128)(2,1)S(1)}, u32[]{:S(2)}, u32[]{:S(2)}) collective-permute-start(bf16[4,32,128]{2,1,0:T(8,128)(2,1)S(1)} %get-tuple-element.56.level3), channel_id=1, source_target_pairs={{0,3},{2,5},{3,0},{4,7},{5,2},{6,9},{7,4},{8,11},{9,6},{10,13},{11... | collective-permute-start | bytes 98312 | tf_op jit(solution)/shard_map/ppermute | solution.py:468

commit v11 on v10

--- a/solution.py
+++ b/solution.py
@@ -78,24 +78,6 @@
                 halves.append(coupling[level, ids[level, 2 * e + f, block_slot(e, f, wr, wc)]])
         return lanes(halves)
 
-    first.wait()
-    levels[0].wait()
-    for wr in range(6):
-        for wc in range(6):
-            at = pl.ds((6 * wr + wc) * RANK, RANK)
-            for e in (0, 1):
-                w0[at, pl.ds(128 * e, 128)] = pair(0, e, wr, wc)
-
-    for level, out, bit in ((1, w1, row % 2), (2, w2, (row // 2) % 2)):
-        levels[level].wait()
-        for e in (0, 1):
-
-            @pl.when(bit == e)
-            def _(level=level, out=out, e=e):
-                for wr in range(6):
-                    for wc in range(6):
-                        out[pl.ds((6 * wr + wc) * RANK, RANK), :] = pair(level, e, wr, wc)
-
     def single(level, e, f, wr, wc):
         row_in = jnp.logical_and(wr >= e + 1, wr <= e + 3)
         col_in = jnp.logical_and(wc >= f + 1, wc <= f + 3)
@@ -105,23 +87,9 @@
         block = coupling[level, ids[level, 2 * e + f, slot]]
         return block * jnp.full((RANK, RANK), keep, F32).astype(BF)
 
-    levels[3].wait()
     e3, f3 = (row // 4) % 2, col % 2
-    first3 = 2 - 2 * (row // 8)
-    for r in range(4):
-        for wc in range(6):
-            w3[pl.ds((6 * r + wc) * RANK, RANK), :] = single(3, e3, f3, r + first3, wc)
-
-    @pl.when(row == 0)
-    def _():
-        for r in range(4):
-            for k in (0, 1):
-                wc = k + 4 - 4 * f3
-                for p in (0, 1):
-                    wx[pl.ds((2 * r + k) * RANK, RANK), pl.ds(128 * p, 128)] = lanes(
-                        [single(3, e, f3, jnp.int32(r + 2 - 2 * p), wc) for e in (0, 1)]
-                    )
-
+    first.wait()
+    levels[0].wait()
     other.wait()
     chip = col // 2
     plane = (chip - row + 16) % 16
@@ -149,6 +117,38 @@
             local4 = (local4 + coupled(4, jnp.int32(target), source + 2, 0)).astype(BF)
             nodes = lanes([dot(local4, down[3, 2 * e + f3]).astype(BF) for e in (0, 1)])
             wt[pl.ds(RANK * source, RANK), pl.ds(128 * target, 128)] = nodes
+
+    for wr in range(6):
+        for wc in range(6):
+            at = pl.ds((6 * wr + wc) * RANK, RANK)
+            for e in (0, 1):
+                w0[at, pl.ds(128 * e, 128)] = pair(0, e, wr, wc)
+
+    for level, out, bit in ((1, w1, row % 2), (2, w2, (row // 2) % 2)):
+        levels[level].wait()
+        for e in (0, 1):
+
+            @pl.when(bit == e)
+            def _(level=level, out=out, e=e):
+                for wr in range(6):
+                    for wc in range(6):
+                        out[pl.ds((6 * wr + wc) * RANK, RANK), :] = pair(level, e, wr, wc)
+
+    levels[3].wait()
+    first3 = 2 - 2 * (row // 8)
+    for r in range(4):
+        for wc in range(6):
+            w3[pl.ds((6 * r + wc) * RANK, RANK), :] = single(3, e3, f3, r + first3, wc)
+
+    @pl.when(row == 0)
+    def _():
+        for r in range(4):
+            for k in (0, 1):
+                wc = k + 4 - 4 * f3
+                for p in (0, 1):
+                    wx[pl.ds((2 * r + k) * RANK, RANK), pl.ds(128 * p, 128)] = lanes(
+                        [single(3, e, f3, jnp.int32(r + 2 - 2 * p), wc) for e in (0, 1)]
+                    )
 
     all0 = lanes([down[0, k] for k in range(4)])
     none0 = jnp.zeros_like(all0)

time: 63.6 us -> 63.6 us (level)
  Pallas kernels: 9.97 us -> 11 us
  blocking collectives: 34.9 us -> 33.9 us
    pallas_call x1, Pallas kernels: 6.11 us -> 7.11 us  [shards(): call(start_kernel, [array((128, 256)), array(up_transfer.shape), array(pr...]
    all_to_all x1, blocking collectives: 19.9 us -> 19.1 us  [shards(): top = lax.all_to_all(shares, 'gx', 0, 0)]
  transfers between devices with their start and end apart: 6 -> 6, of which waited for: 2 -> 2; matrix products, arithmetic and copies ran while one was open for 0% -> 0% of each run, Pallas kernels for 12% -> 14%
where the time goes in v11:
time: 63.6 us; the launch traced here: 63.1 us
  blocking collectives  33.9 us (53%)
  starting transfers between devices  14.9 us (23%)
  Pallas kernels  11 us (17%)
  waiting for transfers between devices  3.23 us (5%)
    all_to_all x1, blocking collectives, shards(): top = lax.all_to_all(shares, 'gx', 0, 0)  19.1 us
    ppermute x6, starting transfers between devices, move(): return lax.ppermute(value, both, route(rule, size_x, size_y))  14.9 us
    all_to_all x1, blocking collectives, shards(): gathered = lax.all_to_all(sent, 'gx', 0, 0)  14.8 us
    pallas_call x1, Pallas kernels, shards(): call(start_kernel, [array((128, 256)), array(up_transfer.shape), array(pr...  7.11 us
    ppermute x6, waiting for transfers between devices, move(): return lax.ppermute(value, both, route(rule, size_x, size_y))  3.23 us
  transfers between devices with their start and end apart: 6, of which 2 were waited for; matrix products, arithmetic and copies ran while one was open for 0% of the time, Pallas kernels for 14%

profile of v11, /device:TPU:1, one launch (start us, length us, event | category | flops | bytes accessed | tf_op | source)
XLA Modules:
  0.0 63.1 jit_solution(5654398618595506995)
XLA Ops:
  0.0 3.9 %collective-permute-start = (bf16[2,8,32,128]{3,2,1,0:T(8,128)(2,1)}, bf16[2,8,32,128]{3,2,1,0:T(8,128)(2,1)S(1)}, u32[]{:S(2)}, u32[]{:S(2)}) collective-permute-start(bf16[2,8,32,128]{3,2,1,0:T(8,128)(2,1)} %own_far.1), channel_id=1, source_target_pairs={{0,32},{1,33},{2,34},{3,35},{4,36},{5,37},{6,38},{7,39},{8,40},{9,... | collective-permute-start | bytes 393224 | tf_op jit(solution)/shard_map/ppermute | solution.py:468
  3.9 1.3 %collective-permute-start.1 = (bf16[2,8,32,128]{3,2,1,0:T(8,128)(2,1)}, bf16[2,8,32,128]{3,2,1,0:T(8,128)(2,1)S(1)}, u32[]{:S(2)}, u32[]{:S(2)}) collective-permute-start(bf16[2,8,32,128]{3,2,1,0:T(8,128)(2,1)} %own_far.1), channel_id=1, source_target_pairs={{32,0},{33,1},{34,2},{35,3},{36,4},{37,5},{38,6},{39,7},{40,8},{41... | collective-permute-start | bytes 393224 | tf_op jit(solution)/shard_map/ppermute | solution.py:468
  5.2 7.1 %shard_map.64 = (bf16[128,256]{1,0:T(8,128)(2,1)S(1)}, bf16[7,4,64,64]{3,2,1,0:T(8,128)(2,1)S(1)}, bf16[2,8,32,128]{3,2,1,0:T(8,128)(2,1)S(1)}, bf16[2,4,32,128]...) custom-call(s32[8,4,27]{2,1,0:T(4,128)} %ids_far.3, ...), custom_call_target="tpu_custom_call" | custom-call | flops 16777216 | bytes 2097152 | tf_op jit(solution)/shard_map/pallas_call | solution.py:490
  12.4 0.0 collective-permute-done.above
  12.4 0.0 collective-permute-done.1.below
  12.4 0.2 shard_map.65
  12.6 14.8 %all_to_all.10.gathered = bf16[16,2,32,128]{3,2,1,0:T(8,128)(2,1)S(1)} all-to-all(bf16[16,2,32,128]{3,2,1,0:T(8,128)(2,1)S(1)} %get-tuple-element.46), channel_id=1, replica_groups=mesh['gx'=16,'gy'=32] {'gx'}, dimensions={0} | all-to-all | bytes 524288 | tf_op jit(solution)/shard_map/all_to_all | solution.py:507
  27.4 0.5 shard_map.66
  27.9 4.6 %collective-permute-start.2 = (bf16[24,32,128]{2,1,0:T(8,128)(2,1)S(1)}, bf16[24,32,128]{2,1,0:T(8,128)(2,1)S(1)}, u32[]{:S(2)}, u32[]{:S(2)}) collective-permute-start(bf16[24,32,128]{2,1,0:T(8,128)(2,1)S(1)} %get-tuple-element.51), channel_id=1, source_target_pairs={{0,1},{1,0},{2,3},{3,2},{4,5},{5,4},{6,7},{7,6},{8,9},{9,8},{10,11... | collective-permute-start | bytes 589832 | tf_op jit(solution)/shard_map/ppermute | solution.py:468
  32.5 1.0 %collective-permute-done.2.packed = bf16[24,32,128]{2,1,0:T(8,128)(2,1)S(1)} collective-permute-done((bf16[24,32,128]{2,1,0:T(8,128)(2,1)S(1)}, bf16[24,32,128]{2,1,0:T(8,128)(2,1)S(1)}, u32[]{:S(2)}, u32[]{:S(2)}) %collective-permute-start.2) | collective-permute-done | bytes 196640 | tf_op jit(solution)/shard_map/ppermute | solution.py:468
  33.6 0.3 shard_map.67
  33.9 3.8 %collective-permute-start.4 = (bf16[26,32,128]{2,1,0:T(8,128)(2,1)S(1)}, bf16[26,32,128]{2,1,0:T(8,128)(2,1)S(1)}, u32[]{:S(2)}, u32[]{:S(2)}) collective-permute-start(bf16[26,32,128]{2,1,0:T(8,128)(2,1)S(1)} %get-tuple-element.55), channel_id=1, source_target_pairs={{1,2},{2,1},{3,4},{4,3},{5,6},{6,5},{7,8},{8,7},{9,10},{10,9},{11,... | collective-permute-start | bytes 638984 | tf_op jit(solution)/shard_map/ppermute | solution.py:468
  37.7 0.7 %collective-permute-start.3 = (bf16[32,128]{1,0:T(8,128)(2,1)S(1)}, bf16[32,128]{1,0:T(8,128)(2,1)S(1)}, u32[]{:S(2)}, u32[]{:S(2)}) collective-permute-start(bf16[32,128]{1,0:T(8,128)(2,1)S(1)} %get-tuple-element.54), channel_id=1, source_target_pairs={{0,0},{1,1},{2,2},{3,3},{4,4},{5,5},{6,6},{7,7},{8,8},{9,9},{10,10... | collective-permute-start | bytes 24584 | tf_op jit(solution)/shard_map/ppermute | solution.py:468
  38.3 0.7 %collective-permute-start.5 = (bf16[4,32,128]{2,1,0:T(8,128)(2,1)S(1)}, bf16[4,32,128]{2,1,0:T(8,128)(2,1)S(1)}, u32[]{:S(2)}, u32[]{:S(2)}) collective-permute-start(bf16[4,32,128]{2,1,0:T(8,128)(2,1)S(1)} %get-tuple-element.56.level3), channel_id=1, source_target_pairs={{0,3},{2,5},{3,0},{4,7},{5,2},{6,9},{7,4},{8,11},{9,6},{10,13},{11... | collective-permute-start | bytes 98312 | tf_op jit(solution)/shard_map/ppermute | solution.py:468
  39.0 2.2 %collective-permute-done.4.tag.side = bf16[26,32,128]{2,1,0:T(8,128)(2,1)S(1)} collective-permute-done((bf16[26,32,128]{2,1,0:T(8,128)(2,1)S(1)}, bf16[26,32,128]{2,1,0:T(8,128)(2,1)S(1)}, u32[]{:S(2)}, u32[]{:S(2)}) %collective-permute-start.4) | collective-permute-done | bytes 213024 | tf_op jit(solution)/shard_map/ppermute | solution.py:468
  41.2 0.1 shard_map.68
  41.3 0.8 %shard_map.69 = (f32[2,8,32,128]{3,2,1,0:T(8,128)S(1)}, f32[128,256]{1,0:T(8,128)S(1)}, f32[64,128]{1,0:T(8,128)S(1)}, f32[32,128]{1,0:T(8,128)S(1)}) custom-call(bf16[2,8,32,128]{3,2,1,0:T(8,128)(2,1)S(1)} %get-tuple-element.47.own, bf16[2,8,32,128]{3,2,1,0:T(8,128)(2,1)S(1)} %collective-permute-done.above, ...), custom_call_target="tpu_custom_call" | custom-call | flops 16777216 | bytes 2097152 | tf_op jit(solution)/shard_map/pallas_call | solution.py:536
  42.1 0.7 %shard_map.70.partial = f32[2,8,32,128]{3,2,1,0:T(8,128)S(1)} custom-call(bf16[26,32,128]{2,1,0:T(8,128)(2,1)S(1)} %collective-permute-done.4.tag.side, bf16[4,32,128]{2,1,0:T(8,128)(2,1)S(1)} %get-tuple-element.56.level3, bf16[1536,64]{1,0:T(8,128)(2,1)S(1)} %get-tuple-element.68.w3, f32[2,8,32,128]{3,2,1,0:T(8,128)S(1)} %get-tuple-element.73.near_sum, ...), custom_call_target="tpu_custom_call" | custom-call | flops 16777216 | bytes 2097152 | tf_op jit(solution)/shard_map/pallas_call | solution.py:547
  42.8 0.0 collective-permute-done.3.block
  42.8 0.0 collective-permute-done.5.third
  42.8 0.3 shard_map.72
  43.2 19.1 %all_to_all.11.top = bf16[16,16,128]{2,1,0:T(8,128)(2,1)S(1)} all-to-all(bf16[16,16,128]{2,1,0:T(8,128)(2,1)S(1)} %shard_map.72), channel_id=1, replica_groups=mesh['gx'=16,'gy'=32] {'gx'}, dimensions={0} | all-to-all | bytes 131072 | tf_op jit(solution)/shard_map/all_to_all | solution.py:558
  62.2 0.9 %shard_map.73 = bf16[2,8,32,128]{3,2,1,0:T(8,128)(2,1)} custom-call(bf16[16,16,128]{2,1,0:T(8,128)(2,1)S(1)} %all_to_all.11.top, f32[2,8,32,128]{3,2,1,0:T(8,128)S(1)} %shard_map.70.partial, bf16[64,2048]{1,0:T(8,128)(2,1)S(1)} %get-tuple-element.82.top_leaf), custom_call_target="tpu_custom_call" | custom-call | flops 16777216 | bytes 2097152 | tf_op jit(solution)/shard_map/pallas_call | solution.py:560
  (1 shorter events, 0.0 us)
Async XLA Ops:
  0.0 12.4 %collective-permute-start = (bf16[2,8,32,128]{3,2,1,0:T(8,128)(2,1)}, bf16[2,8,32,128]{3,2,1,0:T(8,128)(2,1)S(1)}, u32[]{:S(2)}, u32[]{:S(2)}) collective-permute-start(bf16[2,8,32,128]{3,2,1,0:T(8,128)(2,1)} %own_far.1), channel_id=1, source_target_pairs={{0,32},{1,33},{2,34},{3,35},{4,36},{5,37},{6,38},{7,39},{8,40},{9,... | collective-permute-start | bytes 393224 | tf_op jit(solution)/shard_map/ppermute | solution.py:468
  3.9 8.4 %collective-permute-start.1 = (bf16[2,8,32,128]{3,2,1,0:T(8,128)(2,1)}, bf16[2,8,32,128]{3,2,1,0:T(8,128)(2,1)S(1)}, u32[]{:S(2)}, u32[]{:S(2)}) collective-permute-start(bf16[2,8,32,128]{3,2,1,0:T(8,128)(2,1)} %own_far.1), channel_id=1, source_target_pairs={{32,0},{33,1},{34,2},{35,3},{36,4},{37,5},{38,6},{39,7},{40,8},{41... | collective-permute-start | bytes 393224 | tf_op jit(solution)/shard_map/ppermute | solution.py:468
  27.9 5.6 %collective-permute-start.2 = (bf16[24,32,128]{2,1,0:T(8,128)(2,1)S(1)}, bf16[24,32,128]{2,1,0:T(8,128)(2,1)S(1)}, u32[]{:S(2)}, u32[]{:S(2)}) collective-permute-start(bf16[24,32,128]{2,1,0:T(8,128)(2,1)S(1)} %get-tuple-element.51), channel_id=1, source_target_pairs={{0,1},{1,0},{2,3},{3,2},{4,5},{5,4},{6,7},{7,6},{8,9},{9,8},{10,11... | collective-permute-start | bytes 589832 | tf_op jit(solution)/shard_map/ppermute | solution.py:468
  33.9 7.3 %collective-permute-start.4 = (bf16[26,32,128]{2,1,0:T(8,128)(2,1)S(1)}, bf16[26,32,128]{2,1,0:T(8,128)(2,1)S(1)}, u32[]{:S(2)}, u32[]{:S(2)}) collective-permute-start(bf16[26,32,128]{2,1,0:T(8,128)(2,1)S(1)} %get-tuple-element.55), channel_id=1, source_target_pairs={{1,2},{2,1},{3,4},{4,3},{5,6},{6,5},{7,8},{8,7},{9,10},{10,9},{11,... | collective-permute-start | bytes 638984 | tf_op jit(solution)/shard_map/ppermute | solution.py:468
  37.7 5.1 %collective-permute-start.3 = (bf16[32,128]{1,0:T(8,128)(2,1)S(1)}, bf16[32,128]{1,0:T(8,128)(2,1)S(1)}, u32[]{:S(2)}, u32[]{:S(2)}) collective-permute-start(bf16[32,128]{1,0:T(8,128)(2,1)S(1)} %get-tuple-element.54), channel_id=1, source_target_pairs={{0,0},{1,1},{2,2},{3,3},{4,4},{5,5},{6,6},{7,7},{8,8},{9,9},{10,10... | collective-permute-start | bytes 24584 | tf_op jit(solution)/shard_map/ppermute | solution.py:468
  38.3 4.5 %collective-permute-start.5 = (bf16[4,32,128]{2,1,0:T(8,128)(2,1)S(1)}, bf16[4,32,128]{2,1,0:T(8,128)(2,1)S(1)}, u32[]{:S(2)}, u32[]{:S(2)}) collective-permute-start(bf16[4,32,128]{2,1,0:T(8,128)(2,1)S(1)} %get-tuple-element.56.level3), channel_id=1, source_target_pairs={{0,3},{2,5},{3,0},{4,7},{5,2},{6,9},{7,4},{8,11},{9,6},{10,13},{11... | collective-permute-start | bytes 98312 | tf_op jit(solution)/shard_map/ppermute | solution.py:468

commit v12 on v10

--- a/solution.py
+++ b/solution.py
@@ -42,13 +42,13 @@
 def build_weights(
     ids_far, coupling_far, down_far, wide, up,
     w0, w1, w2, w3, table, down0, down1, down2, top_leaf, wt, wx,
-    ids, coupling, down, sems,
+    ids, coupling, down, blocks, sems,
 ):
     row, col, _, _ = places()
     first = pltpu.make_async_copy(ids_far, ids, sems.at[8])
     first.start()
     levels = []
-    for level in range(8):
+    for level in range(4):
         levels.append(
             pltpu.make_async_copy(coupling_far.at[level], coupling.at[level], sems.at[level])
         )
@@ -78,7 +78,32 @@
                 halves.append(coupling[level, ids[level, 2 * e + f, block_slot(e, f, wr, wc)]])
         return lanes(halves)
 
+    def far_slot(e, f, wr, wc):
+        row_in = jnp.logical_and(wr >= e + 1, wr <= e + 3)
+        col_in = jnp.logical_and(wc >= f + 1, wc <= f + 3)
+        skipped = 3 * jnp.clip(wr - 1 - e, 0, 3) + jnp.where(row_in, jnp.clip(wc - 1 - f, 0, 3), 0)
+        slot = jnp.clip(6 * wr + wc - skipped, 0, 26)
+        return slot, jnp.where(jnp.logical_and(row_in, col_in), 0.0, 1.0)
+
+    def single(level, e, f, wr, wc):
+        slot, keep = far_slot(e, f, wr, wc)
+        block = coupling[level, ids[level, 2 * e + f, slot]]
+        return block * jnp.full((RANK, RANK), keep, F32).astype(BF)
+
     first.wait()
+    chip = col // 2
+    plane = (chip - row + 16) % 16
+    fetched, keeps = [], []
+    for level, e, wr in ((7, 0, 2), (6, 0, 2), (5, 0, 2), (4, 0, 2), (4, 1, 2), (4, 0, 3), (4, 1, 3)):
+        theirs, ours = plane // (1 << (level - 4)), chip // (1 << (level - 4))
+        wc = theirs - ours + 2 + ours % 2
+        inside = jnp.where(jnp.logical_and(wc >= 0, wc <= 5), 1.0, 0.0)
+        slot, keep = far_slot(jnp.int32(e), ours % 2, jnp.int32(wr), jnp.clip(wc, 0, 5))
+        at = len(fetched)
+        picked = coupling_far.at[level, ids[level, 2 * e + ours % 2, slot]]
+        fetched.append(pltpu.make_async_copy(picked, blocks.at[at], sems.at[10 + at]))
+        fetched[at].start()
+        keeps.append(keep * inside)
     levels[0].wait()
     for wr in range(6):
         for wc in range(6):
@@ -95,15 +120,6 @@
                 for wr in range(6):
                     for wc in range(6):
                         out[pl.ds((6 * wr + wc) * RANK, RANK), :] = pair(level, e, wr, wc)
-
-    def single(level, e, f, wr, wc):
-        row_in = jnp.logical_and(wr >= e + 1, wr <= e + 3)
-        col_in = jnp.logical_and(wc >= f + 1, wc <= f + 3)
-        skipped = 3 * jnp.clip(wr - 1 - e, 0, 3) + jnp.where(row_in, jnp.clip(wc - 1 - f, 0, 3), 0)
-        slot = jnp.clip(6 * wr + wc - skipped, 0, 26)
-        keep = jnp.where(jnp.logical_and(row_in, col_in), 0.0, 1.0)
-        block = coupling[level, ids[level, 2 * e + f, slot]]
-        return block * jnp.full((RANK, RANK), keep, F32).astype(BF)
 
     levels[3].wait()
     e3, f3 = (row // 4) % 2, col % 2
@@ -123,30 +139,20 @@
                     )
 
     other.wait()
-    chip = col // 2
-    plane = (chip - row + 16) % 16
-
-    def coupled(level, e, wr, height):
-        levels_up = plane // (1 << height), chip // (1 << height)
-        f = levels_up[1] % 2
-        wc = levels_up[0] - levels_up[1] + 2 + f
-        inside = jnp.where(jnp.logical_and(wc >= 0, wc <= 5), 1.0, 0.0)
-        block = single(level, e, f, jnp.int32(wr), jnp.clip(wc, 0, 5))
-        return block.astype(F32) * jnp.full((RANK, RANK), inside, F32)
-
-    for level in (4, 5, 6, 7):
-        levels[level].wait()
-    zero = jnp.int32(0)
-    inner = coupled(7, zero, 2, 3).astype(BF)
+    def coupled(at):
+        fetched[at].wait()
+        return blocks[at].astype(F32) * jnp.full((RANK, RANK), keeps[at], F32)
+
+    inner = coupled(0).astype(BF)
     inner = dot(dot(up[6, (plane // 4) % 2], inner).astype(BF), down[6, (chip // 4) % 2])
-    inner = (inner + coupled(6, zero, 2, 2)).astype(BF)
+    inner = (inner + coupled(1)).astype(BF)
     inner = dot(dot(up[5, (plane // 2) % 2], inner).astype(BF), down[5, (chip // 2) % 2])
-    inner = (inner + coupled(5, zero, 2, 1)).astype(BF)
+    inner = (inner + coupled(2)).astype(BF)
     for source in (0, 1):
         raised = dot(up[4, 2 * source + plane % 2], inner).astype(BF)
         for target in (0, 1):
             local4 = dot(raised, down[4, 2 * target + chip % 2])
-            local4 = (local4 + coupled(4, jnp.int32(target), source + 2, 0)).astype(BF)
+            local4 = (local4 + coupled(3 + 2 * source + target)).astype(BF)
             nodes = lanes([dot(local4, down[3, 2 * e + f3]).astype(BF) for e in (0, 1)])
             wt[pl.ds(RANK * source, RANK), pl.ds(128 * target, 128)] = nodes
 
@@ -176,7 +182,7 @@
     ids_far, coupling_far, down_far, up_far, basis_far, own_far,
     wide, up, own, mine, low,
     w0, w1, w2, w3, table, down0, down1, down2, top_leaf, wt, wx,
-    ids, coupling, down, basis, sems, small_sems,
+    ids, coupling, down, blocks, basis, sems, small_sems,
 ):
     _, _, chip, _ = places()
     small = [
@@ -198,7 +204,7 @@
         build_weights(
             ids_far, coupling_far, down_far, wide, up,
             w0, w1, w2, w3, table, down0, down1, down2, top_leaf, wt, wx,
-            ids, coupling, down, sems,
+            ids, coupling, down, blocks, sems,
         )
 
 
@@ -484,8 +490,8 @@
         array((8 * RANK, 4 * RANK)),
     ]
     build_scratch = [
-        pltpu.SMEM(far_ids.shape, jnp.int32), pltpu.VMEM(coupling.shape, BF),
-        pltpu.VMEM(down_transfer.shape, BF),
+        pltpu.SMEM(far_ids.shape, jnp.int32), pltpu.VMEM((4,) + coupling.shape[1:], BF),
+        pltpu.VMEM(down_transfer.shape, BF), pltpu.VMEM((7, RANK, RANK), BF),
     ]
     wide, up, own, mine, low, *weights = call(
         start_kernel,
@@ -497,7 +503,7 @@
         in_specs=[hbm] * 6,
         scratch=build_scratch
         + [
-            pltpu.VMEM(leaf_basis.shape[::-1], BF), pltpu.SemaphoreType.DMA((10,)),
+            pltpu.VMEM(leaf_basis.shape[::-1], BF), pltpu.SemaphoreType.DMA((17,)),
             pltpu.SemaphoreType.DMA((3,)),
         ],
     )(*far_inputs)
@@ -529,7 +535,7 @@
         weight_shapes,
         in_specs=[hbm] * 3 + [whole] * (3 + count),
         input_output_aliases={6 + at: at for at in range(count)},
-        scratch=build_scratch + [pltpu.SemaphoreType.DMA((10,))],
+        scratch=build_scratch + [pltpu.SemaphoreType.DMA((17,))],
     )(*far_inputs[:3], wide, up, side, *weights)
     w0, w1, w2, w3, table, down0, down1, down2, top_leaf, wt, wx = weights
 

time: 63.6 us -> 63.7 us (level)
  no operation moved by 1% of the time
where the time goes in v12:
time: 63.7 us; the launch traced here: 63.2 us
  blocking collectives  34.8 us (55%)
  starting transfers between devices  15 us (24%)
  Pallas kernels  10.1 us (16%)
  waiting for transfers between devices  3.23 us (5%)
    all_to_all x1, blocking collectives, shards(): top = lax.all_to_all(shares, 'gx', 0, 0)  19.9 us
    ppermute x6, starting transfers between devices, move(): return lax.ppermute(value, both, route(rule, size_x, size_y))  15 us
    all_to_all x1, blocking collectives, shards(): gathered = lax.all_to_all(sent, 'gx', 0, 0)  14.9 us
    pallas_call x1, Pallas kernels, shards(): call(start_kernel, [array((128, 256)), array(up_transfer.shape), array(pr...  6.17 us
    ppermute x6, waiting for transfers between devices, move(): return lax.ppermute(value, both, route(rule, size_x, size_y))  3.23 us
  transfers between devices with their start and end apart: 6, of which 2 were waited for; matrix products, arithmetic and copies ran while one was open for 0% of the time, Pallas kernels for 12%

profile of v12, /device:TPU:1, one launch (start us, length us, event | category | flops | bytes accessed | tf_op | source)
XLA Modules:
  0.0 63.2 jit_solution(8883066673542650908)
XLA Ops:
  0.0 3.9 %collective-permute-start = (bf16[2,8,32,128]{3,2,1,0:T(8,128)(2,1)}, bf16[2,8,32,128]{3,2,1,0:T(8,128)(2,1)S(1)}, u32[]{:S(2)}, u32[]{:S(2)}) collective-permute-start(bf16[2,8,32,128]{3,2,1,0:T(8,128)(2,1)} %own_far.1), channel_id=1, source_target_pairs={{0,32},{1,33},{2,34},{3,35},{4,36},{5,37},{6,38},{7,39},{8,40},{9,... | collective-permute-start | bytes 393224 | tf_op jit(solution)/shard_map/ppermute | solution.py:474
  3.9 1.3 %collective-permute-start.1 = (bf16[2,8,32,128]{3,2,1,0:T(8,128)(2,1)}, bf16[2,8,32,128]{3,2,1,0:T(8,128)(2,1)S(1)}, u32[]{:S(2)}, u32[]{:S(2)}) collective-permute-start(bf16[2,8,32,128]{3,2,1,0:T(8,128)(2,1)} %own_far.1), channel_id=1, source_target_pairs={{32,0},{33,1},{34,2},{35,3},{36,4},{37,5},{38,6},{39,7},{40,8},{41... | collective-permute-start | bytes 393224 | tf_op jit(solution)/shard_map/ppermute | solution.py:474
  5.2 6.2 %shard_map.64 = (bf16[128,256]{1,0:T(8,128)(2,1)S(1)}, bf16[7,4,64,64]{3,2,1,0:T(8,128)(2,1)S(1)}, bf16[2,8,32,128]{3,2,1,0:T(8,128)(2,1)S(1)}, bf16[2,4,32,128]...) custom-call(s32[8,4,27]{2,1,0:T(4,128)} %ids_far.3, ...), custom_call_target="tpu_custom_call" | custom-call | flops 16777216 | bytes 2097152 | tf_op jit(solution)/shard_map/pallas_call | solution.py:496
  11.4 0.0 collective-permute-done.above
  11.4 0.0 collective-permute-done.1.below
  11.4 0.2 shard_map.65
  11.7 14.9 %all_to_all.10.gathered = bf16[16,2,32,128]{3,2,1,0:T(8,128)(2,1)S(1)} all-to-all(bf16[16,2,32,128]{3,2,1,0:T(8,128)(2,1)S(1)} %get-tuple-element.46), channel_id=1, replica_groups=mesh['gx'=16,'gy'=32] {'gx'}, dimensions={0} | all-to-all | bytes 524288 | tf_op jit(solution)/shard_map/all_to_all | solution.py:513
  26.6 0.5 shard_map.66
  27.1 4.6 %collective-permute-start.2 = (bf16[24,32,128]{2,1,0:T(8,128)(2,1)S(1)}, bf16[24,32,128]{2,1,0:T(8,128)(2,1)S(1)}, u32[]{:S(2)}, u32[]{:S(2)}) collective-permute-start(bf16[24,32,128]{2,1,0:T(8,128)(2,1)S(1)} %get-tuple-element.51), channel_id=1, source_target_pairs={{0,1},{1,0},{2,3},{3,2},{4,5},{5,4},{6,7},{7,6},{8,9},{9,8},{10,11... | collective-permute-start | bytes 589832 | tf_op jit(solution)/shard_map/ppermute | solution.py:474
  31.7 1.0 %collective-permute-done.2.packed = bf16[24,32,128]{2,1,0:T(8,128)(2,1)S(1)} collective-permute-done((bf16[24,32,128]{2,1,0:T(8,128)(2,1)S(1)}, bf16[24,32,128]{2,1,0:T(8,128)(2,1)S(1)}, u32[]{:S(2)}, u32[]{:S(2)}) %collective-permute-start.2) | collective-permute-done | bytes 196640 | tf_op jit(solution)/shard_map/ppermute | solution.py:474
  32.8 0.3 shard_map.67
  33.0 3.8 %collective-permute-start.4 = (bf16[26,32,128]{2,1,0:T(8,128)(2,1)S(1)}, bf16[26,32,128]{2,1,0:T(8,128)(2,1)S(1)}, u32[]{:S(2)}, u32[]{:S(2)}) collective-permute-start(bf16[26,32,128]{2,1,0:T(8,128)(2,1)S(1)} %get-tuple-element.55), channel_id=1, source_target_pairs={{1,2},{2,1},{3,4},{4,3},{5,6},{6,5},{7,8},{8,7},{9,10},{10,9},{11,... | collective-permute-start | bytes 638984 | tf_op jit(solution)/shard_map/ppermute | solution.py:474
  36.8 0.7 %collective-permute-start.3 = (bf16[32,128]{1,0:T(8,128)(2,1)S(1)}, bf16[32,128]{1,0:T(8,128)(2,1)S(1)}, u32[]{:S(2)}, u32[]{:S(2)}) collective-permute-start(bf16[32,128]{1,0:T(8,128)(2,1)S(1)} %get-tuple-element.54), channel_id=1, source_target_pairs={{0,0},{1,1},{2,2},{3,3},{4,4},{5,5},{6,6},{7,7},{8,8},{9,9},{10,10... | collective-permute-start | bytes 24584 | tf_op jit(solution)/shard_map/ppermute | solution.py:474
  37.5 0.7 %collective-permute-start.5 = (bf16[4,32,128]{2,1,0:T(8,128)(2,1)S(1)}, bf16[4,32,128]{2,1,0:T(8,128)(2,1)S(1)}, u32[]{:S(2)}, u32[]{:S(2)}) collective-permute-start(bf16[4,32,128]{2,1,0:T(8,128)(2,1)S(1)} %get-tuple-element.56.level3), channel_id=1, source_target_pairs={{0,3},{2,5},{3,0},{4,7},{5,2},{6,9},{7,4},{8,11},{9,6},{10,13},{11... | collective-permute-start | bytes 98312 | tf_op jit(solution)/shard_map/ppermute | solution.py:474
  38.2 2.2 %collective-permute-done.4.tag.side = bf16[26,32,128]{2,1,0:T(8,128)(2,1)S(1)} collective-permute-done((bf16[26,32,128]{2,1,0:T(8,128)(2,1)S(1)}, bf16[26,32,128]{2,1,0:T(8,128)(2,1)S(1)}, u32[]{:S(2)}, u32[]{:S(2)}) %collective-permute-start.4) | collective-permute-done | bytes 213024 | tf_op jit(solution)/shard_map/ppermute | solution.py:474
  40.4 0.2 shard_map.68
  40.5 0.8 %shard_map.69 = (f32[2,8,32,128]{3,2,1,0:T(8,128)S(1)}, f32[128,256]{1,0:T(8,128)S(1)}, f32[64,128]{1,0:T(8,128)S(1)}, f32[32,128]{1,0:T(8,128)S(1)}) custom-call(bf16[2,8,32,128]{3,2,1,0:T(8,128)(2,1)S(1)} %get-tuple-element.47.own, bf16[2,8,32,128]{3,2,1,0:T(8,128)(2,1)S(1)} %collective-permute-done.above, ...), custom_call_target="tpu_custom_call" | custom-call | flops 16777216 | bytes 2097152 | tf_op jit(solution)/shard_map/pallas_call | solution.py:542
  41.3 0.7 %shard_map.70.partial = f32[2,8,32,128]{3,2,1,0:T(8,128)S(1)} custom-call(bf16[26,32,128]{2,1,0:T(8,128)(2,1)S(1)} %collective-permute-done.4.tag.side, bf16[4,32,128]{2,1,0:T(8,128)(2,1)S(1)} %get-tuple-element.56.level3, bf16[1536,64]{1,0:T(8,128)(2,1)S(1)} %get-tuple-element.68.w3, f32[2,8,32,128]{3,2,1,0:T(8,128)S(1)} %get-tuple-element.73.near_sum, ...), custom_call_target="tpu_custom_call" | custom-call | flops 16777216 | bytes 2097152 | tf_op jit(solution)/shard_map/pallas_call | solution.py:553
  42.0 0.0 collective-permute-done.3.block
  42.0 0.0 collective-permute-done.5.third
  42.1 0.3 shard_map.72
  42.4 19.9 %all_to_all.11.top = bf16[16,16,128]{2,1,0:T(8,128)(2,1)S(1)} all-to-all(bf16[16,16,128]{2,1,0:T(8,128)(2,1)S(1)} %shard_map.72), channel_id=1, replica_groups=mesh['gx'=16,'gy'=32] {'gx'}, dimensions={0} | all-to-all | bytes 131072 | tf_op jit(solution)/shard_map/all_to_all | solution.py:564
  62.3 0.9 %shard_map.73 = bf16[2,8,32,128]{3,2,1,0:T(8,128)(2,1)} custom-call(bf16[16,16,128]{2,1,0:T(8,128)(2,1)S(1)} %all_to_all.11.top, f32[2,8,32,128]{3,2,1,0:T(8,128)S(1)} %shard_map.70.partial, bf16[64,2048]{1,0:T(8,128)(2,1)S(1)} %get-tuple-element.82.top_leaf), custom_call_target="tpu_custom_call" | custom-call | flops 16777216 | bytes 2097152 | tf_op jit(solution)/shard_map/pallas_call | solution.py:566
  (1 shorter events, 0.0 us)
Async XLA Ops:
  0.0 11.4 %collective-permute-start = (bf16[2,8,32,128]{3,2,1,0:T(8,128)(2,1)}, bf16[2,8,32,128]{3,2,1,0:T(8,128)(2,1)S(1)}, u32[]{:S(2)}, u32[]{:S(2)}) collective-permute-start(bf16[2,8,32,128]{3,2,1,0:T(8,128)(2,1)} %own_far.1), channel_id=1, source_target_pairs={{0,32},{1,33},{2,34},{3,35},{4,36},{5,37},{6,38},{7,39},{8,40},{9,... | collective-permute-start | bytes 393224 | tf_op jit(solution)/shard_map/ppermute | solution.py:474
  3.9 7.5 %collective-permute-start.1 = (bf16[2,8,32,128]{3,2,1,0:T(8,128)(2,1)}, bf16[2,8,32,128]{3,2,1,0:T(8,128)(2,1)S(1)}, u32[]{:S(2)}, u32[]{:S(2)}) collective-permute-start(bf16[2,8,32,128]{3,2,1,0:T(8,128)(2,1)} %own_far.1), channel_id=1, source_target_pairs={{32,0},{33,1},{34,2},{35,3},{36,4},{37,5},{38,6},{39,7},{40,8},{41... | collective-permute-start | bytes 393224 | tf_op jit(solution)/shard_map/ppermute | solution.py:474
  27.1 5.7 %collective-permute-start.2 = (bf16[24,32,128]{2,1,0:T(8,128)(2,1)S(1)}, bf16[24,32,128]{2,1,0:T(8,128)(2,1)S(1)}, u32[]{:S(2)}, u32[]{:S(2)}) collective-permute-start(bf16[24,32,128]{2,1,0:T(8,128)(2,1)S(1)} %get-tuple-element.51), channel_id=1, source_target_pairs={{0,1},{1,0},{2,3},{3,2},{4,5},{5,4},{6,7},{7,6},{8,9},{9,8},{10,11... | collective-permute-start | bytes 589832 | tf_op jit(solution)/shard_map/ppermute | solution.py:474
  33.0 7.3 %collective-permute-start.4 = (bf16[26,32,128]{2,1,0:T(8,128)(2,1)S(1)}, bf16[26,32,128]{2,1,0:T(8,128)(2,1)S(1)}, u32[]{:S(2)}, u32[]{:S(2)}) collective-permute-start(bf16[26,32,128]{2,1,0:T(8,128)(2,1)S(1)} %get-tuple-element.55), channel_id=1, source_target_pairs={{1,2},{2,1},{3,4},{4,3},{5,6},{6,5},{7,8},{8,7},{9,10},{10,9},{11,... | collective-permute-start | bytes 638984 | tf_op jit(solution)/shard_map/ppermute | solution.py:474
  36.8 5.2 %collective-permute-start.3 = (bf16[32,128]{1,0:T(8,128)(2,1)S(1)}, bf16[32,128]{1,0:T(8,128)(2,1)S(1)}, u32[]{:S(2)}, u32[]{:S(2)}) collective-permute-start(bf16[32,128]{1,0:T(8,128)(2,1)S(1)} %get-tuple-element.54), channel_id=1, source_target_pairs={{0,0},{1,1},{2,2},{3,3},{4,4},{5,5},{6,6},{7,7},{8,8},{9,9},{10,10... | collective-permute-start | bytes 24584 | tf_op jit(solution)/shard_map/ppermute | solution.py:474
  37.5 4.5 %collective-permute-start.5 = (bf16[4,32,128]{2,1,0:T(8,128)(2,1)S(1)}, bf16[4,32,128]{2,1,0:T(8,128)(2,1)S(1)}, u32[]{:S(2)}, u32[]{:S(2)}) collective-permute-start(bf16[4,32,128]{2,1,0:T(8,128)(2,1)S(1)} %get-tuple-element.56.level3), channel_id=1, source_target_pairs={{0,3},{2,5},{3,0},{4,7},{5,2},{6,9},{7,4},{8,11},{9,6},{10,13},{11... | collective-permute-start | bytes 98312 | tf_op jit(solution)/shard_map/ppermute | solution.py:474
